TPU v7x, 128 devices: a whole 4x4x4 slice. The times are simulated.
128 devices in a mesh: group: 8 (over y, core), tensor: 16 (over z, x).
Axes of the slice: x: 4, y: 4, z: 4, core: 2. Of those that a mesh axis runs over, the one named last changes fastest.
Arguments:
- residual: bfloat16 [2048, 7168], P('group'), may hold values from -6 to 6
- queries: bfloat16 [2048, 8, 896], P('group'), may hold values from -100 to 100
- new_kv: bfloat16 [2, 2048, 8, 128], P(None, 'group'), may hold values from -6 to 6
- kv_cache: bfloat16 [2, 2048, 1024, 128], P(None, 'group', 'tensor'), may hold values from -6 to 6
- lengths: int32 [2048], P('group'), may hold values from 1 to 128
- out_weight: bfloat16 [7168, 7168], P('tensor'), may hold values from -0.09375 to 0.09375
- dense_gate: bfloat16 [7168, 4864], P(None, 'tensor'), may hold values from -0.0625 to 0.0625
- dense_up: bfloat16 [7168, 4864], P(None, 'tensor'), may hold values from -0.0625 to 0.0625
- dense_down: bfloat16 [4864, 7168], P('tensor'), may hold values from -0.125 to 0.125
- expert_ids: int32 [2048, 2], P('group'), may hold values from 0 to 7, all different within a row; in each aligned block of 256 rows (0 to 255, 256 to 511, ...) at most 128 rows name the same one
- route_weights: float32 [2048, 2], P('group'), may hold values from 0.2 to 1
- expert_gate: bfloat16 [8, 7168, 4864], P('group', None, 'tensor'), may hold values from -0.0625 to 0.0625
- expert_up: bfloat16 [8, 7168, 4864], P('group', None, 'tensor'), may hold values from -0.0625 to 0.0625
- expert_down: bfloat16 [8, 4864, 7168], P('group', 'tensor'), may hold values from -0.125 to 0.125
Outputs:
- mixed: bfloat16 [2048, 7168], P('group', 'tensor')
Inputs may be any that keep to these rules, and one draw needn't show every extreme that they name: `expert_ids`: among the 256 rows of one group no expert is named by more than 128 rows, a bound that some block reaches of them.
All inputs are finite; a program needn't handle non-finite values.
Results may differ from a plain program's by a relative error of at most 0.02.
Values may be sent and summed in bfloat16 or wider, within the bound.
A program may use at most 256 MiB of HBM per device.

v0:
```python
import math

import jax
import jax.numpy as jnp
from jax import lax
from jax.sharding import PartitionSpec as P


def from_partner(block, axis, apart):
    count = lax.axis_size(axis)
    route = []
    for low in range(count):
        high = low | 1 << apart
        if high != low and high < count:
            route += [(low, high), (high, low)]
    return lax.ppermute(block, axis, route)


def shards(
    residual,
    queries,
    new_kv,
    kv_cache,
    lengths,
    out_weight,
    dense_gate,
    dense_up,
    dense_down,
    expert_ids,
    route_weights,
    expert_gate,
    expert_up,
    expert_down,
):
    row_count = residual.shape[0]
    model_width = residual.shape[1]
    tensor_size = lax.axis_size("tensor")
    group_size = lax.axis_size("group")
    my_rank = lax.axis_index("tensor")
    kv_heads = new_kv.shape[2]
    head_size = new_kv.shape[3]
    split_count = tensor_size // kv_heads
    local_span = kv_cache.shape[2]
    my_head = my_rank // split_count
    my_part = my_rank % split_count
    query_rows = lax.dynamic_index_in_dim(queries, my_head, 1, keepdims=False).reshape(
        row_count, -1, head_size
    )
    new_key = lax.dynamic_index_in_dim(new_kv[0], my_head, 1, keepdims=False)
    new_value = lax.dynamic_index_in_dim(new_kv[1], my_head, 1, keepdims=False)
    scale = 1.0 / math.sqrt(head_size)
    scores = (
        jnp.einsum("tgd,tpd->tgp", query_rows, kv_cache[0], preferred_element_type=jnp.float32)
        * scale
    )
    own_score = (
        jnp.einsum("tgd,td->tg", query_rows, new_key, preferred_element_type=jnp.float32) * scale
    )
    position = my_part * local_span + jnp.arange(local_span, dtype=jnp.int32)
    usable = position[None, None, :] < lengths[:, None, None]
    masked = jnp.where(usable, scores, -1e30)
    highest = jnp.maximum(jnp.max(masked, axis=-1), own_score)
    highest = jnp.maximum(highest, from_partner(highest, "tensor", 0))
    weights = jnp.where(usable, jnp.exp(masked - highest[..., None]), 0.0).astype(jnp.bfloat16)
    own_weight = lax.optimization_barrier(jnp.exp(own_score - highest).astype(jnp.bfloat16)).astype(
        jnp.float32
    )
    leading = (my_part == 0).astype(jnp.float32)
    numerator = jnp.einsum("tgp,tpd->tgd", weights, kv_cache[1], preferred_element_type=jnp.float32)
    numerator = (
        numerator + leading * own_weight[..., None] * new_value.astype(jnp.float32)[:, None, :]
    )
    denominator = jnp.sum(weights.astype(jnp.float32), axis=-1) + leading * own_weight
    other_numerator, other_denominator = from_partner((numerator, denominator), "tensor", 0)
    numerator = numerator + other_numerator
    denominator = denominator + other_denominator
    attention = (numerator / denominator[..., None]).astype(jnp.bfloat16).reshape(row_count, -1)
    slice_width = out_weight.shape[0]
    my_columns = lax.dynamic_slice_in_dim(attention, my_part * slice_width, slice_width, 1)
    projected = lax.psum(
        jnp.dot(my_columns, out_weight, preferred_element_type=jnp.float32), "tensor"
    )
    state = (residual.astype(jnp.float32) + projected).astype(jnp.bfloat16)
    state_wide = state.astype(jnp.float32)
    normed = (
        state_wide * lax.rsqrt(jnp.mean(state_wide * state_wide, axis=-1, keepdims=True) + 1e-05)
    ).astype(jnp.bfloat16)
    dense_inner = (
        jax.nn.silu(jnp.dot(normed, dense_gate, preferred_element_type=jnp.float32))
        * jnp.dot(normed, dense_up, preferred_element_type=jnp.float32)
    ).astype(jnp.bfloat16)
    dense_part = jnp.dot(dense_inner, dense_down, preferred_element_type=jnp.float32)
    column_count = model_width // tensor_size
    capacity = 4 * row_count // group_size
    flat_ids = expert_ids.reshape(-1)
    one_hot = (flat_ids[:, None] == jnp.arange(group_size, dtype=jnp.int32)[None, :]).astype(
        jnp.int32
    )
    earlier = jnp.cumsum(one_hot, axis=0) - one_hot
    slot_index = jnp.sum(earlier * one_hot, axis=1)
    target = flat_ids * capacity + slot_index
    source_row = jnp.arange(2 * row_count, dtype=jnp.int32) // 2
    payload = lax.dynamic_slice_in_dim(normed, my_rank * column_count, column_count, 1)
    buffer = (
        jnp.zeros((group_size * capacity, payload.shape[1]), jnp.bfloat16)
        .at[target]
        .set(payload[source_row])
    )
    buffer = buffer.reshape(group_size, capacity, payload.shape[1])
    inputs = lax.all_gather(
        lax.all_to_all(buffer, "group", split_axis=0, concat_axis=0, tiled=True),
        "tensor",
        axis=2,
        tiled=True,
    )
    flat_inputs = inputs.reshape(-1, model_width)
    hidden_units = (
        jax.nn.silu(jnp.dot(flat_inputs, expert_gate[0], preferred_element_type=jnp.float32))
        * jnp.dot(flat_inputs, expert_up[0], preferred_element_type=jnp.float32)
    ).astype(jnp.bfloat16)
    partial_out = jnp.dot(hidden_units, expert_down[0], preferred_element_type=jnp.float32).reshape(
        inputs.shape[0], inputs.shape[1], model_width
    )
    summed = lax.psum_scatter(
        partial_out.astype(jnp.bfloat16), "tensor", scatter_dimension=2, tiled=True
    ).astype(jnp.float32)
    returned = lax.all_to_all(
        summed.astype(jnp.bfloat16), "group", split_axis=0, concat_axis=0, tiled=True
    ).astype(summed.dtype)
    picked = returned.reshape(group_size * capacity, -1)[target].reshape(row_count, 2, -1)
    mixture = jnp.sum(picked * route_weights[:, :, None], axis=1)
    state_columns = lax.dynamic_slice_in_dim(state_wide, my_rank * column_count, column_count, 1)
    dense_share = lax.psum_scatter(
        dense_part.astype(jnp.bfloat16), "tensor", scatter_dimension=1, tiled=True
    ).astype(jnp.float32)
    total = state_columns + dense_share + mixture
    return total.astype(jnp.bfloat16)


def solution(mesh):
    placed = (
        P("group", None),
        P("group", None, None),
        P(None, "group", None, None),
        P(None, "group", "tensor", None),
        P("group"),
        P("tensor", None),
        P(None, "tensor"),
        P(None, "tensor"),
        P("tensor", None),
        P("group", None),
        P("group", None),
        P("group", None, "tensor"),
        P("group", None, "tensor"),
        P("group", "tensor", None),
    )
    return jax.shard_map(
        shards, mesh=mesh, in_specs=placed, out_specs=P("group", "tensor"), check_vma=False
    )
```

profile of v0, /device:TPU:1, one launch (start us, length us, event | category | flops | bytes accessed | tf_op | source)
XLA Modules:
  0.0 554.5 jit_solution(11366163367687167700)
XLA Ops:
  6.5 3.1 constant_dynamic-slice_fusion.2
  12.8 4.5 fusion.60
  17.4 2.1 collective-permute-start
  23.0 3.1 fusion.28
  26.3 1.7 collective-permute-start.1
  28.1 21.6 %collective-permute-done.2 = f32[256,7]{1,0:T(8,128)S(1)} collective-permute-done((f32[256,7]{1,0:T(8,128)S(1)}, f32[256,7]{1,0:T(8,128)S(1)}, u32[]{:S(2)}, u32[]{:S(2)}) %collective-permute-start.2) | collective-permute-done | bytes 7200 | tf_op jit(solution)/shard_map/ppermute | solution.py:16
  50.7 8.0 %fusion.49 = f32[256,7168]{1,0:T(8,128)} fusion(bf16[448,7168]{1,0:T(8,128)(2,1)} %param.19, bf16[256,896]{0,1:T(8,128)(2,1)S(1)} %bitcast.95, s32[]{:T(128)S(6)} %select_n.70), kind=kOutput, calls=%fused_computation.45 | convolution fusion | flops 1644167168 | bytes 13991940 | tf_op jit(solution)/shard_map/dot_general | solution.py:81
  61.6 133.5 %all-reduce.2.cloned.1.call-done = f32[256,7168]{1,0:T(8,128)} async-done(((f32[256,7168]{1,0:T(8,128)}), f32[256,7168]{1,0:T(8,128)}) %all-reduce.2.cloned.1.call-update) | async-done | bytes 7340048 | tf_op jit(solution)/shard_map/psum | solution.py:80
  195.1 5.2 multiply_reduce_fusion
  201.1 2.1 copy-done
  203.4 1.7 copy-done.1
  205.1 5.0 scatter_custom_fusion
  210.8 18.5 %all_to_all.10 = bf16[8,128,448]{1,2,0:T(8,128)(2,1)S(1)} all-to-all(bf16[8,128,448]{1,2,0:T(8,128)(2,1)S(1)} %copy.76), channel_id=1, replica_groups=mesh['group'=8,'tensor'=16] {'group'}, dimensions={0} | all-to-all | bytes 1835008 | tf_op jit(solution)/shard_map/all_to_all | solution.py:111
  229.3 1.6 copy.77
  231.2 98.6 %all-gather.2.cloned.1.call-done = bf16[8,128,7168]{1,0,2:T(8,128)(2,1)} async-done(((bf16[8,128,448]{1,0,2:T(8,128)(2,1)}), bf16[8,128,7168]{1,0,2:T(8,128)(2,1)}) %all-gather.2.cloned.1.call-update) | async-done | bytes 14680080 | tf_op jit(solution)/shard_map/all_gather | solution.py:110
  329.8 11.3 %fusion = f32[1024,304]{0,1:T(8,128)S(1)} fusion(bf16[896,8,8,128]{3,2,1,0:T(8,128)(2,1)} %bitcast.105, bf16[1,7168,304]{1,2,0:T(8,128)(2,1)} %param.25), kind=kOutput, calls=%fused_computation.3 | convolution fusion | flops 4462739456 | bytes 20283392 | tf_op jit(solution)/shard_map/dot_general | solution.py:118
  341.1 7.0 %fusion.36 = bf16[38,8,8,128]{3,2,1,0:T(8,128)(2,1)S(1)} fusion(bf16[896,8,8,128]{3,2,1,0:T(8,128)(2,1)S(1)} %bitcast.106, bf16[1,7168,304]{1,2,0:T(8,128)(2,1)} %param.26, f32[1024,304]{0,1:T(8,128)S(1)} %fusion), kind=kOutput, calls=%fused_computation.30 | convolution fusion | flops 4464607232 | bytes 20905984 | tf_op jit(solution)/shard_map/dot_general | solution.py:119
  348.1 13.3 %convolution_convert_fusion = bf16[8,128,7168]{1,2,0:T(8,128)(2,1)} fusion(bf16[1,304,7168]{2,1,0:T(8,128)(2,1)} %param.27, bf16[38,8,8,128]{3,2,1,0:T(8,128)(2,1)S(1)} %fusion.36), kind=kOutput, calls=%fused_computation.7 | convolution fusion | flops 4470079488 | bytes 19660800 | tf_op jit(solution)/shard_map/dot_general | solution.py:121
  361.8 4.7 fusion.61
  366.5 12.2 %fusion.6 = bf16[7168,256]{1,0:T(8,128)(2,1)} fusion(bf16[304,7168]{1,0:T(8,128)(2,1)} %param.22, bf16[256,7168]{1,0:T(8,128)(2,1)} %copy-done.1, bf16[7168,304]{0,1:T(8,128)(2,1)} %param.21, f32[256,304]{0,1:T(8,128)S(1)} %fusion.61), kind=kOutput, calls=%fused_computation.11 | convolution fusion | flops 2233671680 | bytes 16367616 | tf_op jit(solution)/shard_map/dot_general | solution.py:92
  378.7 83.9 %reduce-scatter.5.cloned.1.call-done = bf16[8,128,448]{1,2,0:T(8,128)(2,1)} async-done(((bf16[8,128,7168]{1,2,0:T(8,128)(2,1)}), bf16[8,128,448]{1,2,0:T(8,128)(2,1)}) %reduce-scatter.5.cloned.1.call-update) | async-done | bytes 917520 | tf_op jit(solution)/shard_map/reduce_scatter | solution.py:124
  462.6 5.3 all-to-all-start.1
  468.0 72.1 %reduce-scatter.7.cloned.1.call-done = bf16[448,256]{1,0:T(8,128)(2,1)} async-done(((bf16[7168,256]{1,0:T(8,128)(2,1)}), bf16[448,256]{1,0:T(8,128)(2,1)}) %reduce-scatter.7.cloned.1.call-update) | async-done | bytes 229392
  541.7 1.6 gather_fusion
  (67 shorter events, 18.9 us)
Async XLA Ops:
  6.5 4.7 copy-start.2
  6.5 6.2 %copy-start.5 = (s32[256]{0:T(256)S(1)}, s32[256]{0:T(256)}, u32[]{:S(2)}) copy-start(s32[256]{0:T(256)} %param.18) | copy-start | bytes 3076
  6.5 188.6 %all-reduce.2.cloned.1.call-start = ((), (), s32[]{:S(2)}) async-start(), calls=%async_computation.4 | async-start | bytes 14680064 | tf_op jit(solution)/shard_map/psum | solution.py:80
  17.4 4.8 collective-permute-start
  26.3 23.4 %collective-permute-start.1 = (f32[256,7,128]{2,0,1:T(8,128)S(1)}, f32[256,7,128]{2,0,1:T(8,128)S(1)}, u32[]{:S(2)}, u32[]{:S(2)}) collective-permute-start(f32[256,7,128]{2,0,1:T(8,128)S(1)} %copy.68), channel_id=1, source_target_pairs={{0,1},{1,0},{2,3},{3,2},{4,5},{5,4},{6,7},{7,6},{8,9},{9,8},{10,11... | collective-permute-start | bytes 2752520 | tf_op jit(solution)/shard_map/ppermute | solution.py:16
  28.0 21.6 %collective-permute-start.2 = (f32[256,7]{1,0:T(8,128)S(1)}, f32[256,7]{1,0:T(8,128)S(1)}, u32[]{:S(2)}, u32[]{:S(2)}) collective-permute-start(f32[256,7]{1,0:T(8,128)S(1)} %get-tuple-element.11), channel_id=1, source_target_pairs={{0,1},{1,0},{2,3},{3,2},{4,5},{5,4},{6,7},{7,6},{8,9},{9,8},{10,11... | collective-permute-start | bytes 21512 | tf_op jit(solution)/shard_map/ppermute | solution.py:16
  58.7 0.7 copy-start.3
  58.7 271.1 %all-gather.2.cloned.1.call-start = ((), (), s32[]{:S(2)}) async-start(), calls=%async_computation.5 | async-start | bytes 15597568 | tf_op jit(solution)/shard_map/all_gather | solution.py:110
  200.3 2.9 copy-start
  203.2 1.9 copy-start.1
  230.9 231.6 %reduce-scatter.5.cloned.1.call-start = ((), (), s32[]{:S(2)}) async-start(), calls=%async_computation.6 | async-start | bytes 15597568 | tf_op jit(solution)/shard_map/reduce_scatter | solution.py:124
  329.8 11.3 %copy-start.6 = (bf16[8,128,7168]{1,0,2:T(8,128)(2,1)S(1)}, bf16[8,128,7168]{1,0,2:T(8,128)(2,1)}, u32[]{:S(2)}) copy-start(bf16[8,128,7168]{1,0,2:T(8,128)(2,1)} %all-gather.2.cloned.1.call-done) | copy-start | bytes 44040196
  361.5 178.7 %reduce-scatter.7.cloned.1.call-start = ((), (), s32[]{:S(2)}) async-start(), calls=%async_computation.7 | async-start | bytes 3899392
  378.7 89.2 %copy-start.4 = (f32[256,2]{0,1:T(2,128)S(1)}, f32[256,2]{0,1:T(2,128)}, u32[]{:S(2)}) copy-start(f32[256,2]{0,1:T(2,128)} %param.24) | copy-start | bytes 6148
  462.6 78.6 %all-to-all-start.1 = ((bf16[8,128,448]{1,2,0:T(8,128)(2,1)}), bf16[8,128,448]{1,2,0:T(8,128)(2,1)S(1)}, u32[]{:S(2)}, u32[]{:S(2)}) async-start(bf16[8,128,448]{1,2,0:T(8,128)(2,1)} %reduce-scatter.5.cloned.1.call-done), calls=%async_computation.2 | async-start | bytes 1835008 | tf_op jit(solution)/shard_map/all_to_all | solution.py:127
Sparse Core Ops, SparseCore 0:
  58.8 136.2 all-reduce.1
  231.1 98.7 all-gather.1
  361.6 100.9 reduce-scatter.4
  466.2 73.8 reduce-scatter.6
where the time goes:
time: 563 us; the launch traced here: 555 us
  waiting for transfers between devices  411 us (73%)
  matrix products  64.4 us (11%)
  local copies, waits for them, and re-layouts  23.7 us (4%)
  blocking collectives  18.5 us (3%)
  between operations  13.9 us (2%)
  other arithmetic  12.7 us (2%)
  starting transfers between devices  9.96 us (2%)
    psum x1, waiting for transfers between devices, shards(): lax.psum(jnp.dot(my_columns, out_weight, preferred_element_type=jnp.float...  134 us
    all_gather x1, waiting for transfers between devices, shards(): lax.all_gather(lax.all_to_all(buffer, 'group', split_axis=0, concat_axis=...  98.6 us
    reduce_scatter x1, waiting for transfers between devices, shards(): lax.psum_scatter(partial_out.astype(jnp.bfloat16), 'tensor', scatter_dime...  83.9 us
    unnamed x5, waiting for transfers between devices  72.2 us
    ppermute x3, waiting for transfers between devices, from_partner(): return lax.ppermute(block, axis, route)  23.1 us
    all_to_all x1, blocking collectives, shards(): lax.all_to_all(buffer, 'group', split_axis=0, concat_axis=0, tiled=True)  18.5 us
    dot_general x1, matrix products, shards(): jnp.dot(hidden_units, expert_down[0], preferred_element_type=jnp.float32)  13.3 us
    dot_general x1, matrix products, shards(): jnp.dot(dense_inner, dense_down, preferred_element_type=jnp.float32)  12.2 us
  transfers between devices with their start and end apart: 8, of which 6 were waited for; matrix products, arithmetic and copies ran while one was open for 4% of the time, Pallas kernels for 0%

commit v1 on v0

v1 whole, which is shorter than its diff:
```python
import functools
import math

import jax
import jax.numpy as jnp
from jax import lax
from jax.experimental import pallas as pl
from jax.experimental.pallas import tpu as pltpu
from jax.sharding import PartitionSpec as P

BF = jnp.bfloat16
F32 = jnp.float32
SIDE = 4
LANES = 128
CHUNK = 128
SLICE = 448
HALF = SLICE // 2
SHARED = 64
CHUNKS = 8


def ring(value, step):
    return lax.rem(value + step + SIDE, SIDE)


class Place:
    def __init__(self):
        rank = lax.axis_index("tensor")
        self.rank = rank
        self.z = rank // SIDE
        self.x = lax.rem(rank, SIDE)

    def axes(self, odd):
        p = self.x + odd * (self.z - self.x)
        q = self.z + odd * (self.x - self.z)
        return p, q

    def at(self, odd, p, q):
        even_rank = q * SIDE + p
        odd_rank = p * SIDE + q
        return even_rank + odd * (odd_rank - even_rank)


def spot(odd, z, x):
    return z * SIDE + x + odd * ((x * SIDE + z) - (z * SIDE + x))


def copy_to(src, dst, send, recv, rank):
    return pltpu.make_async_remote_copy(
        src_ref=src,
        dst_ref=dst,
        send_sem=send,
        recv_sem=recv,
        device_id={"tensor": rank},
        device_id_type=pl.DeviceIdType.MESH,
    )


def lanes_low(rows):
    return lax.broadcasted_iota(jnp.int32, (rows, LANES), 1) < SHARED


def turned(block):
    return pltpu.roll(block, SHARED, 1)


def unfold_pair(even_half, odd_half):
    low = lanes_low(SHARED)
    e, o = even_half.astype(F32), odd_half.astype(F32)
    top = jnp.where(low, e, o)
    bottom = turned(jnp.where(low, o, e))
    return jnp.concatenate([top, bottom], axis=0).astype(BF)


def fold_pair(tile):
    low = lanes_low(SHARED)
    top, bottom = tile[:SHARED], turned(tile[SHARED:])
    return jnp.where(low, top, bottom).astype(BF), jnp.where(low, bottom, top).astype(BF)


def unfold_own(half):
    half = half.astype(F32)
    return jnp.concatenate([half, turned(half)], axis=0)


def fold_own(tile, is_odd):
    low = lanes_low(SHARED).astype(jnp.int32) != is_odd
    top, bottom = tile[:SHARED], turned(tile[SHARED:])
    return jnp.where(low, top, bottom)


def natural_own(ref, is_odd):
    first = pl.multiple_of(is_odd * SHARED, SHARED)
    half = pl.multiple_of((1 - is_odd) * (SLICE - SHARED), SHARED)
    tiles = [ref[pl.ds(first + k * LANES, LANES), :].astype(F32) for k in range(3)]
    return jnp.concatenate(tiles + [unfold_own(ref[pl.ds(half, SHARED), :])], axis=1)


def store_own(ref, block, is_odd):
    first = pl.multiple_of(is_odd * SHARED, SHARED)
    half = pl.multiple_of((1 - is_odd) * (SLICE - SHARED), SHARED)
    for k in range(3):
        ref[pl.ds(first + k * LANES, LANES), :] = block[:, k * LANES : (k + 1) * LANES].astype(BF)
    ref[pl.ds(half, SHARED), :] = fold_own(block[:, 3 * LANES :], is_odd).astype(BF)


def store_quarter(part, odd, z, block):
    for pair in range(2):
        e, o = spot(odd, z, 2 * pair), spot(odd, z, 2 * pair + 1)
        tiles = [
            block[:, (pair * 7 + k) * LANES : (pair * 7 + k + 1) * LANES] for k in range(7)
        ]
        even_half, odd_half = fold_pair(tiles[3])
        for k in range(3):
            part[e, k * LANES : (k + 1) * LANES, :] = tiles[k].astype(BF)
            part[o, SHARED + k * LANES : SHARED + (k + 1) * LANES, :] = tiles[4 + k].astype(BF)
        part[e, SLICE - SHARED :, :] = even_half
        part[o, :SHARED, :] = odd_half


def load_quarter(part, odd, z):
    blocks = []
    for pair in range(2):
        e, o = spot(odd, z, 2 * pair), spot(odd, z, 2 * pair + 1)
        blocks += [part[e, k * LANES : (k + 1) * LANES, :] for k in range(3)]
        blocks.append(unfold_pair(part[e, SLICE - SHARED :, :], part[o, :SHARED, :]))
        blocks += [part[o, SHARED + k * LANES : SHARED + (k + 1) * LANES, :] for k in range(3)]
    return jnp.concatenate(blocks, axis=1)


def add_into(dst, other):
    dst[...] = (dst[...].astype(F32) + other[...].astype(F32)).astype(BF)


class Summer:
    def __init__(self, place, part, r1, r2, r3, r4, send, recv):
        self.place, self.part = place, part
        self.landing = (r1, r2, r3, r4)
        self.send, self.recv = send, recv

    def copies(self, step, c):
        odd = lax.rem(c, 2)
        place, part = self.place, self.part
        p, q = place.axes(odd)
        result = []
        for way, hop in ((0, 1), (1, -1)):
            if step == 0:
                src = part.at[c, pl.ds(ring(q, 2) * SIDE + 2 * way, 2)]
                to = place.at(odd, p, ring(q, hop))
            elif step == 1:
                src = part.at[c, pl.ds(ring(q, hop) * SIDE, SIDE)]
                to = place.at(odd, p, ring(q, hop))
            elif step == 2:
                src = part.at[c, q * SIDE + ring(p, 2), pl.ds(way * HALF, HALF)]
                to = place.at(odd, ring(p, hop), q)
            else:
                src = part.at[c, q * SIDE + ring(p, hop)]
                to = place.at(odd, ring(p, hop), q)
            result.append(
                copy_to(
                    src,
                    self.landing[step].at[c, way],
                    self.send.at[c, step, way],
                    self.recv.at[c, step, way],
                    to,
                )
            )
        return result

    def start(self, step, c):
        for copy in self.copies(step, c):
            copy.start()

    def arrive(self, step, c):
        for copy in self.copies(step, c):
            copy.wait_recv()
        odd = lax.rem(c, 2)
        part = self.part
        p, q = self.place.axes(odd)
        landed = self.landing[step].at[c]
        if step == 0:
            for way, hop in ((0, 1), (1, -1)):
                for k in range(2):
                    add_into(part.at[c, ring(q, hop) * SIDE + 2 * way + k], landed.at[way, k])
        elif step == 1:
            for k in range(SIDE):
                dst = part.at[c, q * SIDE + k]
                dst[...] = (
                    dst[...].astype(F32) + landed[0, k].astype(F32) + landed[1, k].astype(F32)
                ).astype(BF)
        elif step == 2:
            for way, hop in ((0, 1), (1, -1)):
                add_into(
                    part.at[c, q * SIDE + ring(p, hop), pl.ds(way * HALF, HALF)], landed.at[way]
                )

    def total(self, c):
        odd = lax.rem(c, 2)
        p, q = self.place.axes(odd)
        landed = self.landing[3].at[c]
        return (
            self.part[c, q * SIDE + p].astype(F32) + landed[0].astype(F32) + landed[1].astype(F32)
        )

    def sent(self, c):
        for step in range(4):
            for copy in self.copies(step, c):
                copy.wait_send()


class Spreader:
    def __init__(self, place, part, send, recv):
        self.place, self.part, self.send, self.recv = place, part, send, recv

    def copies(self, step, c):
        odd = lax.rem(c, 2)
        place, part = self.place, self.part
        p, q = place.axes(odd)
        result = []
        for way, hop in ((0, 1), (1, -1)):
            if step == 0:
                ref = part.at[c, q * SIDE + p]
                to = place.at(odd, ring(p, hop), q)
            elif step == 1:
                ref = part.at[c, q * SIDE + ring(p, -hop), pl.ds(way * HALF, HALF)]
                to = place.at(odd, ring(p, hop), q)
            elif step == 2:
                ref = part.at[c, pl.ds(q * SIDE, SIDE)]
                to = place.at(odd, p, ring(q, hop))
            else:
                ref = part.at[c, pl.ds(ring(q, -hop) * SIDE + 2 * way, 2)]
                to = place.at(odd, p, ring(q, hop))
            result.append(
                copy_to(
                    ref, ref, self.send.at[c, step, way], self.recv.at[c, step, way], to
                )
            )
        return result

    def start(self, step, c):
        for copy in self.copies(step, c):
            copy.start()

    def arrive(self, step, c):
        for copy in self.copies(step, c):
            copy.wait_recv()

    def sent(self, c):
        for step in range(4):
            for copy in self.copies(step, c):
                copy.wait_send()


def greet_plane(place, barrier):
    for hop in (1, -1):
        for rank in (
            place.at(0, ring(place.x, hop), place.z),
            place.at(0, place.x, ring(place.z, hop)),
        ):
            pl.semaphore_signal(
                barrier, inc=1, device_id={"tensor": rank}, device_id_type=pl.DeviceIdType.MESH
            )


def project_kernel(
    att_ref, weight_ref, residual_ref, state_ref, part, r1, r2, r3, r4, near, send, recv, local
):
    place = Place()
    barrier = pltpu.get_barrier_semaphore()
    greet_plane(place, barrier)
    pl.semaphore_wait(barrier, 4)
    is_odd = lax.rem(place.rank, 2)
    first_column = pl.multiple_of((place.rank // 2) * 2 * SLICE, 2 * SLICE)
    fetch = pltpu.make_async_copy(
        residual_ref.at[:, pl.ds(first_column, 2 * SLICE)], near, local
    )
    fetch.start()
    summer = Summer(place, part, r1, r2, r3, r4, send, recv)
    count = part.shape[0]
    for c in range(count):
        rows = att_ref[c * CHUNK : (c + 1) * CHUNK, :]

        @pl.loop(0, SIDE)
        def _(z):
            columns = pl.ds(pl.multiple_of(z * 4 * SLICE, 4 * SLICE), 4 * SLICE)
            block = jnp.dot(rows, weight_ref[:, columns], preferred_element_type=F32)
            store_quarter(part.at[c], c % 2, z, block)

        summer.start(0, c)
    for step in range(1, 4):
        for c in range(count):
            summer.arrive(step - 1, c)
            summer.start(step, c)
    fetch.wait()
    for c in range(count):
        summer.arrive(3, c)
        rows = pl.ds(c * CHUNK, CHUNK)
        even = [near[rows, k * LANES : (k + 1) * LANES] for k in range(4)]
        odd = [near[rows, (k + 3) * LANES : (k + 4) * LANES] for k in range(4)]
        whole = jnp.concatenate(
            [
                jnp.where(is_odd == 1, odd[k + 1].astype(F32), even[k].astype(F32))
                for k in range(3)
            ]
            + [even[3].astype(F32)],
            axis=1,
        )
        store_own(state_ref.at[c], whole, is_odd)
        state_ref[c] = (state_ref[c].astype(F32) + summer.total(c)).astype(BF)
    for c in range(count):
        summer.sent(c)


def project(attention, out_weight, residual):
    count = attention.shape[0] // CHUNK
    return pl.pallas_call(
        project_kernel,
        out_shape=jax.ShapeDtypeStruct((count, SLICE, LANES), BF),
        in_specs=[
            pl.BlockSpec(memory_space=pltpu.VMEM),
            pl.BlockSpec(memory_space=pltpu.VMEM),
            pl.BlockSpec(memory_space=pl.ANY),
        ],
        out_specs=pl.BlockSpec(memory_space=pltpu.VMEM),
        scratch_shapes=[
            pltpu.VMEM((count, 16, SLICE, LANES), BF),
            pltpu.VMEM((count, 2, 2, SLICE, LANES), BF),
            pltpu.VMEM((count, 2, SIDE, SLICE, LANES), BF),
            pltpu.VMEM((count, 2, HALF, LANES), BF),
            pltpu.VMEM((count, 2, SLICE, LANES), BF),
            pltpu.VMEM((attention.shape[0], 2 * SLICE), BF),
            pltpu.SemaphoreType.DMA((count, 4, 2)),
            pltpu.SemaphoreType.DMA((count, 4, 2)),
            pltpu.SemaphoreType.DMA,
        ],
        compiler_params=pltpu.CompilerParams(
            collective_id=1, has_side_effects=True, vmem_limit_bytes=48 * 1024 * 1024
        ),
        name="project",
    )(attention, out_weight, residual)


def flipped(group, bits):
    b = (lax.rem(group, 2), lax.rem(group // 2, 2), group // 4)
    return sum((b[k] + bits[k] - 2 * b[k] * bits[k]) * (1 << k) for k in range(3))


def chunk_bits(c):
    if isinstance(c, int):
        a, b, d = c % 2, (c // 2) % 2, c // 4
    else:
        a, b, d = lax.rem(c, 2), lax.rem(c // 2, 2), c // 4
    return a, b + d - 2 * b * d, d


def to_group(src, dst, send, recv, group):
    return pltpu.make_async_remote_copy(
        src_ref=src,
        dst_ref=dst,
        send_sem=send,
        recv_sem=recv,
        device_id={"group": group},
        device_id_type=pl.DeviceIdType.MESH,
    )


def feed_kernel(
    ids_ref,
    flat_ids_ref,
    route_ref,
    state_ref,
    expert_gate,
    expert_up,
    expert_down,
    dense_gate,
    dense_up,
    dense_down,
    mixed_ref,
    part,
    r1,
    r2,
    r3,
    r4,
    w_eg,
    w_eu,
    w_dg,
    w_du,
    w_down,
    outgoing,
    side_out,
    side_in,
    returned,
    own_pos,
    acc,
    hidden,
    summed,
    load_sem,
    spread_send,
    spread_recv,
    sum_send,
    sum_recv,
    go_send,
    go_recv,
    side_send,
    side_recv,
    back_send,
    back_recv,
):
    place = Place()
    group = lax.axis_index("group")
    rank = place.rank
    is_odd = lax.rem(rank, 2)
    hidden_size = w_eg.shape[1]
    rows = ids_ref.shape[0]
    row_blocks = rows // CHUNK
    width = 16 * SLICE

    loads = [
        pltpu.make_async_copy(expert_gate.at[0], w_eg, load_sem.at[0]),
        pltpu.make_async_copy(expert_up.at[0], w_eu, load_sem.at[1]),
        pltpu.make_async_copy(dense_gate, w_dg, load_sem.at[2]),
        pltpu.make_async_copy(dense_up, w_du, load_sem.at[3]),
        pltpu.make_async_copy(expert_down.at[0], w_down.at[pl.ds(0, hidden_size)], load_sem.at[4]),
        pltpu.make_async_copy(
            dense_down, w_down.at[pl.ds(DENSE_AT, hidden_size)], load_sem.at[5]
        ),
    ]
    for load in loads:
        load.start()

    barrier = pltpu.get_barrier_semaphore()
    greet_plane(place, barrier)
    for c in range(1, CHUNKS):
        pl.semaphore_signal(
            barrier,
            inc=1,
            device_id={"group": flipped(group, chunk_bits(c))},
            device_id_type=pl.DeviceIdType.MESH,
        )

    ids = ids_ref[...]
    flat_ids = flat_ids_ref[...]
    lane = lax.broadcasted_iota(jnp.int32, (rows, LANES), 1)
    partner_of_lane = sum(
        jnp.where(lane == c, flipped(group, chunk_bits(c)) + 1, 0) for c in range(CHUNKS)
    ) - 1
    first_choice = ids[:, 0:1] == partner_of_lane
    second_choice = ids[:, 1:2] == partner_of_lane
    named = jnp.where(first_choice | second_choice, 1.0, 0.0)
    line = lax.broadcasted_iota(jnp.int32, (rows, rows), 0)
    column = lax.broadcasted_iota(jnp.int32, (rows, rows), 1)
    before = jnp.where(column < line, 1.0, 0.0).astype(BF)
    place_in = jnp.dot(before, named.astype(BF), preferred_element_type=F32)
    own_pos[...] = jnp.where(named > 0.5, place_in, -1.0)

    sub = lax.broadcasted_iota(jnp.int32, (8, rows), 0)
    partner_of_sub = sum(
        jnp.where(sub == c, flipped(group, chunk_bits(c)) + 1, 0) for c in range(CHUNKS)
    ) - 1
    flat_named = jnp.where(
        (flat_ids[0:1, :] == partner_of_sub) | (flat_ids[1:2, :] == partner_of_sub), 1.0, 0.0
    )
    after = jnp.where(line < column, 1.0, 0.0).astype(BF)
    flat_place = jnp.dot(flat_named.astype(BF), after, preferred_element_type=F32)
    flat_pos = jnp.where(flat_named > 0.5, flat_place, -1.0)

    weight = jnp.where(first_choice, route_ref[:, 0:1], 0.0) + jnp.where(
        second_choice, route_ref[:, 1:2], 0.0
    )
    dense_here = jnp.where(first_choice, 1.0, 0.0)
    source = jnp.concatenate(
        [natural_own(state_ref.at[b], is_odd) for b in range(row_blocks)], axis=0
    ).astype(BF)
    slot_line = lax.broadcasted_iota(jnp.int32, (CHUNK, rows), 0).astype(F32)
    slot_lane = lax.broadcasted_iota(jnp.int32, (rows, CHUNK), 1).astype(F32)
    sides = lax.broadcasted_iota(jnp.int32, (8, LANES), 0)

    def own_spot(c):
        p, q = place.axes(lax.rem(c, 2))
        return q * SIDE + p

    def go(c):
        return [
            to_group(
                outgoing.at[c],
                part.at[c, own_spot(c)],
                go_send.at[c],
                go_recv.at[c],
                flipped(group, chunk_bits(c)),
            ),
            to_group(
                side_out.at[c],
                side_in.at[c],
                side_send.at[c],
                side_recv.at[c],
                flipped(group, chunk_bits(c)),
            ),
        ]

    for c in range(CHUNKS):
        pick = jnp.where(flat_pos[c : c + 1, :] == slot_line, 1.0, 0.0).astype(BF)
        chosen = jnp.dot(pick, source, preferred_element_type=F32)
        at_slot = own_pos[:, c : c + 1] == slot_lane
        w_row = jnp.sum(jnp.where(at_slot, weight[:, c : c + 1], 0.0), axis=0, keepdims=True)
        d_row = jnp.sum(jnp.where(at_slot, dense_here[:, c : c + 1], 0.0), axis=0, keepdims=True)
        side = jnp.where(sides == 0, w_row, jnp.where(sides == 1, d_row, 0.0))
        if c == 0:
            store_own(part.at[0, own_spot(0)], chosen, is_odd)
            side_in[0] = side
            pl.semaphore_wait(barrier, 4 + CHUNKS - 1)
        else:
            store_own(outgoing.at[c], chosen, is_odd)
            side_out[c] = side
            for copy in go(c):
                copy.start()

    spreader = Spreader(place, part, spread_send, spread_recv)
    summer = Summer(place, part, r1, r2, r3, r4, sum_send, sum_recv)

    def back(c):
        return to_group(
            summed.at[c],
            returned.at[c],
            back_send.at[c],
            back_recv.at[c],
            flipped(group, chunk_bits(c)),
        )

    def finish_sum(c):
        summer.arrive(3, c)
        total = summer.total(c).astype(BF)

        @pl.when(c == 0)
        def _():
            returned[0] = total

        @pl.when(c > 0)
        def _():
            summed[c] = total
            back(c).start()

    def compute(c):
        odd = lax.rem(c, 2)
        chunk = part.at[c]
        acc[...] = jnp.zeros_like(acc)

        def gather_products(z, squares):
            block = load_quarter(chunk, odd, z)
            deep = pl.ds(pl.multiple_of(z * 4 * SLICE, 4 * SLICE), 4 * SLICE)
            for k, w in enumerate((w_eg, w_eu, w_dg, w_du)):
                acc[k] += jnp.dot(block, w[deep, :], preferred_element_type=F32)
            for k in range(14):
                wide = block[:, k * LANES : (k + 1) * LANES].astype(F32)
                squares = squares + wide * wide
            return squares

        squares = lax.fori_loop(0, SIDE, gather_products, jnp.zeros((CHUNK, LANES), F32))
        scale = lax.rsqrt(jnp.sum(squares, axis=1, keepdims=True) / width + 1e-05)
        line = lax.broadcasted_iota(jnp.int32, (CHUNK, CHUNK), 0)
        column = lax.broadcasted_iota(jnp.int32, (CHUNK, CHUNK), 1)
        factors = [
            jnp.sum(jnp.where(line == column, side_in[c, k : k + 1, :], 0.0), axis=1, keepdims=True)
            for k in range(2)
        ]
        for k in range(2):
            gate, up = acc[2 * k] * scale, acc[2 * k + 1] * scale
            inner = gate / (1.0 + jnp.exp(-gate)) * up * factors[k]
            hidden[:, k * DENSE_AT : k * DENSE_AT + hidden_size] = inner.astype(BF)

        spreader.sent(c)

        @pl.loop(0, SIDE)
        def _(z):
            columns = pl.ds(pl.multiple_of(z * 4 * SLICE, 4 * SLICE), 4 * SLICE)
            block = jnp.dot(hidden[...], w_down[:, columns], preferred_element_type=F32)
            store_quarter(chunk, odd, z, block)

    hidden[...] = jnp.zeros_like(hidden)
    w_down[hidden_size:DENSE_AT, :] = jnp.zeros((DENSE_AT - hidden_size, width), BF)

    def turn(it, carry):
        def stage(lag, body):
            c = it - lag

            @pl.when((c >= 0) & (c < CHUNKS))
            def _():
                body(c)

        def begin(c):
            @pl.when(c > 0)
            def _():
                for copy in go(c):
                    copy.wait_recv()

            spreader.start(0, c)

        def spread(step):
            def body(c):
                spreader.arrive(step - 1, c)
                spreader.start(step, c)

            return body

        def add(step):
            def body(c):
                summer.arrive(step - 1, c)
                summer.start(step, c)

            return body

        def work(c):
            spreader.arrive(3, c)

            @pl.when(c == 0)
            def _():
                for load in loads:
                    load.wait()

            compute(c)
            summer.start(0, c)

        stage(0, begin)
        stage(1, spread(1))
        stage(2, spread(2))
        stage(3, spread(3))
        stage(5, add(1))
        stage(6, add(2))
        stage(7, add(3))
        stage(8, finish_sum)
        stage(4, work)
        return carry

    lax.fori_loop(0, CHUNKS + 8, turn, 0)

    total = jnp.concatenate(
        [natural_own(state_ref.at[b], is_odd) for b in range(row_blocks)], axis=0
    )
    for c in range(CHUNKS):
        if c > 0:
            back(c).wait_recv()
        at_slot = jnp.where(own_pos[:, c : c + 1] == slot_lane, 1.0, 0.0).astype(BF)
        block = natural_own(returned.at[c], is_odd).astype(BF)
        total = total + jnp.dot(at_slot, block, preferred_element_type=F32)
    for_odd = pltpu.roll(
        jnp.concatenate([total[:, 3 * LANES :], total[:, : 3 * LANES]], axis=1),
        4 * LANES - SHARED,
        1,
    )
    mixed_ref[...] = jnp.where(is_odd == 1, for_odd, total)[:, :SLICE].astype(BF)

    @pl.loop(0, CHUNKS)
    def _(c):
        summer.sent(c)

    for c in range(1, CHUNKS):
        for copy in go(c):
            copy.wait_send()
        back(c).wait_send()


DENSE_AT = 384


def feed(expert_ids, route_weights, state, expert_gate, expert_up, expert_down, dense_gate, dense_up, dense_down):
    rows = expert_ids.shape[0]
    width, hidden_size = dense_gate.shape
    vmem = pl.BlockSpec(memory_space=pltpu.VMEM)
    hbm = pl.BlockSpec(memory_space=pl.ANY)
    return pl.pallas_call(
        feed_kernel,
        out_shape=jax.ShapeDtypeStruct((rows, SLICE), BF),
        in_specs=[vmem] * 4 + [hbm] * 6,
        out_specs=vmem,
        scratch_shapes=[
            pltpu.VMEM((CHUNKS, 16, SLICE, LANES), BF),
            pltpu.VMEM((CHUNKS, 2, 2, SLICE, LANES), BF),
            pltpu.VMEM((CHUNKS, 2, SIDE, SLICE, LANES), BF),
            pltpu.VMEM((CHUNKS, 2, HALF, LANES), BF),
            pltpu.VMEM((CHUNKS, 2, SLICE, LANES), BF),
            pltpu.VMEM((width, hidden_size), BF),
            pltpu.VMEM((width, hidden_size), BF),
            pltpu.VMEM((width, hidden_size), BF),
            pltpu.VMEM((width, hidden_size), BF),
            pltpu.VMEM((DENSE_AT + hidden_size, width), BF),
            pltpu.VMEM((CHUNKS, SLICE, LANES), BF),
            pltpu.VMEM((CHUNKS, 8, LANES), F32),
            pltpu.VMEM((CHUNKS, 8, LANES), F32),
            pltpu.VMEM((CHUNKS, SLICE, LANES), BF),
            pltpu.VMEM((rows, LANES), F32),
            pltpu.VMEM((4, CHUNK, hidden_size), F32),
            pltpu.VMEM((CHUNK, DENSE_AT + hidden_size), BF),
            pltpu.VMEM((CHUNKS, SLICE, LANES), BF),
            pltpu.SemaphoreType.DMA((6,)),
            pltpu.SemaphoreType.DMA((CHUNKS, 4, 2)),
            pltpu.SemaphoreType.DMA((CHUNKS, 4, 2)),
            pltpu.SemaphoreType.DMA((CHUNKS, 4, 2)),
            pltpu.SemaphoreType.DMA((CHUNKS, 4, 2)),
            pltpu.SemaphoreType.DMA((CHUNKS,)),
            pltpu.SemaphoreType.DMA((CHUNKS,)),
            pltpu.SemaphoreType.DMA((CHUNKS,)),
            pltpu.SemaphoreType.DMA((CHUNKS,)),
            pltpu.SemaphoreType.DMA((CHUNKS,)),
            pltpu.SemaphoreType.DMA((CHUNKS,)),
        ],
        compiler_params=pltpu.CompilerParams(
            collective_id=2, has_side_effects=True, vmem_limit_bytes=64 * 1024 * 1024 - 65536
        ),
        name="feed",
    )(
        expert_ids,
        expert_ids.T,
        route_weights,
        state,
        expert_gate,
        expert_up,
        expert_down,
        dense_gate,
        dense_up,
        dense_down,
    )


def from_partner(block):
    return lax.ppermute(block, "tensor", [(i, i ^ 1) for i in range(lax.axis_size("tensor"))])


def attend(queries, new_kv, kv_cache, lengths):
    row_count = queries.shape[0]
    rank = lax.axis_index("tensor")
    my_head, my_part = rank // 2, rank % 2
    head_size = new_kv.shape[3]
    span = kv_cache.shape[2]
    rows = lax.dynamic_index_in_dim(queries, my_head, 1, keepdims=False).reshape(
        row_count, -1, head_size
    )
    new_key = lax.dynamic_index_in_dim(new_kv[0], my_head, 1, keepdims=False)
    new_value = lax.dynamic_index_in_dim(new_kv[1], my_head, 1, keepdims=False)
    scale = 1.0 / math.sqrt(head_size)
    scores = jnp.einsum("tgd,tpd->tgp", rows, kv_cache[0], preferred_element_type=F32) * scale
    own = jnp.einsum("tgd,td->tg", rows, new_key, preferred_element_type=F32) * scale
    position = my_part * span + jnp.arange(span, dtype=jnp.int32)
    usable = position[None, None, :] < lengths[:, None, None]
    masked = jnp.where(usable, scores, -1e30)
    highest = jnp.maximum(jnp.max(masked, axis=-1), own)
    weights = jnp.where(usable, jnp.exp(masked - highest[..., None]), 0.0).astype(BF)
    own_weight = jnp.exp(own - highest)
    leading = (my_part == 0).astype(F32)
    numerator = jnp.einsum("tgp,tpd->tgd", weights, kv_cache[1], preferred_element_type=F32)
    numerator = numerator + leading * own_weight[..., None] * new_value.astype(F32)[:, None, :]
    denominator = jnp.sum(weights.astype(F32), axis=-1) + leading * own_weight
    width = rows.shape[1] * head_size
    flat = numerator.reshape(row_count, width)
    mine = lax.dynamic_slice_in_dim(flat, my_part * (width // 2), width // 2, 1)
    theirs = lax.dynamic_slice_in_dim(flat, (1 - my_part) * (width // 2), width // 2, 1)
    other, other_marks = from_partner((theirs.astype(BF), jnp.stack([highest, denominator])))
    other_highest, other_denominator = other_marks[0], other_marks[1]
    top = jnp.maximum(highest, other_highest)
    keep, take = jnp.exp(highest - top), jnp.exp(other_highest - top)
    below = 1.0 / (denominator * keep + other_denominator * take)
    keep = jnp.repeat(keep * below, head_size, axis=1)
    take = jnp.repeat(take * below, head_size, axis=1)
    keep = lax.dynamic_slice_in_dim(keep, my_part * (width // 2), width // 2, 1)
    take = lax.dynamic_slice_in_dim(take, my_part * (width // 2), width // 2, 1)
    return (mine * keep + other.astype(F32) * take).astype(BF)


def shards(
    residual,
    queries,
    new_kv,
    kv_cache,
    lengths,
    out_weight,
    dense_gate,
    dense_up,
    dense_down,
    expert_ids,
    route_weights,
    expert_gate,
    expert_up,
    expert_down,
):
    attention = attend(queries, new_kv, kv_cache, lengths)
    state = project(attention, out_weight, residual)
    return feed(
        expert_ids,
        route_weights,
        state,
        expert_gate,
        expert_up,
        expert_down,
        dense_gate,
        dense_up,
        dense_down,
    )


def solution(mesh):
    placed = (
        P("group", None),
        P("group", None, None),
        P(None, "group", None, None),
        P(None, "group", "tensor", None),
        P("group"),
        P("tensor", None),
        P(None, "tensor"),
        P(None, "tensor"),
        P("tensor", None),
        P("group", None),
        P("group", None),
        P("group", None, "tensor"),
        P("group", None, "tensor"),
        P("group", "tensor", None),
    )
    return jax.shard_map(
        shards, mesh=mesh, in_specs=placed, out_specs=P("group", "tensor"), check_vma=False
    )
```

time: 563 us -> 288 us (0.51); the launches traced: 555 us -> 287 us
  waiting for transfers between devices: 411 us -> 0.01 us
  Pallas kernels: 0 us -> 233 us
  matrix products: 64.4 us -> 8.02 us
  local copies, waits for them, and re-layouts: 23.7 us -> 42.5 us
  blocking collectives: 18.5 us -> 0 us
  between operations: 13.9 us -> 0.29 us
  other arithmetic: 12.7 us -> 1.34 us
  starting transfers between devices: 9.96 us -> 2.4 us
    pallas_call x0 -> x2, Pallas kernels: none -> 233 us  [the longest x1 198 us: feed(): pl.pallas_call(feed_kernel, out_shape=jax.ShapeDtypeStruct((rows, SLICE),...]
    psum x1 -> x0, waiting for transfers between devices: 134 us -> none  [shards(): lax.psum(jnp.dot(my_columns, out_weight, preferred_element_type=jnp.float...]
    all_gather x1 -> x0, waiting for transfers between devices: 98.6 us -> none  [shards(): lax.all_gather(lax.all_to_all(buffer, 'group', split_axis=0, concat_axis=...]
    reduce_scatter x1 -> x0, waiting for transfers between devices: 83.9 us -> none  [shards(): lax.psum_scatter(partial_out.astype(jnp.bfloat16), 'tensor', scatter_dime...]
    unnamed x5 -> x0, waiting for transfers between devices: 72.2 us -> none
    dot_general x9 -> x3, matrix products: 64.4 us -> 8.02 us  [the longest x1 4.55 us: attend(): jnp.einsum('tgd,tpd->tgp', rows, kv_cache[0], preferred_element_type=F32)]
    unnamed x19 -> x24, local copies, waits for them, and re-layouts: 6.91 us -> 36.1 us
    ppermute x3 -> x2, waiting for transfers between devices: 23.1 us -> 0.01 us  [from_partner(): lax.ppermute(block, 'tensor', [(i, i ^ 1) for i in range(lax.axis_size('t...]
  transfers between devices with their start and end apart: 8 -> 2, of which waited for: 6 -> 0; matrix products, arithmetic and copies ran while one was open for 4% -> 12% of each run, Pallas kernels for 0% -> 0%
where the time goes in v1:
time: 288 us; the launch traced here: 287 us
  Pallas kernels  233 us (81%)
  local copies, waits for them, and re-layouts  42.5 us (15%)
  matrix products  8.02 us (3%)
    pallas_call x1, Pallas kernels, feed(): pl.pallas_call(feed_kernel, out_shape=jax.ShapeDtypeStruct((rows, SLICE),...  198 us
    unnamed x24, local copies, waits for them, and re-layouts  36.1 us
    pallas_call x1, Pallas kernels, project(): pl.pallas_call(project_kernel, out_shape=jax.ShapeDtypeStruct((count, SLI...  34.7 us
  transfers between devices with their start and end apart: 2, of which 0 were waited for; matrix products, arithmetic and copies ran while one was open for 12% of the time, Pallas kernels for 0%

profile of v1, /device:TPU:1, one launch (start us, length us, event | category | flops | bytes accessed | tf_op | source)
XLA Modules:
  0.0 287.3 jit_solution(1425638576837760477)
XLA Ops:
  0.0 3.1 %constant_dynamic-slice_fusion.5 = bf16[256,1,896]{2,1,0:T(2,128)(2,1)S(1)} fusion(bf16[256,8,896]{2,1,0:T(8,128)(2,1)} %param.15, s32[]{:T(128)S(6)} %select_n.35), kind=kLoop, calls=%fused_computation.37 | loop fusion | bytes 917508 | tf_op jit(solution)/shard_map/jit(dynamic_index_in_dim)/dynamic_slice | solution.py:733
  3.1 1.3 copy.116
  4.4 0.3 copy.96
  4.8 0.2 dynamic-slice_convert_fusion
  5.1 0.4 fusion.15
  5.7 4.5 %fusion.27 = (f32[256,7]{1,0:T(8,128)S(1)}, f32[256,7,64]{2,1,0:T(8,128)S(1)}) fusion(bf16[256,7,128]{2,1,0:T(8,128)(2,1)S(1)} %copy.96, bf16[2,256,64,128]{3,2,1,0:T(8,128)(2,1)} %param.17, pred[256,64]{1,0:T(8,128)(4,1)S(1)} %broadcast_compare_fusion), kind=kOutput, calls=%fused_computation.41 | convolution fusion | flops 29702400 | bytes 5135360 | tf_op jit(solution)/shard_map/tgd,tpd->tgp/dot_general | solution.py:739
  10.5 0.7 convert_reduce_fusion
  11.3 2.1 collective-permute-start
  13.6 3.1 %fusion.12 = f32[256,7,128]{2,1,0:T(8,128)S(1)} fusion(bf16[2,256,64,128]{3,2,1,0:T(8,128)(2,1)} %param.17, f32[256,128]{1,0:T(8,128)S(1)} %bitcast.71, f32[256,7]{1,0:T(8,128)S(1)} %copy.100, f32[256,7,64]{2,1,0:T(8,128)S(1)} %get-tuple-element.12, f32[256,7]{1,0:T(8,128)S(1)} %copy.99, pred[256,64]{1,0:T(8,128)(4,1)S(1)} %broadcast_compare_fusion), kind=kOutput, calls=%fused_computation.8 | convolution fusion | flops 30162944 | bytes 5732352 | tf_op jit(solution)/shard_map/tgp,tpd->tgd/dot_general | solution.py:748
  16.7 0.4 copy.101
  17.3 0.3 collective-permute-start.1
  17.6 0.8 copy.108.route_ref
  18.4 0.8 copy.107.ids_ref
  19.4 7.4 %copy.111.dense_gate = bf16[7168,304]{1,0:T(8,128)(2,1)} copy(bf16[7168,304]{0,1:T(8,128)(2,1)} %param.20) | data formatting | bytes 8716288 | tf_op args[6]
  26.8 7.4 %copy.112.dense_up = bf16[7168,304]{1,0:T(8,128)(2,1)} copy(bf16[7168,304]{0,1:T(8,128)(2,1)} %param.21) | data formatting | bytes 8716288 | tf_op args[7]
  34.2 7.4 %copy.109.expert_gate = bf16[1,7168,304]{2,1,0:T(8,128)(2,1)} copy(bf16[1,7168,304]{1,2,0:T(8,128)(2,1)} %param.25) | data formatting | bytes 8716288 | tf_op args[11]
  41.7 7.4 %copy.110.expert_up = bf16[1,7168,304]{2,1,0:T(8,128)(2,1)} copy(bf16[1,7168,304]{1,2,0:T(8,128)(2,1)} %param.26) | data formatting | bytes 8716288 | tf_op args[12]
  49.3 0.2 copy.120
  49.6 0.2 copy.122
  50.0 2.0 copy-done
  52.1 34.7 %project.1.state_ref = bf16[2,448,128]{2,1,0:T(8,128)(2,1)S(1)} custom-call(bf16[256,448]{1,0:T(8,128)(2,1)S(1)} %add_convert_fusion.att_ref, bf16[448,7168]{1,0:T(8,128)(2,1)} %weight_ref.1, bf16[256,7168]{1,0:T(8,128)(2,1)S(1)} %copy-done), custom_call_target="tpu_custom_call" | custom-call | tf_op jit(solution)/shard_map/project/pallas_call | solution.py:316
  86.7 0.7 copy-done.1
  87.4 198.1 %feed.1 = bf16[256,448]{1,0:T(8,128)(2,1)} custom-call(s32[256,2]{1,0:T(8,128)} %copy.107.ids_ref, s32[2,256]{1,0:T(2,128)} %bitcast.75, f32[256,2]{1,0:T(8,128)} %copy.108.route_ref, bf16[2,448,128]{2,1,0:T(8,128)(2,1)} %copy-done.1, bf16[1,7168,304]{2,1,0:T(8,128)(2,1)} %copy.109.expert_gate, bf16[1,7168,304]{2,1,0:T(8,128)(2,1)} %copy.110.expert_up, ...), custom_call_target="tpu_custom_call" | custom-call | tf_op jit(solution)/shard_map/feed/pallas_call | solution.py:669
  285.5 1.8 copy.113
  (34 shorter events, 1.6 us)
Async XLA Ops:
  0.0 4.7 %copy-start.2 = (bf16[2,256,8,128]{3,2,1,0:T(8,128)(2,1)S(1)}, bf16[2,256,8,128]{3,2,1,0:T(8,128)(2,1)}, u32[]{:S(2)}) copy-start(bf16[2,256,8,128]{3,2,1,0:T(8,128)(2,1)} %param.16) | copy-start | bytes 3145732
  0.0 5.6 %copy-start.5 = (s32[256]{0:T(256)S(1)}, s32[256]{0:T(256)}, u32[]{:S(2)}) copy-start(s32[256]{0:T(256)} %param.18) | copy-start | bytes 3076
  11.3 37.8 %collective-permute-start = (f32[2,256,7]{1,2,0:T(8,128)S(1)}, f32[2,256,7]{1,2,0:T(8,128)S(1)}, u32[]{:S(2)}, u32[]{:S(2)}) collective-permute-start(f32[2,256,7]{1,2,0:T(8,128)S(1)} %pad_maximum_fusion), channel_id=1, source_target_pairs={{0,1},{1,0},{2,3},{3,2},{4,5},{5,4},{6,7},{7,6},{8,9},{9,8},{10,11... | collective-permute-start | bytes 43016 | tf_op jit(solution)/shard_map/ppermute | solution.py:724
  13.6 4.0 %copy-start.4 = (f32[256,2]{0,1:T(2,128)S(1)}, f32[256,2]{0,1:T(2,128)}, u32[]{:S(2)}) copy-start(f32[256,2]{0,1:T(2,128)} %param.24) | copy-start | bytes 6148
  13.6 4.8 %copy-start.3 = (s32[256,2]{0,1:T(2,128)S(1)}, s32[256,2]{0,1:T(2,128)}, u32[]{:S(2)}) copy-start(s32[256,2]{0,1:T(2,128)} %param.23) | copy-start | bytes 6148
  17.3 32.5 %collective-permute-start.1 = (bf16[256,448]{1,0:T(8,128)(2,1)S(1)}, bf16[256,448]{1,0:T(8,128)(2,1)S(1)}, u32[]{:S(2)}, u32[]{:S(2)}) collective-permute-start(bf16[256,448]{1,0:T(8,128)(2,1)S(1)} %copy.121), channel_id=1, source_target_pairs={{0,1},{1,0},{2,3},{3,2},{4,5},{5,4},{6,7},{7,6},{8,9},{9,8},{10,11... | collective-permute-start | bytes 688136 | tf_op jit(solution)/shard_map/ppermute | solution.py:724
  50.0 2.0 copy-start
  86.7 0.7 copy-start.1

commit v2 on v1

--- a/solution.py
+++ b/solution.py
@@ -30,19 +30,35 @@
         self.z = rank // SIDE
         self.x = lax.rem(rank, SIDE)
 
-    def axes(self, odd):
-        p = self.x + odd * (self.z - self.x)
-        q = self.z + odd * (self.x - self.z)
-        return p, q
-
-    def at(self, odd, p, q):
-        even_rank = q * SIDE + p
-        odd_rank = p * SIDE + q
-        return even_rank + odd * (odd_rank - even_rank)
-
-
-def spot(odd, z, x):
-    return z * SIDE + x + odd * ((x * SIDE + z) - (z * SIDE + x))
+    def axes(self, half):
+        return (self.x, self.z) if half == 0 else (self.z, self.x)
+
+    def at(self, half, p, q):
+        return q * SIDE + p if half == 0 else p * SIDE + q
+
+
+def spot(half, z, x):
+    return z * SIDE + x if half == 0 else x * SIDE + z
+
+
+def split_rows(low, high):
+    pieces = []
+    if low < HALF:
+        pieces.append((0, low, min(high, HALF), 0))
+    if high > HALF:
+        start = max(low, HALF)
+        pieces.append((1, start - HALF, high - HALF, start - low))
+    return pieces
+
+
+def read_rows(part, z, x, low, high):
+    pieces = [part[h, spot(h, z, x), a:b, :] for h, a, b, _ in split_rows(low, high)]
+    return pieces[0] if len(pieces) == 1 else jnp.concatenate(pieces, axis=0)
+
+
+def write_rows(part, z, x, low, value):
+    for h, a, b, offset in split_rows(low, low + value.shape[0]):
+        part[h, spot(h, z, x), a:b, :] = value[offset : offset + b - a]
 
 
 def copy_to(src, dst, send, recv, rank):
@@ -104,27 +120,33 @@
     ref[pl.ds(half, SHARED), :] = fold_own(block[:, 3 * LANES :], is_odd).astype(BF)
 
 
-def store_quarter(part, odd, z, block):
+def store_quarter(part, z, block):
     for pair in range(2):
-        e, o = spot(odd, z, 2 * pair), spot(odd, z, 2 * pair + 1)
+        e, o = 2 * pair, 2 * pair + 1
         tiles = [
             block[:, (pair * 7 + k) * LANES : (pair * 7 + k + 1) * LANES] for k in range(7)
         ]
         even_half, odd_half = fold_pair(tiles[3])
         for k in range(3):
-            part[e, k * LANES : (k + 1) * LANES, :] = tiles[k].astype(BF)
-            part[o, SHARED + k * LANES : SHARED + (k + 1) * LANES, :] = tiles[4 + k].astype(BF)
-        part[e, SLICE - SHARED :, :] = even_half
-        part[o, :SHARED, :] = odd_half
-
-
-def load_quarter(part, odd, z):
+            write_rows(part, z, e, k * LANES, tiles[k].astype(BF))
+            write_rows(part, z, o, SHARED + k * LANES, tiles[4 + k].astype(BF))
+        write_rows(part, z, e, SLICE - SHARED, even_half)
+        write_rows(part, z, o, 0, odd_half)
+
+
+def load_quarter(part, z):
     blocks = []
     for pair in range(2):
-        e, o = spot(odd, z, 2 * pair), spot(odd, z, 2 * pair + 1)
-        blocks += [part[e, k * LANES : (k + 1) * LANES, :] for k in range(3)]
-        blocks.append(unfold_pair(part[e, SLICE - SHARED :, :], part[o, :SHARED, :]))
-        blocks += [part[o, SHARED + k * LANES : SHARED + (k + 1) * LANES, :] for k in range(3)]
+        e, o = 2 * pair, 2 * pair + 1
+        blocks += [read_rows(part, z, e, k * LANES, (k + 1) * LANES) for k in range(3)]
+        blocks.append(
+            unfold_pair(
+                read_rows(part, z, e, SLICE - SHARED, SLICE), read_rows(part, z, o, 0, SHARED)
+            )
+        )
+        blocks += [
+            read_rows(part, z, o, SHARED + k * LANES, SHARED + (k + 1) * LANES) for k in range(3)
+        ]
     return jnp.concatenate(blocks, axis=1)
 
 
@@ -132,123 +154,126 @@
     dst[...] = (dst[...].astype(F32) + other[...].astype(F32)).astype(BF)
 
 
-class Summer:
-    def __init__(self, place, part, r1, r2, r3, r4, send, recv):
-        self.place, self.part = place, part
-        self.landing = (r1, r2, r3, r4)
+class Exchange:
+    def start(self, step, c):
+        for copy in self.copies(step, c):
+            copy.start()
+
+    def arrive(self, step, c):
+        for copy in self.copies(step, c):
+            copy.wait_recv()
+
+    def sent(self, c):
+        for step in range(4):
+            for copy in self.copies(step, c):
+                copy.wait_send()
+
+
+WAYS = ((0, 0, 1), (0, 1, -1), (1, 0, 1), (1, 1, -1))
+QUARTER = HALF // 2
+
+
+class Summer(Exchange):
+    def __init__(self, place, part, landing, send, recv):
+        self.place, self.part, self.landing = place, part, landing
         self.send, self.recv = send, recv
 
     def copies(self, step, c):
-        odd = lax.rem(c, 2)
-        place, part = self.place, self.part
-        p, q = place.axes(odd)
+        place = self.place
         result = []
-        for way, hop in ((0, 1), (1, -1)):
+        for h, way, hop in WAYS:
+            part = self.part.at[c, h]
+            p, q = place.axes(h)
             if step == 0:
-                src = part.at[c, pl.ds(ring(q, 2) * SIDE + 2 * way, 2)]
-                to = place.at(odd, p, ring(q, hop))
+                src = part.at[pl.ds(ring(q, 2) * SIDE + 2 * way, 2)]
+                to = place.at(h, p, ring(q, hop))
             elif step == 1:
-                src = part.at[c, pl.ds(ring(q, hop) * SIDE, SIDE)]
-                to = place.at(odd, p, ring(q, hop))
+                src = part.at[pl.ds(ring(q, hop) * SIDE, SIDE)]
+                to = place.at(h, p, ring(q, hop))
             elif step == 2:
-                src = part.at[c, q * SIDE + ring(p, 2), pl.ds(way * HALF, HALF)]
-                to = place.at(odd, ring(p, hop), q)
+                src = part.at[q * SIDE + ring(p, 2), pl.ds(way * QUARTER, QUARTER)]
+                to = place.at(h, ring(p, hop), q)
             else:
-                src = part.at[c, q * SIDE + ring(p, hop)]
-                to = place.at(odd, ring(p, hop), q)
+                src = part.at[q * SIDE + ring(p, hop)]
+                to = place.at(h, ring(p, hop), q)
             result.append(
                 copy_to(
                     src,
-                    self.landing[step].at[c, way],
-                    self.send.at[c, step, way],
-                    self.recv.at[c, step, way],
+                    self.landing[step].at[c, h, way],
+                    self.send.at[c, step, h, way],
+                    self.recv.at[c, step, h, way],
                     to,
                 )
             )
         return result
 
-    def start(self, step, c):
-        for copy in self.copies(step, c):
-            copy.start()
-
-    def arrive(self, step, c):
-        for copy in self.copies(step, c):
-            copy.wait_recv()
-        odd = lax.rem(c, 2)
-        part = self.part
-        p, q = self.place.axes(odd)
-        landed = self.landing[step].at[c]
-        if step == 0:
-            for way, hop in ((0, 1), (1, -1)):
-                for k in range(2):
-                    add_into(part.at[c, ring(q, hop) * SIDE + 2 * way + k], landed.at[way, k])
-        elif step == 1:
-            for k in range(SIDE):
-                dst = part.at[c, q * SIDE + k]
-                dst[...] = (
-                    dst[...].astype(F32) + landed[0, k].astype(F32) + landed[1, k].astype(F32)
-                ).astype(BF)
-        elif step == 2:
-            for way, hop in ((0, 1), (1, -1)):
-                add_into(
-                    part.at[c, q * SIDE + ring(p, hop), pl.ds(way * HALF, HALF)], landed.at[way]
-                )
+    def add(self, step, c):
+        for h in range(2):
+            part = self.part.at[c, h]
+            p, q = self.place.axes(h)
+            landed = self.landing[step].at[c, h]
+            if step == 0:
+                for way, hop in ((0, 1), (1, -1)):
+                    for k in range(2):
+                        add_into(part.at[ring(q, hop) * SIDE + 2 * way + k], landed.at[way, k])
+            elif step == 1:
+                for k in range(SIDE):
+                    dst = part.at[q * SIDE + k]
+                    dst[...] = (
+                        dst[...].astype(F32) + landed[0, k].astype(F32) + landed[1, k].astype(F32)
+                    ).astype(BF)
+            elif step == 2:
+                for way, hop in ((0, 1), (1, -1)):
+                    add_into(
+                        part.at[q * SIDE + ring(p, hop), pl.ds(way * QUARTER, QUARTER)],
+                        landed.at[way],
+                    )
 
     def total(self, c):
-        odd = lax.rem(c, 2)
-        p, q = self.place.axes(odd)
-        landed = self.landing[3].at[c]
-        return (
-            self.part[c, q * SIDE + p].astype(F32) + landed[0].astype(F32) + landed[1].astype(F32)
-        )
-
-    def sent(self, c):
-        for step in range(4):
-            for copy in self.copies(step, c):
-                copy.wait_send()
-
-
-class Spreader:
+        halves = []
+        for h in range(2):
+            p, q = self.place.axes(h)
+            landed = self.landing[3].at[c, h]
+            halves.append(
+                self.part[c, h, q * SIDE + p].astype(F32)
+                + landed[0].astype(F32)
+                + landed[1].astype(F32)
+            )
+        return jnp.concatenate(halves, axis=0)
+
+
+class Spreader(Exchange):
     def __init__(self, place, part, send, recv):
         self.place, self.part, self.send, self.recv = place, part, send, recv
 
     def copies(self, step, c):
-        odd = lax.rem(c, 2)
-        place, part = self.place, self.part
-        p, q = place.axes(odd)
+        place = self.place
         result = []
-        for way, hop in ((0, 1), (1, -1)):
+        for h, way, hop in WAYS:
+            part = self.part.at[c, h]
+            p, q = place.axes(h)
             if step == 0:
-                ref = part.at[c, q * SIDE + p]
-                to = place.at(odd, ring(p, hop), q)
+                ref = part.at[q * SIDE + p]
+                to = place.at(h, ring(p, hop), q)
             elif step == 1:
-                ref = part.at[c, q * SIDE + ring(p, -hop), pl.ds(way * HALF, HALF)]
-                to = place.at(odd, ring(p, hop), q)
+                ref = part.at[q * SIDE + ring(p, -hop), pl.ds(way * QUARTER, QUARTER)]
+                to = place.at(h, ring(p, hop), q)
             elif step == 2:
-                ref = part.at[c, pl.ds(q * SIDE, SIDE)]
-                to = place.at(odd, p, ring(q, hop))
+                ref = part.at[pl.ds(q * SIDE, SIDE)]
+                to = place.at(h, p, ring(q, hop))
             else:
-                ref = part.at[c, pl.ds(ring(q, -hop) * SIDE + 2 * way, 2)]
-                to = place.at(odd, p, ring(q, hop))
+                ref = part.at[pl.ds(ring(q, -hop) * SIDE + 2 * way, 2)]
+                to = place.at(h, p, ring(q, hop))
             result.append(
                 copy_to(
-                    ref, ref, self.send.at[c, step, way], self.recv.at[c, step, way], to
+                    ref,
+                    ref,
+                    self.send.at[c, step, h, way],
+                    self.recv.at[c, step, h, way],
+                    to,
                 )
             )
         return result
-
-    def start(self, step, c):
-        for copy in self.copies(step, c):
-            copy.start()
-
-    def arrive(self, step, c):
-        for copy in self.copies(step, c):
-            copy.wait_recv()
-
-    def sent(self, c):
-        for step in range(4):
-            for copy in self.copies(step, c):
-                copy.wait_send()
 
 
 def greet_plane(place, barrier):
@@ -275,7 +300,7 @@
         residual_ref.at[:, pl.ds(first_column, 2 * SLICE)], near, local
     )
     fetch.start()
-    summer = Summer(place, part, r1, r2, r3, r4, send, recv)
+    summer = Summer(place, part, (r1, r2, r3, r4), send, recv)
     count = part.shape[0]
     for c in range(count):
         rows = att_ref[c * CHUNK : (c + 1) * CHUNK, :]
@@ -284,12 +309,13 @@
         def _(z):
             columns = pl.ds(pl.multiple_of(z * 4 * SLICE, 4 * SLICE), 4 * SLICE)
             block = jnp.dot(rows, weight_ref[:, columns], preferred_element_type=F32)
-            store_quarter(part.at[c], c % 2, z, block)
+            store_quarter(part.at[c], z, block)
 
         summer.start(0, c)
     for step in range(1, 4):
         for c in range(count):
             summer.arrive(step - 1, c)
+            summer.add(step - 1, c)
             summer.start(step, c)
     fetch.wait()
     for c in range(count):
@@ -323,14 +349,14 @@
         ],
         out_specs=pl.BlockSpec(memory_space=pltpu.VMEM),
         scratch_shapes=[
-            pltpu.VMEM((count, 16, SLICE, LANES), BF),
-            pltpu.VMEM((count, 2, 2, SLICE, LANES), BF),
-            pltpu.VMEM((count, 2, SIDE, SLICE, LANES), BF),
-            pltpu.VMEM((count, 2, HALF, LANES), BF),
-            pltpu.VMEM((count, 2, SLICE, LANES), BF),
+            pltpu.VMEM((count, 2, 16, HALF, LANES), BF),
+            pltpu.VMEM((count, 2, 2, 2, HALF, LANES), BF),
+            pltpu.VMEM((count, 2, 2, SIDE, HALF, LANES), BF),
+            pltpu.VMEM((count, 2, 2, QUARTER, LANES), BF),
+            pltpu.VMEM((count, 2, 2, HALF, LANES), BF),
             pltpu.VMEM((attention.shape[0], 2 * SLICE), BF),
-            pltpu.SemaphoreType.DMA((count, 4, 2)),
-            pltpu.SemaphoreType.DMA((count, 4, 2)),
+            pltpu.SemaphoreType.DMA((count, 4, 2, 2)),
+            pltpu.SemaphoreType.DMA((count, 4, 2, 2)),
             pltpu.SemaphoreType.DMA,
         ],
         compiler_params=pltpu.CompilerParams(
@@ -381,10 +407,7 @@
     r2,
     r3,
     r4,
-    w_eg,
-    w_eu,
-    w_dg,
-    w_du,
+    w_in,
     w_down,
     outgoing,
     side_out,
@@ -410,16 +433,17 @@
     group = lax.axis_index("group")
     rank = place.rank
     is_odd = lax.rem(rank, 2)
-    hidden_size = w_eg.shape[1]
+    hidden_size = w_in.shape[0] // 4
     rows = ids_ref.shape[0]
     row_blocks = rows // CHUNK
     width = 16 * SLICE
 
     loads = [
-        pltpu.make_async_copy(expert_gate.at[0], w_eg, load_sem.at[0]),
-        pltpu.make_async_copy(expert_up.at[0], w_eu, load_sem.at[1]),
-        pltpu.make_async_copy(dense_gate, w_dg, load_sem.at[2]),
-        pltpu.make_async_copy(dense_up, w_du, load_sem.at[3]),
+        pltpu.make_async_copy(
+            ref, w_in.at[pl.ds(k * hidden_size, hidden_size)], load_sem.at[k]
+        )
+        for k, ref in enumerate((expert_gate.at[0], expert_up.at[0], dense_gate, dense_up))
+    ] + [
         pltpu.make_async_copy(expert_down.at[0], w_down.at[pl.ds(0, hidden_size)], load_sem.at[4]),
         pltpu.make_async_copy(
             dense_down, w_down.at[pl.ds(DENSE_AT, hidden_size)], load_sem.at[5]
@@ -475,27 +499,18 @@
     slot_lane = lax.broadcasted_iota(jnp.int32, (rows, CHUNK), 1).astype(F32)
     sides = lax.broadcasted_iota(jnp.int32, (8, LANES), 0)
 
-    def own_spot(c):
-        p, q = place.axes(lax.rem(c, 2))
-        return q * SIDE + p
-
     def go(c):
+        to = flipped(group, chunk_bits(c))
         return [
             to_group(
-                outgoing.at[c],
-                part.at[c, own_spot(c)],
-                go_send.at[c],
-                go_recv.at[c],
-                flipped(group, chunk_bits(c)),
-            ),
-            to_group(
-                side_out.at[c],
-                side_in.at[c],
-                side_send.at[c],
-                side_recv.at[c],
-                flipped(group, chunk_bits(c)),
-            ),
-        ]
+                outgoing.at[c, pl.ds(h * HALF, HALF)],
+                part.at[c, h, spot(h, place.z, place.x)],
+                go_send.at[c, h],
+                go_recv.at[c, h],
+                to,
+            )
+            for h in range(2)
+        ] + [to_group(side_out.at[c], side_in.at[c], side_send.at[c], side_recv.at[c], to)]
 
     for c in range(CHUNKS):
         pick = jnp.where(flat_pos[c : c + 1, :] == slot_line, 1.0, 0.0).astype(BF)
@@ -504,18 +519,19 @@
         w_row = jnp.sum(jnp.where(at_slot, weight[:, c : c + 1], 0.0), axis=0, keepdims=True)
         d_row = jnp.sum(jnp.where(at_slot, dense_here[:, c : c + 1], 0.0), axis=0, keepdims=True)
         side = jnp.where(sides == 0, w_row, jnp.where(sides == 1, d_row, 0.0))
+        store_own(outgoing.at[c], chosen, is_odd)
         if c == 0:
-            store_own(part.at[0, own_spot(0)], chosen, is_odd)
+            for h in range(2):
+                part[0, h, spot(h, place.z, place.x)] = outgoing[0, h * HALF : (h + 1) * HALF, :]
             side_in[0] = side
             pl.semaphore_wait(barrier, 4 + CHUNKS - 1)
         else:
-            store_own(outgoing.at[c], chosen, is_odd)
             side_out[c] = side
             for copy in go(c):
                 copy.start()
 
     spreader = Spreader(place, part, spread_send, spread_recv)
-    summer = Summer(place, part, r1, r2, r3, r4, sum_send, sum_recv)
+    summer = Summer(place, part, (r1, r2, r3, r4), sum_send, sum_recv)
 
     def back(c):
         return to_group(
@@ -540,15 +556,15 @@
             back(c).start()
 
     def compute(c):
-        odd = lax.rem(c, 2)
         chunk = part.at[c]
         acc[...] = jnp.zeros_like(acc)
 
         def gather_products(z, squares):
-            block = load_quarter(chunk, odd, z)
+            block = load_quarter(chunk, z)
             deep = pl.ds(pl.multiple_of(z * 4 * SLICE, 4 * SLICE), 4 * SLICE)
-            for k, w in enumerate((w_eg, w_eu, w_dg, w_du)):
-                acc[k] += jnp.dot(block, w[deep, :], preferred_element_type=F32)
+            acc[...] += lax.dot_general(
+                block, w_in[:, deep], (((1,), (1,)), ((), ())), preferred_element_type=F32
+            )
             for k in range(14):
                 wide = block[:, k * LANES : (k + 1) * LANES].astype(F32)
                 squares = squares + wide * wide
@@ -563,7 +579,10 @@
             for k in range(2)
         ]
         for k in range(2):
-            gate, up = acc[2 * k] * scale, acc[2 * k + 1] * scale
+            gate, up = [
+                acc[:, (2 * k + j) * hidden_size : (2 * k + j + 1) * hidden_size] * scale
+                for j in range(2)
+            ]
             inner = gate / (1.0 + jnp.exp(-gate)) * up * factors[k]
             hidden[:, k * DENSE_AT : k * DENSE_AT + hidden_size] = inner.astype(BF)
 
@@ -573,7 +592,7 @@
         def _(z):
             columns = pl.ds(pl.multiple_of(z * 4 * SLICE, 4 * SLICE), 4 * SLICE)
             block = jnp.dot(hidden[...], w_down[:, columns], preferred_element_type=F32)
-            store_quarter(chunk, odd, z, block)
+            store_quarter(chunk, z, block)
 
     hidden[...] = jnp.zeros_like(hidden)
     w_down[hidden_size:DENSE_AT, :] = jnp.zeros((DENSE_AT - hidden_size, width), BF)
@@ -604,6 +623,7 @@
         def add(step):
             def body(c):
                 summer.arrive(step - 1, c)
+                summer.add(step - 1, c)
                 summer.start(step, c)
 
             return body
@@ -672,31 +692,28 @@
         in_specs=[vmem] * 4 + [hbm] * 6,
         out_specs=vmem,
         scratch_shapes=[
-            pltpu.VMEM((CHUNKS, 16, SLICE, LANES), BF),
-            pltpu.VMEM((CHUNKS, 2, 2, SLICE, LANES), BF),
-            pltpu.VMEM((CHUNKS, 2, SIDE, SLICE, LANES), BF),
-            pltpu.VMEM((CHUNKS, 2, HALF, LANES), BF),
-            pltpu.VMEM((CHUNKS, 2, SLICE, LANES), BF),
-            pltpu.VMEM((width, hidden_size), BF),
-            pltpu.VMEM((width, hidden_size), BF),
-            pltpu.VMEM((width, hidden_size), BF),
-            pltpu.VMEM((width, hidden_size), BF),
+            pltpu.VMEM((CHUNKS, 2, 16, HALF, LANES), BF),
+            pltpu.VMEM((CHUNKS, 2, 2, 2, HALF, LANES), BF),
+            pltpu.VMEM((CHUNKS, 2, 2, SIDE, HALF, LANES), BF),
+            pltpu.VMEM((CHUNKS, 2, 2, QUARTER, LANES), BF),
+            pltpu.VMEM((CHUNKS, 2, 2, HALF, LANES), BF),
+            pltpu.VMEM((4 * hidden_size, width), BF),
             pltpu.VMEM((DENSE_AT + hidden_size, width), BF),
             pltpu.VMEM((CHUNKS, SLICE, LANES), BF),
             pltpu.VMEM((CHUNKS, 8, LANES), F32),
             pltpu.VMEM((CHUNKS, 8, LANES), F32),
             pltpu.VMEM((CHUNKS, SLICE, LANES), BF),
             pltpu.VMEM((rows, LANES), F32),
-            pltpu.VMEM((4, CHUNK, hidden_size), F32),
+            pltpu.VMEM((CHUNK, 4 * hidden_size), F32),
             pltpu.VMEM((CHUNK, DENSE_AT + hidden_size), BF),
             pltpu.VMEM((CHUNKS, SLICE, LANES), BF),
             pltpu.SemaphoreType.DMA((6,)),
-            pltpu.SemaphoreType.DMA((CHUNKS, 4, 2)),
-            pltpu.SemaphoreType.DMA((CHUNKS, 4, 2)),
-            pltpu.SemaphoreType.DMA((CHUNKS, 4, 2)),
-            pltpu.SemaphoreType.DMA((CHUNKS, 4, 2)),
-            pltpu.SemaphoreType.DMA((CHUNKS,)),
-            pltpu.SemaphoreType.DMA((CHUNKS,)),
+            pltpu.SemaphoreType.DMA((CHUNKS, 4, 2, 2)),
+            pltpu.SemaphoreType.DMA((CHUNKS, 4, 2, 2)),
+            pltpu.SemaphoreType.DMA((CHUNKS, 4, 2, 2)),
+            pltpu.SemaphoreType.DMA((CHUNKS, 4, 2, 2)),
+            pltpu.SemaphoreType.DMA((CHUNKS, 2)),
+            pltpu.SemaphoreType.DMA((CHUNKS, 2)),
             pltpu.SemaphoreType.DMA((CHUNKS,)),
             pltpu.SemaphoreType.DMA((CHUNKS,)),
             pltpu.SemaphoreType.DMA((CHUNKS,)),
@@ -711,11 +728,11 @@
         expert_ids.T,
         route_weights,
         state,
-        expert_gate,
-        expert_up,
+        jnp.swapaxes(expert_gate, 1, 2),
+        jnp.swapaxes(expert_up, 1, 2),
         expert_down,
-        dense_gate,
-        dense_up,
+        dense_gate.T,
+        dense_up.T,
         dense_down,
     )
 

time: 288 us -> 250 us (0.87)
  local copies, waits for them, and re-layouts: 42.5 us -> 13.9 us
  Pallas kernels: 233 us -> 220 us
  waiting for transfers between devices: 0.01 us -> 3.75 us
    unnamed x24 -> x18, local copies, waits for them, and re-layouts: 36.1 us -> 6.35 us
    pallas_call x1, Pallas kernels: 198 us -> 187 us  [feed(): pl.pallas_call(feed_kernel, out_shape=jax.ShapeDtypeStruct((rows, SLICE),...]
    ppermute x2, waiting for transfers between devices: 0.01 us -> 3.75 us  [from_partner(): lax.ppermute(block, 'tensor', [(i, i ^ 1) for i in range(lax.axis_size('t...]
  transfers between devices with their start and end apart: 2 -> 2, of which waited for: 0 -> 1; matrix products, arithmetic and copies ran while one was open for 12% -> 1% of each run, Pallas kernels for 0% -> 0%
where the time goes in v2:
time: 250 us
  Pallas kernels  220 us (88%)
  local copies, waits for them, and re-layouts  13.9 us (6%)
  matrix products  8.02 us (3%)
  waiting for transfers between devices  3.75 us (2%)
    pallas_call x1, Pallas kernels, feed(): pl.pallas_call(feed_kernel, out_shape=jax.ShapeDtypeStruct((rows, SLICE),...  187 us
    pallas_call x1, Pallas kernels, project(): pl.pallas_call(project_kernel, out_shape=jax.ShapeDtypeStruct((count, SLI...  33.3 us
    unnamed x18, local copies, waits for them, and re-layouts  6.35 us
  transfers between devices with their start and end apart: 2, of which 1 were waited for; matrix products, arithmetic and copies ran while one was open for 1% of the time, Pallas kernels for 0%

profile of v2, /device:TPU:1, one launch (start us, length us, event | category | flops | bytes accessed | tf_op | source)
XLA Modules:
  0.0 249.8 jit_solution(7737750205344680156)
XLA Ops:
  0.0 1.3 fusion.26
  1.3 0.2 dynamic-slice_convert_fusion
  1.6 3.0 %constant_dynamic-slice_fusion.5 = bf16[256,1,896]{2,1,0:T(2,128)(2,1)S(1)} fusion(bf16[256,8,896]{2,1,0:T(8,128)(2,1)} %param.15, s32[]{:T(128)S(6)} %select_n.35), kind=kLoop, calls=%fused_computation.37 | loop fusion | bytes 917508 | tf_op jit(solution)/shard_map/jit(dynamic_index_in_dim)/dynamic_slice | solution.py:750
  4.6 1.3 copy.92
  5.9 0.3 copy.76
  6.2 0.4 fusion.15
  6.8 4.5 %fusion.27 = (f32[256,7]{1,0:T(8,128)S(1)}, f32[256,7,64]{2,1,0:T(8,128)S(1)}) fusion(bf16[256,7,128]{2,1,0:T(8,128)(2,1)S(1)} %copy.76, bf16[2,256,64,128]{3,2,1,0:T(8,128)(2,1)} %param.17, pred[256,64]{1,0:T(8,128)(4,1)S(1)} %broadcast_compare_fusion), kind=kOutput, calls=%fused_computation.41 | convolution fusion | flops 29702400 | bytes 5135360 | tf_op jit(solution)/shard_map/tgd,tpd->tgp/dot_general | solution.py:756
  11.6 0.7 convert_reduce_fusion
  12.6 3.1 %fusion.12 = f32[256,7,128]{2,1,0:T(8,128)S(1)} fusion(bf16[2,256,64,128]{3,2,1,0:T(8,128)(2,1)} %param.17, f32[256,128]{1,0:T(8,128)S(1)} %bitcast.79, f32[256,7]{1,0:T(8,128)S(1)} %copy.80, f32[256,7,64]{2,1,0:T(8,128)S(1)} %get-tuple-element.12, f32[256,7]{1,0:T(8,128)S(1)} %copy.79, pred[256,64]{1,0:T(8,128)(4,1)S(1)} %broadcast_compare_fusion), kind=kOutput, calls=%fused_computation.8 | convolution fusion | flops 30162944 | bytes 5732352 | tf_op jit(solution)/shard_map/tgp,tpd->tgd/dot_general | solution.py:765
  15.7 0.4 copy.81
  16.2 2.1 collective-permute-start.1
  18.4 0.3 collective-permute-start
  18.7 0.2 copy.95
  18.9 0.8 copy.87.ids_ref
  19.7 0.8 copy.88.route_ref
  20.5 3.7 %collective-permute-done = f32[2,256,7]{1,2,0:T(8,128)S(1)} collective-permute-done((f32[2,256,7]{1,2,0:T(8,128)S(1)}, f32[2,256,7]{1,2,0:T(8,128)S(1)}, u32[]{:S(2)}, u32[]{:S(2)}) %collective-permute-start) | collective-permute-done | bytes 14368 | tf_op jit(solution)/shard_map/ppermute | solution.py:741
  24.4 0.2 copy.96
  24.7 0.2 copy.98
  24.9 0.2 add_convert_fusion.att_ref
  25.1 2.0 copy-done
  27.2 33.3 %project.1.state_ref = bf16[2,448,128]{2,1,0:T(8,128)(2,1)S(1)} custom-call(bf16[256,448]{1,0:T(8,128)(2,1)S(1)} %add_convert_fusion.att_ref, bf16[448,7168]{1,0:T(8,128)(2,1)} %weight_ref.1, bf16[256,7168]{1,0:T(8,128)(2,1)S(1)} %copy-done), custom_call_target="tpu_custom_call" | custom-call | tf_op jit(solution)/shard_map/project/pallas_call | solution.py:342
  60.5 0.7 copy-done.1
  61.2 186.9 %feed.1 = bf16[256,448]{1,0:T(8,128)(2,1)} custom-call(s32[256,2]{1,0:T(8,128)} %copy.87.ids_ref, s32[2,256]{1,0:T(2,128)} %bitcast.83, f32[256,2]{1,0:T(8,128)} %copy.88.route_ref, bf16[2,448,128]{2,1,0:T(8,128)(2,1)} %copy-done.1, bf16[1,304,7168]{2,1,0:T(8,128)(2,1)} %bitcast.70, bf16[1,304,7168]{2,1,0:T(8,128)(2,1)} %bitcast.71, ...), custom_call_target="tpu_custom_call" | custom-call | tf_op jit(solution)/shard_map/feed/pallas_call | solution.py:689
  248.0 1.8 copy.89
  (28 shorter events, 1.1 us)
Async XLA Ops:
  0.0 6.7 %copy-start.4 = (s32[256]{0:T(256)S(1)}, s32[256]{0:T(256)}, u32[]{:S(2)}) copy-start(s32[256]{0:T(256)} %param.18) | copy-start | bytes 3076
  12.6 6.3 %copy-start.2 = (s32[256,2]{0,1:T(2,128)S(1)}, s32[256,2]{0,1:T(2,128)}, u32[]{:S(2)}) copy-start(s32[256,2]{0,1:T(2,128)} %param.23) | copy-start | bytes 6148
  12.6 7.1 %copy-start.3 = (f32[256,2]{0,1:T(2,128)S(1)}, f32[256,2]{0,1:T(2,128)}, u32[]{:S(2)}) copy-start(f32[256,2]{0,1:T(2,128)} %param.24) | copy-start | bytes 6148
  16.2 8.7 %collective-permute-start.1 = (bf16[256,448]{1,0:T(8,128)(2,1)S(1)}, bf16[256,448]{1,0:T(8,128)(2,1)S(1)}, u32[]{:S(2)}, u32[]{:S(2)}) collective-permute-start(bf16[256,448]{1,0:T(8,128)(2,1)S(1)} %copy.97), channel_id=1, source_target_pairs={{0,1},{1,0},{2,3},{3,2},{4,5},{5,4},{6,7},{7,6},{8,9},{9,8},{10,11... | collective-permute-start | bytes 688136 | tf_op jit(solution)/shard_map/ppermute | solution.py:741
  18.4 5.9 %collective-permute-start = (f32[2,256,7]{1,2,0:T(8,128)S(1)}, f32[2,256,7]{1,2,0:T(8,128)S(1)}, u32[]{:S(2)}, u32[]{:S(2)}) collective-permute-start(f32[2,256,7]{1,2,0:T(8,128)S(1)} %pad_maximum_fusion), channel_id=1, source_target_pairs={{0,1},{1,0},{2,3},{3,2},{4,5},{5,4},{6,7},{7,6},{8,9},{9,8},{10,11... | collective-permute-start | bytes 43016 | tf_op jit(solution)/shard_map/ppermute | solution.py:741
  25.1 2.0 copy-start
  60.5 0.7 copy-start.1

commit v3 on v2

--- a/solution.py
+++ b/solution.py
@@ -177,6 +177,10 @@
     def __init__(self, place, part, landing, send, recv):
         self.place, self.part, self.landing = place, part, landing
         self.send, self.recv = send, recv
+
+    def landed(self, step, c):
+        landing = self.landing[step]
+        return landing.at[lax.rem(c, landing.shape[0])]
 
     def copies(self, step, c):
         place = self.place
@@ -199,7 +203,7 @@
             result.append(
                 copy_to(
                     src,
-                    self.landing[step].at[c, h, way],
+                    self.landed(step, c).at[h, way],
                     self.send.at[c, step, h, way],
                     self.recv.at[c, step, h, way],
                     to,
@@ -211,7 +215,7 @@
         for h in range(2):
             part = self.part.at[c, h]
             p, q = self.place.axes(h)
-            landed = self.landing[step].at[c, h]
+            landed = self.landed(step, c).at[h]
             if step == 0:
                 for way, hop in ((0, 1), (1, -1)):
                     for k in range(2):
@@ -233,7 +237,7 @@
         halves = []
         for h in range(2):
             p, q = self.place.axes(h)
-            landed = self.landing[3].at[c, h]
+            landed = self.landed(3, c).at[h]
             halves.append(
                 self.part[c, h, q * SIDE + p].astype(F32)
                 + landed[0].astype(F32)
@@ -371,12 +375,20 @@
     return sum((b[k] + bits[k] - 2 * b[k] * bits[k]) * (1 << k) for k in range(3))
 
 
+PARTNERS = (0, 1, 3, 7, 2, 6, 4, 5)
+WHOLE = (1, 4, 5)
+SPREAD = (2, 3, 6, 7)
+TURNS = CHUNKS // 2
+SLOTS = 6
+
+
 def chunk_bits(c):
     if isinstance(c, int):
-        a, b, d = c % 2, (c // 2) % 2, c // 4
-    else:
-        a, b, d = lax.rem(c, 2), lax.rem(c // 2, 2), c // 4
-    return a, b + d - 2 * b * d, d
+        return tuple((PARTNERS[c] >> k) & 1 for k in range(3))
+    return tuple(
+        sum(jnp.where(c == i, 1, 0) for i in range(CHUNKS) if (PARTNERS[i] >> k) & 1)
+        for k in range(3)
+    )
 
 
 def to_group(src, dst, send, recv, group):
@@ -392,7 +404,6 @@
 
 def feed_kernel(
     ids_ref,
-    flat_ids_ref,
     route_ref,
     state_ref,
     expert_gate,
@@ -403,6 +414,8 @@
     dense_down,
     mixed_ref,
     part,
+    full,
+    ready,
     r1,
     r2,
     r3,
@@ -413,11 +426,14 @@
     side_out,
     side_in,
     returned,
+    summed,
     own_pos,
     acc,
     hidden,
-    summed,
+    mixing,
     load_sem,
+    full_send,
+    full_recv,
     spread_send,
     spread_recv,
     sum_send,
@@ -431,10 +447,9 @@
 ):
     place = Place()
     group = lax.axis_index("group")
-    rank = place.rank
-    is_odd = lax.rem(rank, 2)
+    is_odd = lax.rem(place.rank, 2)
     hidden_size = w_in.shape[0] // 4
-    rows = ids_ref.shape[0]
+    rows = ids_ref.shape[1]
     row_blocks = rows // CHUNK
     width = 16 * SLICE
 
@@ -444,10 +459,10 @@
         )
         for k, ref in enumerate((expert_gate.at[0], expert_up.at[0], dense_gate, dense_up))
     ] + [
-        pltpu.make_async_copy(expert_down.at[0], w_down.at[pl.ds(0, hidden_size)], load_sem.at[4]),
         pltpu.make_async_copy(
-            dense_down, w_down.at[pl.ds(DENSE_AT, hidden_size)], load_sem.at[5]
-        ),
+            ref, w_down.at[pl.ds(k * hidden_size, hidden_size)], load_sem.at[4 + k]
+        )
+        for k, ref in enumerate((expert_down.at[0], dense_down))
     ]
     for load in loads:
         load.start()
@@ -461,85 +476,141 @@
             device_id={"group": flipped(group, chunk_bits(c))},
             device_id_type=pl.DeviceIdType.MESH,
         )
-
-    ids = ids_ref[...]
-    flat_ids = flat_ids_ref[...]
-    lane = lax.broadcasted_iota(jnp.int32, (rows, LANES), 1)
-    partner_of_lane = sum(
-        jnp.where(lane == c, flipped(group, chunk_bits(c)) + 1, 0) for c in range(CHUNKS)
-    ) - 1
-    first_choice = ids[:, 0:1] == partner_of_lane
-    second_choice = ids[:, 1:2] == partner_of_lane
-    named = jnp.where(first_choice | second_choice, 1.0, 0.0)
+    for b in range(row_blocks):
+        for h in range(2):
+            full[b, h, spot(h, place.z, place.x)] = state_ref[b, h * HALF : (h + 1) * HALF, :]
+    pl.semaphore_wait(barrier, 4 + CHUNKS - 1)
+
+    gatherer = Spreader(place, full, full_send, full_recv)
+    spreader = Spreader(place, part, spread_send, spread_recv)
+    summer = Summer(place, part, (r1, r2, r3, r4), sum_send, sum_recv)
+    for b in range(row_blocks):
+        gatherer.start(0, b)
+
     line = lax.broadcasted_iota(jnp.int32, (rows, rows), 0)
     column = lax.broadcasted_iota(jnp.int32, (rows, rows), 1)
+
+    def upright(row):
+        return jnp.sum(jnp.where(line == column, row, 0.0), axis=1, keepdims=True)
+
+    flat_ids = [ids_ref[k : k + 1, :].astype(F32) for k in range(2)]
+    ids = [upright(row) for row in flat_ids]
+    route = [upright(route_ref[k : k + 1, :]) for k in range(2)]
+    partners = [flipped(group, chunk_bits(c)).astype(F32) for c in range(CHUNKS)]
+    lane = lax.broadcasted_iota(jnp.int32, (rows, LANES), 1)
+    partner_of_lane = jnp.full((rows, LANES), -1.0, F32)
+    sub = lax.broadcasted_iota(jnp.int32, (CHUNKS, rows), 0)
+    partner_of_sub = jnp.zeros((CHUNKS, rows), F32)
+    for c in range(CHUNKS):
+        partner_of_lane = jnp.where(lane == c, partners[c], partner_of_lane)
+        partner_of_sub = jnp.where(sub == c, partners[c], partner_of_sub)
+    first_choice, second_choice = [choice == partner_of_lane for choice in ids]
+    named = jnp.where(first_choice | second_choice, 1.0, 0.0)
     before = jnp.where(column < line, 1.0, 0.0).astype(BF)
     place_in = jnp.dot(before, named.astype(BF), preferred_element_type=F32)
-    own_pos[...] = jnp.where(named > 0.5, place_in, -1.0)
-
-    sub = lax.broadcasted_iota(jnp.int32, (8, rows), 0)
-    partner_of_sub = sum(
-        jnp.where(sub == c, flipped(group, chunk_bits(c)) + 1, 0) for c in range(CHUNKS)
-    ) - 1
+    positions = jnp.where(named > 0.5, place_in, -1.0)
+    own_pos[...] = positions
     flat_named = jnp.where(
-        (flat_ids[0:1, :] == partner_of_sub) | (flat_ids[1:2, :] == partner_of_sub), 1.0, 0.0
+        (flat_ids[0] == partner_of_sub) | (flat_ids[1] == partner_of_sub), 1.0, 0.0
     )
     after = jnp.where(line < column, 1.0, 0.0).astype(BF)
     flat_place = jnp.dot(flat_named.astype(BF), after, preferred_element_type=F32)
     flat_pos = jnp.where(flat_named > 0.5, flat_place, -1.0)
-
-    weight = jnp.where(first_choice, route_ref[:, 0:1], 0.0) + jnp.where(
-        second_choice, route_ref[:, 1:2], 0.0
-    )
+    weight = jnp.where(first_choice, route[0], 0.0) + jnp.where(second_choice, route[1], 0.0)
     dense_here = jnp.where(first_choice, 1.0, 0.0)
-    source = jnp.concatenate(
-        [natural_own(state_ref.at[b], is_odd) for b in range(row_blocks)], axis=0
-    ).astype(BF)
     slot_line = lax.broadcasted_iota(jnp.int32, (CHUNK, rows), 0).astype(F32)
     slot_lane = lax.broadcasted_iota(jnp.int32, (rows, CHUNK), 1).astype(F32)
     sides = lax.broadcasted_iota(jnp.int32, (8, LANES), 0)
-
-    def go(c):
-        to = flipped(group, chunk_bits(c))
+    for b in range(row_blocks):
+        mixing[b * CHUNK : (b + 1) * CHUNK, :] = natural_own(state_ref.at[b], is_odd)
+
+    def pick(c):
+        return jnp.where(flat_pos[c : c + 1, :] == slot_line, 1.0, 0.0).astype(BF)
+
+    def partner(c):
+        return flipped(group, chunk_bits(c))
+
+    def side(c):
+        return to_group(
+            side_out.at[c], side_in.at[c], side_send.at[c], side_recv.at[c], partner(c)
+        )
+
+    def slices(c):
         return [
             to_group(
-                outgoing.at[c, pl.ds(h * HALF, HALF)],
+                outgoing.at[SPREAD.index(c), pl.ds(h * HALF, HALF)],
                 part.at[c, h, spot(h, place.z, place.x)],
                 go_send.at[c, h],
                 go_recv.at[c, h],
-                to,
+                partner(c),
             )
             for h in range(2)
-        ] + [to_group(side_out.at[c], side_in.at[c], side_send.at[c], side_recv.at[c], to)]
-
+        ]
+
+    def whole(c):
+        slot = 1 if c == 5 else 0
+        return to_group(
+            ready.at[slot], part.at[c], go_send.at[c, 0], go_recv.at[c, 0], partner(c)
+        )
+
+    for c in SPREAD:
+        chosen = jnp.dot(pick(c), mixing[...].astype(BF), preferred_element_type=F32)
+        store_own(outgoing.at[SPREAD.index(c)], chosen, is_odd)
+        for copy in slices(c):
+            copy.start()
+    for b in range(row_blocks):
+        gatherer.arrive(0, b)
+        gatherer.start(1, b)
     for c in range(CHUNKS):
-        pick = jnp.where(flat_pos[c : c + 1, :] == slot_line, 1.0, 0.0).astype(BF)
-        chosen = jnp.dot(pick, source, preferred_element_type=F32)
-        at_slot = own_pos[:, c : c + 1] == slot_lane
+        at_slot = positions[:, c : c + 1] == slot_lane
         w_row = jnp.sum(jnp.where(at_slot, weight[:, c : c + 1], 0.0), axis=0, keepdims=True)
         d_row = jnp.sum(jnp.where(at_slot, dense_here[:, c : c + 1], 0.0), axis=0, keepdims=True)
-        side = jnp.where(sides == 0, w_row, jnp.where(sides == 1, d_row, 0.0))
-        store_own(outgoing.at[c], chosen, is_odd)
+        both = jnp.where(sides == 0, w_row, jnp.where(sides == 1, d_row, 0.0))
         if c == 0:
-            for h in range(2):
-                part[0, h, spot(h, place.z, place.x)] = outgoing[0, h * HALF : (h + 1) * HALF, :]
-            side_in[0] = side
-            pl.semaphore_wait(barrier, 4 + CHUNKS - 1)
+            side_in[0] = both
         else:
-            side_out[c] = side
-            for copy in go(c):
-                copy.start()
-
-    spreader = Spreader(place, part, spread_send, spread_recv)
-    summer = Summer(place, part, (r1, r2, r3, r4), sum_send, sum_recv)
+            side_out[c] = both
+            side(c).start()
+    for b in range(row_blocks):
+        gatherer.arrive(1, b)
+        gatherer.start(2, b)
+    for c in SPREAD[:2]:
+        for copy in slices(c):
+            copy.wait_recv()
+        spreader.start(0, c)
+    for b in range(row_blocks):
+        gatherer.arrive(2, b)
+        gatherer.start(3, b)
+    for c in SPREAD[:2]:
+        spreader.arrive(0, c)
+        spreader.start(1, c)
+    for b in range(row_blocks):
+        gatherer.arrive(3, b)
+
+    def choose_whole(c, target):
+        chosen_rows = pick(c)
+
+        @pl.loop(0, SIDE)
+        def _(z):
+            source = jnp.concatenate(
+                [load_quarter(full.at[b], z) for b in range(row_blocks)], axis=0
+            )
+            store_quarter(
+                target, z, jnp.dot(chosen_rows, source, preferred_element_type=F32)
+            )
+
+    choose_whole(1, ready.at[0])
+    whole(1).start()
+    choose_whole(5, ready.at[1])
+    whole(5).start()
+    whole(1).wait_send()
+    choose_whole(4, ready.at[0])
+    whole(4).start()
+    choose_whole(0, part.at[0])
 
     def back(c):
         return to_group(
-            summed.at[c],
-            returned.at[c],
-            back_send.at[c],
-            back_recv.at[c],
-            flipped(group, chunk_bits(c)),
+            summed.at[c], returned.at[c], back_send.at[c], back_recv.at[c], partner(c)
         )
 
     def finish_sum(c):
@@ -555,12 +626,22 @@
             summed[c] = total
             back(c).start()
 
-    def compute(c):
-        chunk = part.at[c]
+    def mix(c):
+        @pl.when(c > 0)
+        def _():
+            back(c).wait_recv()
+
+        position = jnp.sum(jnp.where(lane == c, own_pos[...], 0.0), axis=1, keepdims=True)
+        at_slot = jnp.where(position == slot_lane, 1.0, 0.0).astype(BF)
+        block = natural_own(returned.at[c], is_odd).astype(BF)
+        mixing[...] += jnp.dot(at_slot, block, preferred_element_type=F32)
+
+    def compute(j):
+        chunks = [part.at[2 * j + i] for i in range(2)]
         acc[...] = jnp.zeros_like(acc)
 
         def gather_products(z, squares):
-            block = load_quarter(chunk, z)
+            block = jnp.concatenate([load_quarter(chunk, z) for chunk in chunks], axis=0)
             deep = pl.ds(pl.multiple_of(z * 4 * SLICE, 4 * SLICE), 4 * SLICE)
             acc[...] += lax.dot_general(
                 block, w_in[:, deep], (((1,), (1,)), ((), ())), preferred_element_type=F32
@@ -570,55 +651,50 @@
                 squares = squares + wide * wide
             return squares
 
-        squares = lax.fori_loop(0, SIDE, gather_products, jnp.zeros((CHUNK, LANES), F32))
+        squares = lax.fori_loop(0, SIDE, gather_products, jnp.zeros((2 * CHUNK, LANES), F32))
         scale = lax.rsqrt(jnp.sum(squares, axis=1, keepdims=True) / width + 1e-05)
-        line = lax.broadcasted_iota(jnp.int32, (CHUNK, CHUNK), 0)
-        column = lax.broadcasted_iota(jnp.int32, (CHUNK, CHUNK), 1)
-        factors = [
-            jnp.sum(jnp.where(line == column, side_in[c, k : k + 1, :], 0.0), axis=1, keepdims=True)
-            for k in range(2)
-        ]
+        diagonal = lax.broadcasted_iota(jnp.int32, (CHUNK, CHUNK), 0) == lax.broadcasted_iota(
+            jnp.int32, (CHUNK, CHUNK), 1
+        )
         for k in range(2):
+            factor = jnp.concatenate(
+                [
+                    jnp.sum(
+                        jnp.where(diagonal, side_in[2 * j + i, k : k + 1, :], 0.0),
+                        axis=1,
+                        keepdims=True,
+                    )
+                    for i in range(2)
+                ],
+                axis=0,
+            )
             gate, up = [
-                acc[:, (2 * k + j) * hidden_size : (2 * k + j + 1) * hidden_size] * scale
-                for j in range(2)
+                acc[:, (2 * k + i) * hidden_size : (2 * k + i + 1) * hidden_size] * scale
+                for i in range(2)
             ]
-            inner = gate / (1.0 + jnp.exp(-gate)) * up * factors[k]
-            hidden[:, k * DENSE_AT : k * DENSE_AT + hidden_size] = inner.astype(BF)
-
-        spreader.sent(c)
+            inner = gate / (1.0 + jnp.exp(-gate)) * up * factor
+            hidden[:, k * hidden_size : (k + 1) * hidden_size] = inner.astype(BF)
+
+        @pl.when(lax.rem(j, 2) == 1)
+        def _():
+            for i in range(2):
+                spreader.sent(2 * j + i)
 
         @pl.loop(0, SIDE)
         def _(z):
             columns = pl.ds(pl.multiple_of(z * 4 * SLICE, 4 * SLICE), 4 * SLICE)
             block = jnp.dot(hidden[...], w_down[:, columns], preferred_element_type=F32)
-            store_quarter(chunk, z, block)
-
-    hidden[...] = jnp.zeros_like(hidden)
-    w_down[hidden_size:DENSE_AT, :] = jnp.zeros((DENSE_AT - hidden_size, width), BF)
+            for i in range(2):
+                store_quarter(chunks[i], z, block[i * CHUNK : (i + 1) * CHUNK])
 
     def turn(it, carry):
         def stage(lag, body):
-            c = it - lag
-
-            @pl.when((c >= 0) & (c < CHUNKS))
+            j = it - lag
+
+            @pl.when((j >= 0) & (j < TURNS))
             def _():
-                body(c)
-
-        def begin(c):
-            @pl.when(c > 0)
-            def _():
-                for copy in go(c):
-                    copy.wait_recv()
-
-            spreader.start(0, c)
-
-        def spread(step):
-            def body(c):
-                spreader.arrive(step - 1, c)
-                spreader.start(step, c)
-
-            return body
+                for i in range(2):
+                    body(2 * j + i)
 
         def add(step):
             def body(c):
@@ -628,39 +704,67 @@
 
             return body
 
-        def work(c):
-            spreader.arrive(3, c)
-
-            @pl.when(c == 0)
-            def _():
-                for load in loads:
-                    load.wait()
-
-            compute(c)
-            summer.start(0, c)
-
-        stage(0, begin)
-        stage(1, spread(1))
-        stage(2, spread(2))
-        stage(3, spread(3))
-        stage(5, add(1))
-        stage(6, add(2))
-        stage(7, add(3))
-        stage(8, finish_sum)
-        stage(4, work)
+        def spread(step, chunks):
+            for c in chunks:
+                if step == 0:
+                    for copy in slices(c):
+                        copy.wait_recv()
+                else:
+                    spreader.arrive(step - 1, c)
+                if step < 4:
+                    spreader.start(step, c)
+
+        stage(5, mix)
+        stage(4, finish_sum)
+        stage(3, add(3))
+        stage(2, add(2))
+        stage(1, add(1))
+
+        @pl.when(it == 0)
+        def _():
+            spread(2, SPREAD[:2])
+            spread(0, SPREAD[2:])
+            whole(1).wait_recv()
+            side(1).wait_recv()
+            for load in loads:
+                load.wait()
+
+        @pl.when(it == 1)
+        def _():
+            spread(2, SPREAD[2:])
+            spread(4, SPREAD[:2])
+            for c in SPREAD[:2]:
+                side(c).wait_recv()
+
+        @pl.when(it == 2)
+        def _():
+            spread(3, SPREAD[2:])
+            for c in WHOLE[1:]:
+                whole(c).wait_recv()
+                side(c).wait_recv()
+
+        @pl.when(it == 3)
+        def _():
+            spread(4, SPREAD[2:])
+            for c in SPREAD[2:]:
+                side(c).wait_recv()
+
+        @pl.when(it < TURNS)
+        def _():
+            compute(it)
+            for i in range(2):
+                summer.start(0, 2 * it + i)
+
+        @pl.when(it == 0)
+        def _():
+            spread(3, SPREAD[:2])
+            spread(1, SPREAD[2:])
+
         return carry
 
-    lax.fori_loop(0, CHUNKS + 8, turn, 0)
-
-    total = jnp.concatenate(
-        [natural_own(state_ref.at[b], is_odd) for b in range(row_blocks)], axis=0
-    )
-    for c in range(CHUNKS):
-        if c > 0:
-            back(c).wait_recv()
-        at_slot = jnp.where(own_pos[:, c : c + 1] == slot_lane, 1.0, 0.0).astype(BF)
-        block = natural_own(returned.at[c], is_odd).astype(BF)
-        total = total + jnp.dot(at_slot, block, preferred_element_type=F32)
+    lax.fori_loop(0, TURNS + 5, turn, 0)
+
+    total = mixing[...]
     for_odd = pltpu.roll(
         jnp.concatenate([total[:, 3 * LANES :], total[:, : 3 * LANES]], axis=1),
         4 * LANES - SHARED,
@@ -672,61 +776,71 @@
     def _(c):
         summer.sent(c)
 
+    for b in range(row_blocks):
+        gatherer.sent(b)
     for c in range(1, CHUNKS):
-        for copy in go(c):
+        side(c).wait_send()
+        back(c).wait_send()
+    for c in SPREAD:
+        for copy in slices(c):
             copy.wait_send()
-        back(c).wait_send()
-
-
-DENSE_AT = 384
-
-
-def feed(expert_ids, route_weights, state, expert_gate, expert_up, expert_down, dense_gate, dense_up, dense_down):
+    for c in WHOLE[1:]:
+        whole(c).wait_send()
+
+
+def feed(
+    expert_ids,
+    route_weights,
+    state,
+    expert_gate,
+    expert_up,
+    expert_down,
+    dense_gate,
+    dense_up,
+    dense_down,
+):
     rows = expert_ids.shape[0]
     width, hidden_size = dense_gate.shape
     vmem = pl.BlockSpec(memory_space=pltpu.VMEM)
     hbm = pl.BlockSpec(memory_space=pl.ANY)
+    row_blocks = rows // CHUNK
     return pl.pallas_call(
         feed_kernel,
         out_shape=jax.ShapeDtypeStruct((rows, SLICE), BF),
-        in_specs=[vmem] * 4 + [hbm] * 6,
+        in_specs=[vmem] * 3 + [hbm] * 6,
         out_specs=vmem,
         scratch_shapes=[
             pltpu.VMEM((CHUNKS, 2, 16, HALF, LANES), BF),
-            pltpu.VMEM((CHUNKS, 2, 2, 2, HALF, LANES), BF),
-            pltpu.VMEM((CHUNKS, 2, 2, SIDE, HALF, LANES), BF),
-            pltpu.VMEM((CHUNKS, 2, 2, QUARTER, LANES), BF),
-            pltpu.VMEM((CHUNKS, 2, 2, HALF, LANES), BF),
+            pltpu.VMEM((row_blocks, 2, 16, HALF, LANES), BF),
+            pltpu.VMEM((2, 2, 16, HALF, LANES), BF),
+            pltpu.VMEM((SLOTS, 2, 2, 2, HALF, LANES), BF),
+            pltpu.VMEM((SLOTS, 2, 2, SIDE, HALF, LANES), BF),
+            pltpu.VMEM((SLOTS, 2, 2, QUARTER, LANES), BF),
+            pltpu.VMEM((SLOTS, 2, 2, HALF, LANES), BF),
             pltpu.VMEM((4 * hidden_size, width), BF),
-            pltpu.VMEM((DENSE_AT + hidden_size, width), BF),
-            pltpu.VMEM((CHUNKS, SLICE, LANES), BF),
+            pltpu.VMEM((2 * hidden_size, width), BF),
+            pltpu.VMEM((len(SPREAD), SLICE, LANES), BF),
             pltpu.VMEM((CHUNKS, 8, LANES), F32),
             pltpu.VMEM((CHUNKS, 8, LANES), F32),
             pltpu.VMEM((CHUNKS, SLICE, LANES), BF),
+            pltpu.VMEM((CHUNKS, SLICE, LANES), BF),
             pltpu.VMEM((rows, LANES), F32),
-            pltpu.VMEM((CHUNK, 4 * hidden_size), F32),
-            pltpu.VMEM((CHUNK, DENSE_AT + hidden_size), BF),
-            pltpu.VMEM((CHUNKS, SLICE, LANES), BF),
+            pltpu.VMEM((2 * CHUNK, 4 * hidden_size), F32),
+            pltpu.VMEM((2 * CHUNK, 2 * hidden_size), BF),
+            pltpu.VMEM((rows, 4 * LANES), F32),
             pltpu.SemaphoreType.DMA((6,)),
-            pltpu.SemaphoreType.DMA((CHUNKS, 4, 2, 2)),
-            pltpu.SemaphoreType.DMA((CHUNKS, 4, 2, 2)),
-            pltpu.SemaphoreType.DMA((CHUNKS, 4, 2, 2)),
-            pltpu.SemaphoreType.DMA((CHUNKS, 4, 2, 2)),
-            pltpu.SemaphoreType.DMA((CHUNKS, 2)),
-            pltpu.SemaphoreType.DMA((CHUNKS, 2)),
-            pltpu.SemaphoreType.DMA((CHUNKS,)),
-            pltpu.SemaphoreType.DMA((CHUNKS,)),
-            pltpu.SemaphoreType.DMA((CHUNKS,)),
-            pltpu.SemaphoreType.DMA((CHUNKS,)),
-        ],
+        ]
+        + [pltpu.SemaphoreType.DMA((row_blocks, 4, 2, 2))] * 2
+        + [pltpu.SemaphoreType.DMA((CHUNKS, 4, 2, 2))] * 4
+        + [pltpu.SemaphoreType.DMA((CHUNKS, 2))] * 2
+        + [pltpu.SemaphoreType.DMA((CHUNKS,))] * 4,
         compiler_params=pltpu.CompilerParams(
             collective_id=2, has_side_effects=True, vmem_limit_bytes=64 * 1024 * 1024 - 65536
         ),
         name="feed",
     )(
-        expert_ids,
         expert_ids.T,
-        route_weights,
+        route_weights.T,
         state,
         jnp.swapaxes(expert_gate, 1, 2),
         jnp.swapaxes(expert_up, 1, 2),

time: 250 us -> 227 us (0.908)
  Pallas kernels: 220 us -> 196 us
  local copies, waits for them, and re-layouts: 13.9 us -> 11.1 us
    pallas_call x1, Pallas kernels: 187 us -> 163 us  [feed(): pl.pallas_call(feed_kernel, out_shape=jax.ShapeDtypeStruct((rows, SLICE),...]
    unnamed x18 -> x14, local copies, waits for them, and re-layouts: 6.35 us -> 4.75 us
  transfers between devices with their start and end apart: 2 -> 2, of which waited for: 1 -> 1; matrix products, arithmetic and copies ran while one was open for 1% -> 2% of each run, Pallas kernels for 0% -> 0%
where the time goes in v3:
time: 227 us; the launch traced here: 225 us
  Pallas kernels  196 us (86%)
  local copies, waits for them, and re-layouts  11.1 us (5%)
  matrix products  8.02 us (4%)
  waiting for transfers between devices  5.9 us (3%)
    pallas_call x1, Pallas kernels, feed(): pl.pallas_call(feed_kernel, out_shape=jax.ShapeDtypeStruct((rows, SLICE),...  163 us
    pallas_call x1, Pallas kernels, project(): pl.pallas_call(project_kernel, out_shape=jax.ShapeDtypeStruct((count, SLI...  32.5 us
    ppermute x2, waiting for transfers between devices, from_partner(): lax.ppermute(block, 'tensor', [(i, i ^ 1) for i in range(lax.axis_size('t...  5.9 us
    unnamed x14, local copies, waits for them, and re-layouts  4.75 us
    dot_general x1, matrix products, attend(): jnp.einsum('tgd,tpd->tgp', rows, kv_cache[0], preferred_element_type=F32)  4.55 us
  transfers between devices with their start and end apart: 2, of which 1 were waited for; matrix products, arithmetic and copies ran while one was open for 2% of the time, Pallas kernels for 0%

profile of v3, /device:TPU:1, one launch (start us, length us, event | category | flops | bytes accessed | tf_op | source)
XLA Modules:
  0.0 224.8 jit_solution(16826522826910618916)
XLA Ops:
  0.0 3.1 %constant_dynamic-slice_fusion.5 = bf16[256,1,896]{2,1,0:T(2,128)(2,1)S(1)} fusion(bf16[256,8,896]{2,1,0:T(8,128)(2,1)} %param.15, s32[]{:T(128)S(6)} %select_n.35), kind=kLoop, calls=%fused_computation.37 | loop fusion | bytes 917508 | tf_op jit(solution)/shard_map/jit(dynamic_index_in_dim)/dynamic_slice | solution.py:864
  3.1 1.3 copy.80
  4.4 0.3 copy.66
  4.8 0.2 dynamic-slice_convert_fusion
  5.1 0.4 fusion.15
  5.6 0.1 broadcast_compare_fusion
  5.7 4.5 %fusion.27 = (f32[256,7]{1,0:T(8,128)S(1)}, f32[256,7,64]{2,1,0:T(8,128)S(1)}) fusion(bf16[256,7,128]{2,1,0:T(8,128)(2,1)S(1)} %copy.66, bf16[2,256,64,128]{3,2,1,0:T(8,128)(2,1)} %param.17, pred[256,64]{1,0:T(8,128)(4,1)S(1)} %broadcast_compare_fusion), kind=kOutput, calls=%fused_computation.41 | convolution fusion | flops 29702400 | bytes 5135360 | tf_op jit(solution)/shard_map/tgd,tpd->tgp/dot_general | solution.py:870
  10.3 0.1 copy.69
  10.5 0.7 convert_reduce_fusion
  11.3 2.1 collective-permute-start
  13.5 0.1 copy.70
  13.6 3.1 %fusion.12 = f32[256,7,128]{2,1,0:T(8,128)S(1)} fusion(bf16[2,256,64,128]{3,2,1,0:T(8,128)(2,1)} %param.17, f32[256,128]{1,0:T(8,128)S(1)} %bitcast.80, f32[256,7]{1,0:T(8,128)S(1)} %copy.70, f32[256,7,64]{2,1,0:T(8,128)S(1)} %get-tuple-element.12, f32[256,7]{1,0:T(8,128)S(1)} %copy.69, pred[256,64]{1,0:T(8,128)(4,1)S(1)} %broadcast_compare_fusion), kind=kOutput, calls=%fused_computation.8 | convolution fusion | flops 30162944 | bytes 5732352 | tf_op jit(solution)/shard_map/tgp,tpd->tgd/dot_general | solution.py:879
  16.7 0.4 copy.71
  17.1 0.1 copy.85
  17.4 0.2 copy.83
  17.7 0.2 copy.84
  18.1 0.2 copy.86
  18.3 5.9 %collective-permute-done.1 = bf16[256,448]{1,0:T(8,128)(2,1)S(1)} collective-permute-done((bf16[256,448]{1,0:T(8,128)(2,1)S(1)}, bf16[256,448]{1,0:T(8,128)(2,1)S(1)}, u32[]{:S(2)}, u32[]{:S(2)}) %collective-permute-start.1) | collective-permute-done | bytes 229408 | tf_op jit(solution)/shard_map/ppermute | solution.py:855
  24.2 0.2 add_convert_fusion.att_ref
  24.4 2.0 copy-done
  26.4 32.5 %project.1.state_ref = bf16[2,448,128]{2,1,0:T(8,128)(2,1)S(1)} custom-call(bf16[256,448]{1,0:T(8,128)(2,1)S(1)} %add_convert_fusion.att_ref, bf16[448,7168]{1,0:T(8,128)(2,1)} %weight_ref.1, bf16[256,7168]{1,0:T(8,128)(2,1)S(1)} %copy-done), custom_call_target="tpu_custom_call" | custom-call | tf_op jit(solution)/shard_map/project/pallas_call | solution.py:346
  58.9 0.7 copy-done.1
  59.6 163.4 %feed.1 = bf16[256,448]{1,0:T(8,128)(2,1)} custom-call(s32[2,256]{1,0:T(2,128)} %bitcast.84, f32[2,256]{1,0:T(2,128)} %bitcast.85, bf16[2,448,128]{2,1,0:T(8,128)(2,1)} %copy-done.1, bf16[1,304,7168]{2,1,0:T(8,128)(2,1)} %bitcast.71, bf16[1,304,7168]{2,1,0:T(8,128)(2,1)} %bitcast.72, bf16[1,304,7168]{2,1,0:T(8,128)(2,1)} %expert_down.1, ...), custom_call_target="tpu_custom_call" | custom-call | tf_op jit(solution)/shard_map/feed/pallas_call | solution.py:807
  223.0 1.8 copy.77
  (24 shorter events, 0.8 us)
Async XLA Ops:
  0.0 4.7 %copy-start.2 = (bf16[2,256,8,128]{3,2,1,0:T(8,128)(2,1)S(1)}, bf16[2,256,8,128]{3,2,1,0:T(8,128)(2,1)}, u32[]{:S(2)}) copy-start(bf16[2,256,8,128]{3,2,1,0:T(8,128)(2,1)} %param.16) | copy-start | bytes 3145732
  0.0 5.6 %copy-start.3 = (s32[256]{0:T(256)S(1)}, s32[256]{0:T(256)}, u32[]{:S(2)}) copy-start(s32[256]{0:T(256)} %param.18) | copy-start | bytes 3076
  11.3 6.2 %collective-permute-start = (f32[2,256,7]{1,2,0:T(8,128)S(1)}, f32[2,256,7]{1,2,0:T(8,128)S(1)}, u32[]{:S(2)}, u32[]{:S(2)}) collective-permute-start(f32[2,256,7]{1,2,0:T(8,128)S(1)} %pad_maximum_fusion), channel_id=1, source_target_pairs={{0,1},{1,0},{2,3},{3,2},{4,5},{5,4},{6,7},{7,6},{8,9},{9,8},{10,11... | collective-permute-start | bytes 43016 | tf_op jit(solution)/shard_map/ppermute | solution.py:855
  17.2 6.9 %collective-permute-start.1 = (bf16[256,448]{1,0:T(8,128)(2,1)S(1)}, bf16[256,448]{1,0:T(8,128)(2,1)S(1)}, u32[]{:S(2)}, u32[]{:S(2)}) collective-permute-start(bf16[256,448]{1,0:T(8,128)(2,1)S(1)} %copy.85), channel_id=1, source_target_pairs={{0,1},{1,0},{2,3},{3,2},{4,5},{5,4},{6,7},{7,6},{8,9},{9,8},{10,11... | collective-permute-start | bytes 688136 | tf_op jit(solution)/shard_map/ppermute | solution.py:855
  24.4 2.0 copy-start
  58.9 0.7 copy-start.1

commit v4 on v3

--- a/solution.py
+++ b/solution.py
@@ -56,9 +56,10 @@
     return pieces[0] if len(pieces) == 1 else jnp.concatenate(pieces, axis=0)
 
 
-def write_rows(part, z, x, low, value):
+def write_rows(part, z, x, low, value, halves=(0, 1)):
     for h, a, b, offset in split_rows(low, low + value.shape[0]):
-        part[h, spot(h, z, x), a:b, :] = value[offset : offset + b - a]
+        if h in halves:
+            part[h, spot(h, z, x), a:b, :] = value[offset : offset + b - a]
 
 
 def copy_to(src, dst, send, recv, rank):
@@ -120,7 +121,7 @@
     ref[pl.ds(half, SHARED), :] = fold_own(block[:, 3 * LANES :], is_odd).astype(BF)
 
 
-def store_quarter(part, z, block):
+def store_quarter(part, z, block, halves=(0, 1)):
     for pair in range(2):
         e, o = 2 * pair, 2 * pair + 1
         tiles = [
@@ -128,10 +129,10 @@
         ]
         even_half, odd_half = fold_pair(tiles[3])
         for k in range(3):
-            write_rows(part, z, e, k * LANES, tiles[k].astype(BF))
-            write_rows(part, z, o, SHARED + k * LANES, tiles[4 + k].astype(BF))
-        write_rows(part, z, e, SLICE - SHARED, even_half)
-        write_rows(part, z, o, 0, odd_half)
+            write_rows(part, z, e, k * LANES, tiles[k].astype(BF), halves)
+            write_rows(part, z, o, SHARED + k * LANES, tiles[4 + k].astype(BF), halves)
+        write_rows(part, z, e, SLICE - SHARED, even_half, halves)
+        write_rows(part, z, o, 0, odd_half, halves)
 
 
 def load_quarter(part, z):
@@ -247,13 +248,16 @@
 
 
 class Spreader(Exchange):
-    def __init__(self, place, part, send, recv):
+    def __init__(self, place, part, send, recv, halves=None):
         self.place, self.part, self.send, self.recv = place, part, send, recv
+        self.halves = halves or {}
 
     def copies(self, step, c):
         place = self.place
         result = []
         for h, way, hop in WAYS:
+            if h not in self.halves.get(c, (0, 1)):
+                continue
             part = self.part.at[c, h]
             p, q = place.axes(h)
             if step == 0:
@@ -375,9 +379,10 @@
     return sum((b[k] + bits[k] - 2 * b[k] * bits[k]) * (1 << k) for k in range(3))
 
 
-PARTNERS = (0, 1, 3, 7, 2, 6, 4, 5)
+PARTNERS = (0, 1, 4, 5, 2, 6, 3, 7)
 WHOLE = (1, 4, 5)
 SPREAD = (2, 3, 6, 7)
+SPREAD_HALVES = {2: (0, 1), 3: (0, 1), 6: (1,), 7: (0,)}
 TURNS = CHUNKS // 2
 SLOTS = 6
 
@@ -482,7 +487,7 @@
     pl.semaphore_wait(barrier, 4 + CHUNKS - 1)
 
     gatherer = Spreader(place, full, full_send, full_recv)
-    spreader = Spreader(place, part, spread_send, spread_recv)
+    spreader = Spreader(place, part, spread_send, spread_recv, SPREAD_HALVES)
     summer = Summer(place, part, (r1, r2, r3, r4), sum_send, sum_recv)
     for b in range(row_blocks):
         gatherer.start(0, b)
@@ -544,13 +549,19 @@
                 go_recv.at[c, h],
                 partner(c),
             )
-            for h in range(2)
+            for h in SPREAD_HALVES[c]
         ]
 
     def whole(c):
         slot = 1 if c == 5 else 0
         return to_group(
             ready.at[slot], part.at[c], go_send.at[c, 0], go_recv.at[c, 0], partner(c)
+        )
+
+    def other_half(c):
+        h = 1 - SPREAD_HALVES[c][0]
+        return to_group(
+            ready.at[c - 6, h], part.at[c, h], go_send.at[c, h], go_recv.at[c, h], partner(c)
         )
 
     for c in SPREAD:
@@ -584,10 +595,13 @@
     for c in SPREAD[:2]:
         spreader.arrive(0, c)
         spreader.start(1, c)
+    for c in SPREAD[:2]:
+        spreader.arrive(1, c)
+        spreader.start(2, c)
     for b in range(row_blocks):
         gatherer.arrive(3, b)
 
-    def choose_whole(c, target):
+    def choose_whole(c, target, halves=(0, 1)):
         chosen_rows = pick(c)
 
         @pl.loop(0, SIDE)
@@ -596,7 +610,7 @@
                 [load_quarter(full.at[b], z) for b in range(row_blocks)], axis=0
             )
             store_quarter(
-                target, z, jnp.dot(chosen_rows, source, preferred_element_type=F32)
+                target, z, jnp.dot(chosen_rows, source, preferred_element_type=F32), halves
             )
 
     choose_whole(1, ready.at[0])
@@ -675,10 +689,12 @@
             inner = gate / (1.0 + jnp.exp(-gate)) * up * factor
             hidden[:, k * hidden_size : (k + 1) * hidden_size] = inner.astype(BF)
 
-        @pl.when(lax.rem(j, 2) == 1)
-        def _():
-            for i in range(2):
-                spreader.sent(2 * j + i)
+        for chosen in (SPREAD[:2], SPREAD[2:]):
+
+            @pl.when(2 * j == chosen[0])
+            def _():
+                for c in chosen:
+                    spreader.sent(c)
 
         @pl.loop(0, SIDE)
         def _(z):
@@ -722,8 +738,8 @@
 
         @pl.when(it == 0)
         def _():
-            spread(2, SPREAD[:2])
             spread(0, SPREAD[2:])
+            spread(3, SPREAD[:2])
             whole(1).wait_recv()
             side(1).wait_recv()
             for load in loads:
@@ -738,7 +754,11 @@
 
         @pl.when(it == 2)
         def _():
-            spread(3, SPREAD[2:])
+            for c in WHOLE[1:]:
+                whole(c).wait_send()
+            for c in SPREAD[2:]:
+                choose_whole(c, ready.at[c - 6], (1 - SPREAD_HALVES[c][0],))
+                other_half(c).start()
             for c in WHOLE[1:]:
                 whole(c).wait_recv()
                 side(c).wait_recv()
@@ -747,6 +767,7 @@
         def _():
             spread(4, SPREAD[2:])
             for c in SPREAD[2:]:
+                other_half(c).wait_recv()
                 side(c).wait_recv()
 
         @pl.when(it < TURNS)
@@ -757,8 +778,11 @@
 
         @pl.when(it == 0)
         def _():
-            spread(3, SPREAD[:2])
             spread(1, SPREAD[2:])
+
+        @pl.when(it == 1)
+        def _():
+            spread(3, SPREAD[2:])
 
         return carry
 
@@ -784,8 +808,8 @@
     for c in SPREAD:
         for copy in slices(c):
             copy.wait_send()
-    for c in WHOLE[1:]:
-        whole(c).wait_send()
+    for c in SPREAD[2:]:
+        other_half(c).wait_send()
 
 
 def feed(

time: 227 us -> 219 us (0.965)
  Pallas kernels: 196 us -> 189 us
    pallas_call x1, Pallas kernels: 163 us -> 157 us  [feed(): pl.pallas_call(feed_kernel, out_shape=jax.ShapeDtypeStruct((rows, SLICE),...]
where the time goes in v4:
time: 219 us; the launch traced here: 218 us
  Pallas kernels  189 us (86%)
  local copies, waits for them, and re-layouts  11.1 us (5%)
  matrix products  8.02 us (4%)
  waiting for transfers between devices  5.9 us (3%)
  starting transfers between devices  2.22 us (1%)
    pallas_call x1, Pallas kernels, feed(): pl.pallas_call(feed_kernel, out_shape=jax.ShapeDtypeStruct((rows, SLICE),...  157 us
    pallas_call x1, Pallas kernels, project(): pl.pallas_call(project_kernel, out_shape=jax.ShapeDtypeStruct((count, SLI...  32.5 us
    ppermute x2, waiting for transfers between devices, from_partner(): lax.ppermute(block, 'tensor', [(i, i ^ 1) for i in range(lax.axis_size('t...  5.9 us
    unnamed x14, local copies, waits for them, and re-layouts  4.75 us
    dot_general x1, matrix products, attend(): jnp.einsum('tgd,tpd->tgp', rows, kv_cache[0], preferred_element_type=F32)  4.55 us
  transfers between devices with their start and end apart: 2, of which 1 were waited for; matrix products, arithmetic and copies ran while one was open for 2% of the time, Pallas kernels for 0%

profile of v4, /device:TPU:1, one launch (start us, length us, event | category | flops | bytes accessed | tf_op | source)
XLA Modules:
  0.0 218.3 jit_solution(3546002825329491484)
XLA Ops:
  0.0 3.1 %constant_dynamic-slice_fusion.5 = bf16[256,1,896]{2,1,0:T(2,128)(2,1)S(1)} fusion(bf16[256,8,896]{2,1,0:T(8,128)(2,1)} %param.15, s32[]{:T(128)S(6)} %select_n.35), kind=kLoop, calls=%fused_computation.37 | loop fusion | bytes 917508 | tf_op jit(solution)/shard_map/jit(dynamic_index_in_dim)/dynamic_slice | solution.py:888
  3.1 1.3 copy.80
  4.4 0.3 copy.66
  4.8 0.2 dynamic-slice_convert_fusion
  5.1 0.4 fusion.15
  5.6 0.1 broadcast_compare_fusion
  5.7 4.5 %fusion.27 = (f32[256,7]{1,0:T(8,128)S(1)}, f32[256,7,64]{2,1,0:T(8,128)S(1)}) fusion(bf16[256,7,128]{2,1,0:T(8,128)(2,1)S(1)} %copy.66, bf16[2,256,64,128]{3,2,1,0:T(8,128)(2,1)} %param.17, pred[256,64]{1,0:T(8,128)(4,1)S(1)} %broadcast_compare_fusion), kind=kOutput, calls=%fused_computation.41 | convolution fusion | flops 29702400 | bytes 5135360 | tf_op jit(solution)/shard_map/tgd,tpd->tgp/dot_general | solution.py:894
  10.3 0.1 copy.69
  10.5 0.7 convert_reduce_fusion
  11.3 2.1 collective-permute-start
  13.5 0.1 copy.70
  13.6 3.1 %fusion.12 = f32[256,7,128]{2,1,0:T(8,128)S(1)} fusion(bf16[2,256,64,128]{3,2,1,0:T(8,128)(2,1)} %param.17, f32[256,128]{1,0:T(8,128)S(1)} %bitcast.80, f32[256,7]{1,0:T(8,128)S(1)} %copy.70, f32[256,7,64]{2,1,0:T(8,128)S(1)} %get-tuple-element.12, f32[256,7]{1,0:T(8,128)S(1)} %copy.69, pred[256,64]{1,0:T(8,128)(4,1)S(1)} %broadcast_compare_fusion), kind=kOutput, calls=%fused_computation.8 | convolution fusion | flops 30162944 | bytes 5732352 | tf_op jit(solution)/shard_map/tgp,tpd->tgd/dot_general | solution.py:903
  16.7 0.4 copy.71
  17.1 0.1 copy.85
  17.4 0.2 copy.83
  17.7 0.2 copy.84
  18.1 0.2 copy.86
  18.3 5.9 %collective-permute-done.1 = bf16[256,448]{1,0:T(8,128)(2,1)S(1)} collective-permute-done((bf16[256,448]{1,0:T(8,128)(2,1)S(1)}, bf16[256,448]{1,0:T(8,128)(2,1)S(1)}, u32[]{:S(2)}, u32[]{:S(2)}) %collective-permute-start.1) | collective-permute-done | bytes 229408 | tf_op jit(solution)/shard_map/ppermute | solution.py:879
  24.2 0.2 add_convert_fusion.att_ref
  24.4 2.0 copy-done
  26.4 32.5 %project.1.state_ref = bf16[2,448,128]{2,1,0:T(8,128)(2,1)S(1)} custom-call(bf16[256,448]{1,0:T(8,128)(2,1)S(1)} %add_convert_fusion.att_ref, bf16[448,7168]{1,0:T(8,128)(2,1)} %weight_ref.1, bf16[256,7168]{1,0:T(8,128)(2,1)S(1)} %copy-done), custom_call_target="tpu_custom_call" | custom-call | tf_op jit(solution)/shard_map/project/pallas_call | solution.py:350
  58.9 0.7 copy-done.1
  59.6 157.0 %feed.1 = bf16[256,448]{1,0:T(8,128)(2,1)} custom-call(s32[2,256]{1,0:T(2,128)} %bitcast.84, f32[2,256]{1,0:T(2,128)} %bitcast.85, bf16[2,448,128]{2,1,0:T(8,128)(2,1)} %copy-done.1, bf16[1,304,7168]{2,1,0:T(8,128)(2,1)} %bitcast.71, bf16[1,304,7168]{2,1,0:T(8,128)(2,1)} %bitcast.72, bf16[1,304,7168]{2,1,0:T(8,128)(2,1)} %expert_down.1, ...), custom_call_target="tpu_custom_call" | custom-call | tf_op jit(solution)/shard_map/feed/pallas_call | solution.py:831
  216.6 1.8 copy.77
  (24 shorter events, 0.8 us)
Async XLA Ops:
  0.0 4.7 %copy-start.2 = (bf16[2,256,8,128]{3,2,1,0:T(8,128)(2,1)S(1)}, bf16[2,256,8,128]{3,2,1,0:T(8,128)(2,1)}, u32[]{:S(2)}) copy-start(bf16[2,256,8,128]{3,2,1,0:T(8,128)(2,1)} %param.16) | copy-start | bytes 3145732
  0.0 5.6 %copy-start.3 = (s32[256]{0:T(256)S(1)}, s32[256]{0:T(256)}, u32[]{:S(2)}) copy-start(s32[256]{0:T(256)} %param.18) | copy-start | bytes 3076
  11.3 6.2 %collective-permute-start = (f32[2,256,7]{1,2,0:T(8,128)S(1)}, f32[2,256,7]{1,2,0:T(8,128)S(1)}, u32[]{:S(2)}, u32[]{:S(2)}) collective-permute-start(f32[2,256,7]{1,2,0:T(8,128)S(1)} %pad_maximum_fusion), channel_id=1, source_target_pairs={{0,1},{1,0},{2,3},{3,2},{4,5},{5,4},{6,7},{7,6},{8,9},{9,8},{10,11... | collective-permute-start | bytes 43016 | tf_op jit(solution)/shard_map/ppermute | solution.py:879
  17.2 6.9 %collective-permute-start.1 = (bf16[256,448]{1,0:T(8,128)(2,1)S(1)}, bf16[256,448]{1,0:T(8,128)(2,1)S(1)}, u32[]{:S(2)}, u32[]{:S(2)}) collective-permute-start(bf16[256,448]{1,0:T(8,128)(2,1)S(1)} %copy.85), channel_id=1, source_target_pairs={{0,1},{1,0},{2,3},{3,2},{4,5},{5,4},{6,7},{7,6},{8,9},{9,8},{10,11... | collective-permute-start | bytes 688136 | tf_op jit(solution)/shard_map/ppermute | solution.py:879
  24.4 2.0 copy-start
  58.9 0.7 copy-start.1

commit v5 on v4

--- a/solution.py
+++ b/solution.py
@@ -295,85 +295,6 @@
             )
 
 
-def project_kernel(
-    att_ref, weight_ref, residual_ref, state_ref, part, r1, r2, r3, r4, near, send, recv, local
-):
-    place = Place()
-    barrier = pltpu.get_barrier_semaphore()
-    greet_plane(place, barrier)
-    pl.semaphore_wait(barrier, 4)
-    is_odd = lax.rem(place.rank, 2)
-    first_column = pl.multiple_of((place.rank // 2) * 2 * SLICE, 2 * SLICE)
-    fetch = pltpu.make_async_copy(
-        residual_ref.at[:, pl.ds(first_column, 2 * SLICE)], near, local
-    )
-    fetch.start()
-    summer = Summer(place, part, (r1, r2, r3, r4), send, recv)
-    count = part.shape[0]
-    for c in range(count):
-        rows = att_ref[c * CHUNK : (c + 1) * CHUNK, :]
-
-        @pl.loop(0, SIDE)
-        def _(z):
-            columns = pl.ds(pl.multiple_of(z * 4 * SLICE, 4 * SLICE), 4 * SLICE)
-            block = jnp.dot(rows, weight_ref[:, columns], preferred_element_type=F32)
-            store_quarter(part.at[c], z, block)
-
-        summer.start(0, c)
-    for step in range(1, 4):
-        for c in range(count):
-            summer.arrive(step - 1, c)
-            summer.add(step - 1, c)
-            summer.start(step, c)
-    fetch.wait()
-    for c in range(count):
-        summer.arrive(3, c)
-        rows = pl.ds(c * CHUNK, CHUNK)
-        even = [near[rows, k * LANES : (k + 1) * LANES] for k in range(4)]
-        odd = [near[rows, (k + 3) * LANES : (k + 4) * LANES] for k in range(4)]
-        whole = jnp.concatenate(
-            [
-                jnp.where(is_odd == 1, odd[k + 1].astype(F32), even[k].astype(F32))
-                for k in range(3)
-            ]
-            + [even[3].astype(F32)],
-            axis=1,
-        )
-        store_own(state_ref.at[c], whole, is_odd)
-        state_ref[c] = (state_ref[c].astype(F32) + summer.total(c)).astype(BF)
-    for c in range(count):
-        summer.sent(c)
-
-
-def project(attention, out_weight, residual):
-    count = attention.shape[0] // CHUNK
-    return pl.pallas_call(
-        project_kernel,
-        out_shape=jax.ShapeDtypeStruct((count, SLICE, LANES), BF),
-        in_specs=[
-            pl.BlockSpec(memory_space=pltpu.VMEM),
-            pl.BlockSpec(memory_space=pltpu.VMEM),
-            pl.BlockSpec(memory_space=pl.ANY),
-        ],
-        out_specs=pl.BlockSpec(memory_space=pltpu.VMEM),
-        scratch_shapes=[
-            pltpu.VMEM((count, 2, 16, HALF, LANES), BF),
-            pltpu.VMEM((count, 2, 2, 2, HALF, LANES), BF),
-            pltpu.VMEM((count, 2, 2, SIDE, HALF, LANES), BF),
-            pltpu.VMEM((count, 2, 2, QUARTER, LANES), BF),
-            pltpu.VMEM((count, 2, 2, HALF, LANES), BF),
-            pltpu.VMEM((attention.shape[0], 2 * SLICE), BF),
-            pltpu.SemaphoreType.DMA((count, 4, 2, 2)),
-            pltpu.SemaphoreType.DMA((count, 4, 2, 2)),
-            pltpu.SemaphoreType.DMA,
-        ],
-        compiler_params=pltpu.CompilerParams(
-            collective_id=1, has_side_effects=True, vmem_limit_bytes=48 * 1024 * 1024
-        ),
-        name="project",
-    )(attention, out_weight, residual)
-
-
 def flipped(group, bits):
     b = (lax.rem(group, 2), lax.rem(group // 2, 2), group // 4)
     return sum((b[k] + bits[k] - 2 * b[k] * bits[k]) * (1 << k) for k in range(3))
@@ -384,7 +305,7 @@
 SPREAD = (2, 3, 6, 7)
 SPREAD_HALVES = {2: (0, 1), 3: (0, 1), 6: (1,), 7: (0,)}
 TURNS = CHUNKS // 2
-SLOTS = 6
+SLOTS = 4
 
 
 def chunk_bits(c):
@@ -407,10 +328,13 @@
     )
 
 
-def feed_kernel(
+def layer_kernel(
+    numerator_ref,
+    marks_ref,
     ids_ref,
     route_ref,
-    state_ref,
+    residual_ref,
+    out_weight,
     expert_gate,
     expert_up,
     expert_down,
@@ -418,6 +342,10 @@
     dense_up,
     dense_down,
     mixed_ref,
+    other,
+    other_marks,
+    near,
+    state_ref,
     part,
     full,
     ready,
@@ -431,12 +359,16 @@
     side_out,
     side_in,
     returned,
-    summed,
     own_pos,
     acc,
     hidden,
     mixing,
     load_sem,
+    first_sem,
+    swap_send,
+    swap_recv,
+    state_send,
+    state_recv,
     full_send,
     full_recv,
     spread_send,
@@ -458,6 +390,15 @@
     row_blocks = rows // CHUNK
     width = 16 * SLICE
 
+    head_part = lax.rem(place.rank, 2)
+    skipped = pl.multiple_of(head_part * SHARED, SHARED)
+    fetch_out = pltpu.make_async_copy(
+        out_weight, w_in.at[pl.ds(skipped, SLICE)], first_sem.at[0]
+    )
+    first_column = pl.multiple_of((place.rank // 2) * 2 * SLICE, 2 * SLICE)
+    fetch_near = pltpu.make_async_copy(
+        residual_ref.at[:, pl.ds(first_column, 2 * SLICE)], near, first_sem.at[1]
+    )
     loads = [
         pltpu.make_async_copy(
             ref, w_in.at[pl.ds(k * hidden_size, hidden_size)], load_sem.at[k]
@@ -469,8 +410,13 @@
         )
         for k, ref in enumerate((expert_down.at[0], dense_down))
     ]
-    for load in loads:
+    fetch_out.start()
+    fetch_near.start()
+    for load in loads[4:]:
         load.start()
+    w_in[pl.ds(pl.multiple_of((1 - head_part) * SLICE, SHARED), SHARED), :] = jnp.zeros(
+        (SHARED, width), BF
+    )
 
     barrier = pltpu.get_barrier_semaphore()
     greet_plane(place, barrier)
@@ -481,16 +427,29 @@
             device_id={"group": flipped(group, chunk_bits(c))},
             device_id_type=pl.DeviceIdType.MESH,
         )
-    for b in range(row_blocks):
-        for h in range(2):
-            full[b, h, spot(h, place.z, place.x)] = state_ref[b, h * HALF : (h + 1) * HALF, :]
     pl.semaphore_wait(barrier, 4 + CHUNKS - 1)
+
+    mate = place.rank + 1 - 2 * head_part
+    theirs = pl.multiple_of((1 - head_part) * 3 * LANES, LANES)
+    mine = head_part * 3 * LANES
+
+    swaps = [copy_to(marks_ref, other_marks, swap_send.at[0], swap_recv.at[0], mate)] + [
+        copy_to(
+            numerator_ref.at[pl.ds(b * CHUNK, CHUNK), pl.ds(theirs, 4 * LANES)],
+            other.at[pl.ds(b * CHUNK, CHUNK)],
+            swap_send.at[1 + b],
+            swap_recv.at[1 + b],
+            mate,
+        )
+        for b in range(row_blocks)
+    ]
+    for copy in swaps:
+        copy.start()
 
     gatherer = Spreader(place, full, full_send, full_recv)
     spreader = Spreader(place, part, spread_send, spread_recv, SPREAD_HALVES)
     summer = Summer(place, part, (r1, r2, r3, r4), sum_send, sum_recv)
-    for b in range(row_blocks):
-        gatherer.start(0, b)
+    state_summer = Summer(place, ready, (r1, r2, r3, r4), state_send, state_recv)
 
     line = lax.broadcasted_iota(jnp.int32, (rows, rows), 0)
     column = lax.broadcasted_iota(jnp.int32, (rows, rows), 1)
@@ -526,8 +485,6 @@
     slot_line = lax.broadcasted_iota(jnp.int32, (CHUNK, rows), 0).astype(F32)
     slot_lane = lax.broadcasted_iota(jnp.int32, (rows, CHUNK), 1).astype(F32)
     sides = lax.broadcasted_iota(jnp.int32, (8, LANES), 0)
-    for b in range(row_blocks):
-        mixing[b * CHUNK : (b + 1) * CHUNK, :] = natural_own(state_ref.at[b], is_odd)
 
     def pick(c):
         return jnp.where(flat_pos[c : c + 1, :] == slot_line, 1.0, 0.0).astype(BF)
@@ -564,14 +521,57 @@
             ready.at[c - 6, h], part.at[c, h], go_send.at[c, h], go_recv.at[c, h], partner(c)
         )
 
-    for c in SPREAD:
-        chosen = jnp.dot(pick(c), mixing[...].astype(BF), preferred_element_type=F32)
-        store_own(outgoing.at[SPREAD.index(c)], chosen, is_odd)
-        for copy in slices(c):
-            copy.start()
+    swaps[0].wait_recv()
+    top = jnp.maximum(marks_ref[0:8, :], other_marks[0:8, :])
+    keep = jnp.exp(marks_ref[0:8, :] - top)
+    take = jnp.exp(other_marks[0:8, :] - top)
+    below = 1.0 / (marks_ref[8:16, :] * keep + other_marks[8:16, :] * take)
+    scales = jnp.concatenate(
+        [keep * below, take * below, jnp.zeros((LANES - 16, rows), F32)], axis=0
+    ).T
+    low = lanes_low(CHUNK)
     for b in range(row_blocks):
-        gatherer.arrive(0, b)
-        gatherer.start(1, b)
+        swaps[1 + b].wait_recv()
+        block_rows = slice(b * CHUNK, (b + 1) * CHUNK)
+        joined = []
+        for k in range(4):
+            factors = [
+                jnp.where(
+                    head_part == 1,
+                    scales[block_rows, at + k + 3 : at + k + 4],
+                    scales[block_rows, at + k : at + k + 1],
+                )
+                for at in (0, 8)
+            ]
+            here = numerator_ref[
+                block_rows, pl.ds(pl.multiple_of(mine + k * LANES, LANES), LANES)
+            ].astype(F32)
+            there = other[block_rows, k * LANES : (k + 1) * LANES].astype(F32)
+            tile = here * factors[0] + there * factors[1]
+            if k == 0:
+                tile = jnp.where(low & (head_part == 1), 0.0, tile)
+            if k == 3:
+                tile = jnp.where(low | (head_part == 1), tile, 0.0)
+            joined.append(tile.astype(BF))
+        attention = jnp.concatenate(joined, axis=1)
+        if b == 0:
+            fetch_out.wait()
+
+        @pl.loop(0, SIDE)
+        def _(z):
+            columns = pl.ds(pl.multiple_of(z * 4 * SLICE, 4 * SLICE), 4 * SLICE)
+            block = jnp.dot(
+                attention, w_in[: SLICE + SHARED, columns], preferred_element_type=F32
+            )
+            store_quarter(ready.at[b], z, block)
+
+        state_summer.start(0, b)
+    for load in loads[:4]:
+        load.start()
+    for b in range(row_blocks):
+        state_summer.arrive(0, b)
+        state_summer.add(0, b)
+        state_summer.start(1, b)
     for c in range(CHUNKS):
         at_slot = positions[:, c : c + 1] == slot_lane
         w_row = jnp.sum(jnp.where(at_slot, weight[:, c : c + 1], 0.0), axis=0, keepdims=True)
@@ -582,6 +582,35 @@
         else:
             side_out[c] = both
             side(c).start()
+    for step in range(2, 4):
+        for b in range(row_blocks):
+            state_summer.arrive(step - 1, b)
+            state_summer.add(step - 1, b)
+            state_summer.start(step, b)
+    fetch_near.wait()
+    for b in range(row_blocks):
+        block_rows = slice(b * CHUNK, (b + 1) * CHUNK)
+        even = [near[block_rows, k * LANES : (k + 1) * LANES].astype(F32) for k in range(4)]
+        odd = [near[block_rows, (k + 4) * LANES : (k + 5) * LANES].astype(F32) for k in range(3)]
+        whole_tiles = [jnp.where(is_odd == 1, odd[k], even[k]) for k in range(3)]
+        store_own(state_ref.at[b], jnp.concatenate(whole_tiles + [even[3]], axis=1), is_odd)
+        state_summer.arrive(3, b)
+        state = (state_ref[b].astype(F32) + state_summer.total(b)).astype(BF)
+        state_ref[b] = state
+        for h in range(2):
+            full[b, h, spot(h, place.z, place.x)] = state[h * HALF : (h + 1) * HALF]
+        gatherer.start(0, b)
+    for b in range(row_blocks):
+        mixing[b * CHUNK : (b + 1) * CHUNK, :] = natural_own(state_ref.at[b], is_odd)
+
+    for c in SPREAD:
+        chosen = jnp.dot(pick(c), mixing[...].astype(BF), preferred_element_type=F32)
+        store_own(outgoing.at[SPREAD.index(c)], chosen, is_odd)
+        for copy in slices(c):
+            copy.start()
+    for b in range(row_blocks):
+        gatherer.arrive(0, b)
+        gatherer.start(1, b)
     for b in range(row_blocks):
         gatherer.arrive(1, b)
         gatherer.start(2, b)
@@ -613,6 +642,8 @@
                 target, z, jnp.dot(chosen_rows, source, preferred_element_type=F32), halves
             )
 
+    for b in range(row_blocks):
+        state_summer.sent(b)
     choose_whole(1, ready.at[0])
     whole(1).start()
     choose_whole(5, ready.at[1])
@@ -623,9 +654,16 @@
     choose_whole(0, part.at[0])
 
     def back(c):
-        return to_group(
-            summed.at[c], returned.at[c], back_send.at[c], back_recv.at[c], partner(c)
-        )
+        return [
+            to_group(
+                ready.at[0, 1, 2 * c + h],
+                returned.at[c, pl.ds(h * HALF, HALF)],
+                back_send.at[c, h],
+                back_recv.at[c, h],
+                partner(c),
+            )
+            for h in range(2)
+        ]
 
     def finish_sum(c):
         summer.arrive(3, c)
@@ -637,13 +675,15 @@
 
         @pl.when(c > 0)
         def _():
-            summed[c] = total
-            back(c).start()
+            for h, copy in enumerate(back(c)):
+                ready[0, 1, 2 * c + h] = total[h * HALF : (h + 1) * HALF]
+                copy.start()
 
     def mix(c):
         @pl.when(c > 0)
         def _():
-            back(c).wait_recv()
+            for copy in back(c):
+                copy.wait_recv()
 
         position = jnp.sum(jnp.where(lane == c, own_pos[...], 0.0), axis=1, keepdims=True)
         at_slot = jnp.where(position == slot_lane, 1.0, 0.0).astype(BF)
@@ -800,11 +840,14 @@
     def _(c):
         summer.sent(c)
 
+    for copy in swaps:
+        copy.wait_send()
     for b in range(row_blocks):
         gatherer.sent(b)
     for c in range(1, CHUNKS):
         side(c).wait_send()
-        back(c).wait_send()
+        for copy in back(c):
+            copy.wait_send()
     for c in SPREAD:
         for copy in slices(c):
             copy.wait_send()
@@ -812,10 +855,13 @@
         other_half(c).wait_send()
 
 
-def feed(
+def finish_layer(
+    numerator,
+    marks,
+    residual,
+    out_weight,
     expert_ids,
     route_weights,
-    state,
     expert_gate,
     expert_up,
     expert_down,
@@ -829,11 +875,15 @@
     hbm = pl.BlockSpec(memory_space=pl.ANY)
     row_blocks = rows // CHUNK
     return pl.pallas_call(
-        feed_kernel,
+        layer_kernel,
         out_shape=jax.ShapeDtypeStruct((rows, SLICE), BF),
-        in_specs=[vmem] * 3 + [hbm] * 6,
+        in_specs=[vmem] * 4 + [hbm] * 8,
         out_specs=vmem,
         scratch_shapes=[
+            pltpu.VMEM((rows, 4 * LANES), BF),
+            pltpu.VMEM((16, rows), F32),
+            pltpu.VMEM((rows, 2 * SLICE), BF),
+            pltpu.VMEM((row_blocks, SLICE, LANES), BF),
             pltpu.VMEM((CHUNKS, 2, 16, HALF, LANES), BF),
             pltpu.VMEM((row_blocks, 2, 16, HALF, LANES), BF),
             pltpu.VMEM((2, 2, 16, HALF, LANES), BF),
@@ -847,25 +897,31 @@
             pltpu.VMEM((CHUNKS, 8, LANES), F32),
             pltpu.VMEM((CHUNKS, 8, LANES), F32),
             pltpu.VMEM((CHUNKS, SLICE, LANES), BF),
-            pltpu.VMEM((CHUNKS, SLICE, LANES), BF),
             pltpu.VMEM((rows, LANES), F32),
             pltpu.VMEM((2 * CHUNK, 4 * hidden_size), F32),
             pltpu.VMEM((2 * CHUNK, 2 * hidden_size), BF),
             pltpu.VMEM((rows, 4 * LANES), F32),
             pltpu.SemaphoreType.DMA((6,)),
+            pltpu.SemaphoreType.DMA((2,)),
+            pltpu.SemaphoreType.DMA((1 + row_blocks,)),
+            pltpu.SemaphoreType.DMA((1 + row_blocks,)),
         ]
-        + [pltpu.SemaphoreType.DMA((row_blocks, 4, 2, 2))] * 2
+        + [pltpu.SemaphoreType.DMA((row_blocks, 4, 2, 2))] * 4
         + [pltpu.SemaphoreType.DMA((CHUNKS, 4, 2, 2))] * 4
         + [pltpu.SemaphoreType.DMA((CHUNKS, 2))] * 2
-        + [pltpu.SemaphoreType.DMA((CHUNKS,))] * 4,
+        + [pltpu.SemaphoreType.DMA((CHUNKS,))] * 2
+        + [pltpu.SemaphoreType.DMA((CHUNKS, 2))] * 2,
         compiler_params=pltpu.CompilerParams(
-            collective_id=2, has_side_effects=True, vmem_limit_bytes=64 * 1024 * 1024 - 65536
+            collective_id=1, has_side_effects=True, vmem_limit_bytes=64 * 1024 * 1024 - 65536
         ),
-        name="feed",
+        name="layer",
     )(
+        numerator,
+        marks,
         expert_ids.T,
         route_weights.T,
-        state,
+        residual,
+        out_weight,
         jnp.swapaxes(expert_gate, 1, 2),
         jnp.swapaxes(expert_up, 1, 2),
         expert_down,
@@ -873,10 +929,6 @@
         dense_up.T,
         dense_down,
     )
-
-
-def from_partner(block):
-    return lax.ppermute(block, "tensor", [(i, i ^ 1) for i in range(lax.axis_size("tensor"))])
 
 
 def attend(queries, new_kv, kv_cache, lengths):
@@ -903,20 +955,14 @@
     numerator = jnp.einsum("tgp,tpd->tgd", weights, kv_cache[1], preferred_element_type=F32)
     numerator = numerator + leading * own_weight[..., None] * new_value.astype(F32)[:, None, :]
     denominator = jnp.sum(weights.astype(F32), axis=-1) + leading * own_weight
-    width = rows.shape[1] * head_size
-    flat = numerator.reshape(row_count, width)
-    mine = lax.dynamic_slice_in_dim(flat, my_part * (width // 2), width // 2, 1)
-    theirs = lax.dynamic_slice_in_dim(flat, (1 - my_part) * (width // 2), width // 2, 1)
-    other, other_marks = from_partner((theirs.astype(BF), jnp.stack([highest, denominator])))
-    other_highest, other_denominator = other_marks[0], other_marks[1]
-    top = jnp.maximum(highest, other_highest)
-    keep, take = jnp.exp(highest - top), jnp.exp(other_highest - top)
-    below = 1.0 / (denominator * keep + other_denominator * take)
-    keep = jnp.repeat(keep * below, head_size, axis=1)
-    take = jnp.repeat(take * below, head_size, axis=1)
-    keep = lax.dynamic_slice_in_dim(keep, my_part * (width // 2), width // 2, 1)
-    take = lax.dynamic_slice_in_dim(take, my_part * (width // 2), width // 2, 1)
-    return (mine * keep + other.astype(F32) * take).astype(BF)
+    flat = numerator.astype(BF).reshape(row_count, -1)
+    marks = jnp.concatenate(
+        [
+            jnp.pad(highest.T, ((0, 1), (0, 0))),
+            jnp.pad(denominator.T, ((0, 1), (0, 0)), constant_values=1.0),
+        ]
+    )
+    return flat, marks
 
 
 def shards(
@@ -935,12 +981,14 @@
     expert_up,
     expert_down,
 ):
-    attention = attend(queries, new_kv, kv_cache, lengths)
-    state = project(attention, out_weight, residual)
-    return feed(
+    numerator, marks = attend(queries, new_kv, kv_cache, lengths)
+    return finish_layer(
+        numerator,
+        marks,
+        residual,
+        out_weight,
         expert_ids,
         route_weights,
-        state,
         expert_gate,
         expert_up,
         expert_down,

time: 219 us -> 207 us (0.945)
  waiting for transfers between devices: 5.9 us -> 0 us
  local copies, waits for them, and re-layouts: 11.1 us -> 8.26 us
  starting transfers between devices: 2.22 us -> 0 us
    ppermute x2 -> x0, waiting for transfers between devices: 5.9 us -> none  [from_partner(): lax.ppermute(block, 'tensor', [(i, i ^ 1) for i in range(lax.axis_size('t...]
    unnamed x14 -> x4, local copies, waits for them, and re-layouts: 4.75 us -> 1.3 us
    pallas_call x2 -> x1, Pallas kernels: 189 us -> 187 us  [finish_layer(): pl.pallas_call(layer_kernel, out_shape=jax.ShapeDtypeStruct((rows, SLICE)...]
    ppermute x2 -> x0, starting transfers between devices: 2.22 us -> none  [from_partner(): lax.ppermute(block, 'tensor', [(i, i ^ 1) for i in range(lax.axis_size('t...]
  transfers between devices with their start and end apart: 2 -> 0, of which waited for: 1 -> 0; matrix products, arithmetic and copies ran while one was open for 2% -> 0% of each run, Pallas kernels for 0% -> 0%
where the time goes in v5:
time: 207 us; the launch traced here: 206 us
  Pallas kernels  187 us (90%)
  matrix products  8.42 us (4%)
  local copies, waits for them, and re-layouts  8.26 us (4%)
  other arithmetic  2.5 us (1%)
    pallas_call x1, Pallas kernels, finish_layer(): pl.pallas_call(layer_kernel, out_shape=jax.ShapeDtypeStruct((rows, SLICE)...  187 us
    dot_general x1, matrix products, attend(): jnp.einsum('tgd,tpd->tgp', rows, kv_cache[0], preferred_element_type=F32)  4.56 us

profile of v5, /device:TPU:1, one launch (start us, length us, event | category | flops | bytes accessed | tf_op | source)
XLA Modules:
  0.0 206.2 jit_solution(9271878426421213711)
XLA Ops:
  0.0 0.0 copy-start
  0.0 0.9 broadcast_compare_fusion
  0.9 3.0 %constant_dynamic-slice_fusion.1 = bf16[256,1,896]{2,1,0:T(2,128)(2,1)S(1)} fusion(bf16[256,8,896]{2,1,0:T(8,128)(2,1)} %param.15, s32[]{:T(128)S(6)} %select_n.27), kind=kLoop, calls=%fused_computation.29 | loop fusion | bytes 917508 | tf_op jit(solution)/shard_map/jit(dynamic_index_in_dim)/dynamic_slice | solution.py:940
  3.9 1.3 copy.39
  5.2 0.3 copy.27
  5.5 0.0 copy-done
  5.5 0.1 fusion.23
  5.6 0.2 dynamic-slice_convert_fusion
  5.9 0.4 fusion.18
  6.3 0.1 copy.38
  6.4 4.6 %fusion.24 = (f32[256,7]{1,0:T(8,128)S(1)}, f32[256,7,64]{2,1,0:T(8,128)S(1)}) fusion(bf16[256,7,128]{2,1,0:T(8,128)(2,1)S(1)} %copy.27, bf16[2,256,64,128]{3,2,1,0:T(8,128)(2,1)} %param.17, pred[256,64]{1,0:T(8,128)(4,1)S(1)} %broadcast_compare_fusion), kind=kOutput, calls=%fused_computation.32 | convolution fusion | flops 29702400 | bytes 5135360 | tf_op jit(solution)/shard_map/tgd,tpd->tgp/dot_general | solution.py:946
  10.9 0.1 copy.29
  11.0 0.1 copy.30
  11.2 0.7 convert_reduce_fusion
  11.9 0.1 copy.34
  12.0 0.6 select_maximum_fusion.marks_ref
  12.6 0.1 copy.31
  12.8 3.5 %fusion.15 = bf16[256,7,128]{2,1,0:T(8,128)(2,1)S(1)} fusion(bf16[2,256,64,128]{3,2,1,0:T(8,128)(2,1)} %param.17, f32[256,128]{1,0:T(8,128)S(1)} %bitcast.69, f32[256,7]{1,0:T(8,128)S(1)} %copy.31, f32[256,7,64]{2,1,0:T(8,128)S(1)} %get-tuple-element.12, f32[256,7]{1,0:T(8,128)S(1)} %copy.30, pred[256,64]{1,0:T(8,128)(4,1)S(1)} %broadcast_compare_fusion), kind=kOutput, calls=%fused_computation.9 | convolution fusion | flops 30392320 | bytes 5273600 | tf_op jit(solution)/shard_map/tgp,tpd->tgd/dot_general | solution.py:955
  16.2 0.3 copy.32
  16.5 1.0 copy.35.numerator_ref
  17.5 186.9 %layer.1 = bf16[256,448]{1,0:T(8,128)(2,1)} custom-call(bf16[256,896]{1,0:T(8,128)(2,1)} %copy.35.numerator_ref, f32[16,256]{1,0:T(8,128)} %select_maximum_fusion.marks_ref, s32[2,256]{1,0:T(2,128)} %bitcast.71, f32[2,256]{1,0:T(2,128)} %bitcast.72, bf16[256,7168]{1,0:T(8,128)(2,1)} %residual_ref.1, bf16[448,7168]{1,0:T(8,128)(2,1)} %out_weight.1, ...), custom_call_target="tpu_custom_call" | custom-call | tf_op jit(solution)/shard_map/layer/pallas_call | solution.py:877
  204.5 1.8 copy.36
  (4 shorter events, 0.1 us)
Async XLA Ops:
  0.0 5.5 %copy-start = (bf16[2,256,8,128]{3,2,1,0:T(8,128)(2,1)S(1)}, bf16[2,256,8,128]{3,2,1,0:T(8,128)(2,1)}, u32[]{:S(2)}) copy-start(bf16[2,256,8,128]{3,2,1,0:T(8,128)(2,1)} %param.16) | copy-start | bytes 3145732

commit v6 on v5

--- a/solution.py
+++ b/solution.py
@@ -156,12 +156,12 @@
 
 
 class Exchange:
-    def start(self, step, c):
-        for copy in self.copies(step, c):
+    def start(self, step, c, halves=(0, 1)):
+        for copy in self.copies(step, c, halves):
             copy.start()
 
-    def arrive(self, step, c):
-        for copy in self.copies(step, c):
+    def arrive(self, step, c, halves=(0, 1)):
+        for copy in self.copies(step, c, halves):
             copy.wait_recv()
 
     def sent(self, c):
@@ -183,10 +183,12 @@
         landing = self.landing[step]
         return landing.at[lax.rem(c, landing.shape[0])]
 
-    def copies(self, step, c):
+    def copies(self, step, c, halves=(0, 1)):
         place = self.place
         result = []
         for h, way, hop in WAYS:
+            if h not in halves:
+                continue
             part = self.part.at[c, h]
             p, q = place.axes(h)
             if step == 0:
@@ -212,27 +214,32 @@
             )
         return result
 
-    def add(self, step, c):
+    def pass_on(self, step, c):
         for h in range(2):
-            part = self.part.at[c, h]
-            p, q = self.place.axes(h)
-            landed = self.landed(step, c).at[h]
-            if step == 0:
-                for way, hop in ((0, 1), (1, -1)):
-                    for k in range(2):
-                        add_into(part.at[ring(q, hop) * SIDE + 2 * way + k], landed.at[way, k])
-            elif step == 1:
-                for k in range(SIDE):
-                    dst = part.at[q * SIDE + k]
-                    dst[...] = (
-                        dst[...].astype(F32) + landed[0, k].astype(F32) + landed[1, k].astype(F32)
-                    ).astype(BF)
-            elif step == 2:
-                for way, hop in ((0, 1), (1, -1)):
-                    add_into(
-                        part.at[q * SIDE + ring(p, hop), pl.ds(way * QUARTER, QUARTER)],
-                        landed.at[way],
-                    )
+            self.arrive(step, c, (h,))
+            self.add(step, c, h)
+            self.start(step + 1, c, (h,))
+
+    def add(self, step, c, h):
+        part = self.part.at[c, h]
+        p, q = self.place.axes(h)
+        landed = self.landed(step, c).at[h]
+        if step == 0:
+            for way, hop in ((0, 1), (1, -1)):
+                for k in range(2):
+                    add_into(part.at[ring(q, hop) * SIDE + 2 * way + k], landed.at[way, k])
+        elif step == 1:
+            for k in range(SIDE):
+                dst = part.at[q * SIDE + k]
+                dst[...] = (
+                    dst[...].astype(F32) + landed[0, k].astype(F32) + landed[1, k].astype(F32)
+                ).astype(BF)
+        elif step == 2:
+            for way, hop in ((0, 1), (1, -1)):
+                add_into(
+                    part.at[q * SIDE + ring(p, hop), pl.ds(way * QUARTER, QUARTER)],
+                    landed.at[way],
+                )
 
     def total(self, c):
         halves = []
@@ -252,11 +259,11 @@
         self.place, self.part, self.send, self.recv = place, part, send, recv
         self.halves = halves or {}
 
-    def copies(self, step, c):
+    def copies(self, step, c, halves=(0, 1)):
         place = self.place
         result = []
         for h, way, hop in WAYS:
-            if h not in self.halves.get(c, (0, 1)):
+            if h not in halves or h not in self.halves.get(c, (0, 1)):
                 continue
             part = self.part.at[c, h]
             p, q = place.axes(h)
@@ -569,9 +576,7 @@
     for load in loads[:4]:
         load.start()
     for b in range(row_blocks):
-        state_summer.arrive(0, b)
-        state_summer.add(0, b)
-        state_summer.start(1, b)
+        state_summer.pass_on(0, b)
     for c in range(CHUNKS):
         at_slot = positions[:, c : c + 1] == slot_lane
         w_row = jnp.sum(jnp.where(at_slot, weight[:, c : c + 1], 0.0), axis=0, keepdims=True)
@@ -584,9 +589,7 @@
             side(c).start()
     for step in range(2, 4):
         for b in range(row_blocks):
-            state_summer.arrive(step - 1, b)
-            state_summer.add(step - 1, b)
-            state_summer.start(step, b)
+            state_summer.pass_on(step - 1, b)
     fetch_near.wait()
     for b in range(row_blocks):
         block_rows = slice(b * CHUNK, (b + 1) * CHUNK)
@@ -609,18 +612,21 @@
         for copy in slices(c):
             copy.start()
     for b in range(row_blocks):
-        gatherer.arrive(0, b)
-        gatherer.start(1, b)
+        for h in range(2):
+            gatherer.arrive(0, b, (h,))
+            gatherer.start(1, b, (h,))
     for b in range(row_blocks):
-        gatherer.arrive(1, b)
-        gatherer.start(2, b)
+        for h in range(2):
+            gatherer.arrive(1, b, (h,))
+            gatherer.start(2, b, (h,))
     for c in SPREAD[:2]:
         for copy in slices(c):
             copy.wait_recv()
         spreader.start(0, c)
     for b in range(row_blocks):
-        gatherer.arrive(2, b)
-        gatherer.start(3, b)
+        for h in range(2):
+            gatherer.arrive(2, b, (h,))
+            gatherer.start(3, b, (h,))
     for c in SPREAD[:2]:
         spreader.arrive(0, c)
         spreader.start(1, c)
@@ -689,6 +695,16 @@
         at_slot = jnp.where(position == slot_lane, 1.0, 0.0).astype(BF)
         block = natural_own(returned.at[c], is_odd).astype(BF)
         mixing[...] += jnp.dot(at_slot, block, preferred_element_type=F32)
+
+    def spread(step, chunks):
+        for c in chunks:
+            if step == 0:
+                for copy in slices(c):
+                    copy.wait_recv()
+            else:
+                spreader.arrive(step - 1, c)
+            if step < 4:
+                spreader.start(step, c)
 
     def compute(j):
         chunks = [part.at[2 * j + i] for i in range(2)]
@@ -729,6 +745,11 @@
             inner = gate / (1.0 + jnp.exp(-gate)) * up * factor
             hidden[:, k * hidden_size : (k + 1) * hidden_size] = inner.astype(BF)
 
+        @pl.when(j == 0)
+        def _():
+            spread(3, SPREAD[:2])
+            spread(1, SPREAD[2:])
+
         for chosen in (SPREAD[:2], SPREAD[2:]):
 
             @pl.when(2 * j == chosen[0])
@@ -736,13 +757,20 @@
                 for c in chosen:
                     spreader.sent(c)
 
+
         @pl.loop(0, SIDE)
-        def _(z):
+        def _(step):
+            z = ring(place.z, step + 2 - SIDE)
             columns = pl.ds(pl.multiple_of(z * 4 * SLICE, 4 * SLICE), 4 * SLICE)
             block = jnp.dot(hidden[...], w_down[:, columns], preferred_element_type=F32)
             for i in range(2):
                 store_quarter(chunks[i], z, block[i * CHUNK : (i + 1) * CHUNK])
 
+            @pl.when(step == 0)
+            def _():
+                for i in range(2):
+                    summer.start(0, 2 * j + i, (0,))
+
     def turn(it, carry):
         def stage(lag, body):
             j = it - lag
@@ -754,21 +782,9 @@
 
         def add(step):
             def body(c):
-                summer.arrive(step - 1, c)
-                summer.add(step - 1, c)
-                summer.start(step, c)
+                summer.pass_on(step - 1, c)
 
             return body
-
-        def spread(step, chunks):
-            for c in chunks:
-                if step == 0:
-                    for copy in slices(c):
-                        copy.wait_recv()
-                else:
-                    spreader.arrive(step - 1, c)
-                if step < 4:
-                    spreader.start(step, c)
 
         stage(5, mix)
         stage(4, finish_sum)
@@ -779,7 +795,6 @@
         @pl.when(it == 0)
         def _():
             spread(0, SPREAD[2:])
-            spread(3, SPREAD[:2])
             whole(1).wait_recv()
             side(1).wait_recv()
             for load in loads:
@@ -814,11 +829,7 @@
         def _():
             compute(it)
             for i in range(2):
-                summer.start(0, 2 * it + i)
-
-        @pl.when(it == 0)
-        def _():
-            spread(1, SPREAD[2:])
+                summer.start(0, 2 * it + i, (1,))
 
         @pl.when(it == 1)
         def _():
@@ -828,13 +839,9 @@
 
     lax.fori_loop(0, TURNS + 5, turn, 0)
 
-    total = mixing[...]
-    for_odd = pltpu.roll(
-        jnp.concatenate([total[:, 3 * LANES :], total[:, : 3 * LANES]], axis=1),
-        4 * LANES - SHARED,
-        1,
-    )
-    mixed_ref[...] = jnp.where(is_odd == 1, for_odd, total)[:, :SLICE].astype(BF)
+    total = mixing[...].T
+    for_odd = jnp.concatenate([total[3 * LANES + SHARED :], total[: 3 * LANES]], axis=0)
+    mixed_ref[...] = jnp.where(is_odd == 1, for_odd, total[:SLICE]).astype(BF)
 
     @pl.loop(0, CHUNKS)
     def _(c):
@@ -876,7 +883,7 @@
     row_blocks = rows // CHUNK
     return pl.pallas_call(
         layer_kernel,
-        out_shape=jax.ShapeDtypeStruct((rows, SLICE), BF),
+        out_shape=jax.ShapeDtypeStruct((SLICE, rows), BF),
         in_specs=[vmem] * 4 + [hbm] * 8,
         out_specs=vmem,
         scratch_shapes=[
@@ -928,7 +935,7 @@
         dense_gate.T,
         dense_up.T,
         dense_down,
-    )
+    ).T
 
 
 def attend(queries, new_kv, kv_cache, lengths):
@@ -937,9 +944,9 @@
     my_head, my_part = rank // 2, rank % 2
     head_size = new_kv.shape[3]
     span = kv_cache.shape[2]
-    rows = lax.dynamic_index_in_dim(queries, my_head, 1, keepdims=False).reshape(
-        row_count, -1, head_size
-    )
+    heads = jnp.arange(queries.shape[1], dtype=jnp.int32)[None, :, None] == my_head
+    rows = jnp.sum(jnp.where(heads, queries, 0).astype(F32), axis=1).astype(BF)
+    rows = rows.reshape(row_count, -1, head_size)
     new_key = lax.dynamic_index_in_dim(new_kv[0], my_head, 1, keepdims=False)
     new_value = lax.dynamic_index_in_dim(new_kv[1], my_head, 1, keepdims=False)
     scale = 1.0 / math.sqrt(head_size)

time: 207 us -> 210 us (1.014)
  local copies, waits for them, and re-layouts: 8.26 us -> 4.06 us
  other arithmetic: 2.5 us -> 6.59 us
  Pallas kernels: 187 us -> 190 us
    reduce_sum x0 -> x1, other arithmetic: none -> 4.08 us  [attend(): rows = jnp.sum(jnp.where(heads, queries, 0).astype(F32), axis=1).astype(BF)]
    pallas_call x1, Pallas kernels: 187 us -> 190 us  [finish_layer(): pl.pallas_call(layer_kernel, out_shape=jax.ShapeDtypeStruct((SLICE, rows)...]
    dynamic_slice x1 -> x0, local copies, waits for them, and re-layouts: 2.99 us -> none  [attend(): lax.dynamic_index_in_dim(queries, my_head, 1, keepdims=False)]
where the time goes in v6:
time: 210 us
  Pallas kernels  190 us (90%)
  matrix products  8.42 us (4%)
  other arithmetic  6.59 us (3%)
  local copies, waits for them, and re-layouts  4.06 us (2%)
    pallas_call x1, Pallas kernels, finish_layer(): pl.pallas_call(layer_kernel, out_shape=jax.ShapeDtypeStruct((SLICE, rows)...  190 us
    dot_general x1, matrix products, attend(): jnp.einsum('tgd,tpd->tgp', rows, kv_cache[0], preferred_element_type=F32)  4.56 us

profile of v6, /device:TPU:1, one launch (start us, length us, event | category | flops | bytes accessed | tf_op | source)
XLA Modules:
  0.0 209.6 jit_solution(13486012701159943185)
XLA Ops:
  0.0 0.0 copy-start
  0.0 0.9 broadcast_compare_fusion
  0.9 4.1 %select_reduce_fusion = bf16[256,896]{1,0:T(8,128)(2,1)S(1)} fusion(bf16[256,8,896]{2,1,0:T(8,128)(2,1)} %param.15, pred[8]{0:T(512)(128)(4,1)S(1)} %iota_compare_fusion.2), kind=kLoop, calls=%fused_computation.6 | loop fusion | flops 3440640 | bytes 4128776 | tf_op jit(solution)/shard_map/reduce_sum | solution.py:948
  5.0 0.2 copy.23
  5.2 0.3 copy.24
  5.5 0.0 copy-done
  5.5 0.1 fusion.23
  5.6 0.2 dynamic-slice_convert_fusion
  5.9 0.4 fusion.18
  6.3 0.1 copy.34
  6.4 4.6 %fusion.24 = (f32[256,7]{1,0:T(8,128)S(1)}, f32[256,7,64]{2,1,0:T(8,128)S(1)}) fusion(bf16[256,7,128]{2,1,0:T(8,128)(2,1)S(1)} %copy.24, bf16[2,256,64,128]{3,2,1,0:T(8,128)(2,1)} %param.17, pred[256,64]{1,0:T(8,128)(4,1)S(1)} %broadcast_compare_fusion), kind=kOutput, calls=%fused_computation.33 | convolution fusion | flops 29702400 | bytes 5135360 | tf_op jit(solution)/shard_map/tgd,tpd->tgp/dot_general | solution.py:953
  10.9 0.1 copy.26
  11.0 0.1 copy.27
  11.2 0.7 convert_reduce_fusion
  11.9 0.1 copy.31
  12.0 0.6 select_maximum_fusion.marks_ref
  12.6 0.1 copy.28
  12.8 3.5 %fusion.15 = bf16[256,7,128]{2,1,0:T(8,128)(2,1)S(1)} fusion(bf16[2,256,64,128]{3,2,1,0:T(8,128)(2,1)} %param.17, f32[256,128]{1,0:T(8,128)S(1)} %bitcast.71, f32[256,7]{1,0:T(8,128)S(1)} %copy.28, f32[256,7,64]{2,1,0:T(8,128)S(1)} %get-tuple-element.12, f32[256,7]{1,0:T(8,128)S(1)} %copy.27, pred[256,64]{1,0:T(8,128)(4,1)S(1)} %broadcast_compare_fusion), kind=kOutput, calls=%fused_computation.10 | convolution fusion | flops 30392320 | bytes 5273600 | tf_op jit(solution)/shard_map/tgp,tpd->tgd/dot_general | solution.py:962
  16.2 0.3 copy.29
  16.6 1.0 copy.32.numerator_ref
  17.5 190.4 %layer.1 = bf16[448,256]{1,0:T(8,128)(2,1)} custom-call(bf16[256,896]{1,0:T(8,128)(2,1)} %copy.32.numerator_ref, f32[16,256]{1,0:T(8,128)} %select_maximum_fusion.marks_ref, s32[2,256]{1,0:T(2,128)} %bitcast.73, f32[2,256]{1,0:T(2,128)} %bitcast.74, bf16[256,7168]{1,0:T(8,128)(2,1)} %residual_ref.1, bf16[448,7168]{1,0:T(8,128)(2,1)} %out_weight.1, ...), custom_call_target="tpu_custom_call" | custom-call | tf_op jit(solution)/shard_map/layer/pallas_call | solution.py:884
  208.0 1.6 copy.42
  (5 shorter events, 0.1 us)
Async XLA Ops:
  0.0 5.5 %copy-start = (bf16[2,256,8,128]{3,2,1,0:T(8,128)(2,1)S(1)}, bf16[2,256,8,128]{3,2,1,0:T(8,128)(2,1)}, u32[]{:S(2)}) copy-start(bf16[2,256,8,128]{3,2,1,0:T(8,128)(2,1)} %param.16) | copy-start | bytes 3145732

commit v7 on v6

--- a/solution.py
+++ b/solution.py
@@ -255,15 +255,14 @@
 
 
 class Spreader(Exchange):
-    def __init__(self, place, part, send, recv, halves=None):
+    def __init__(self, place, part, send, recv):
         self.place, self.part, self.send, self.recv = place, part, send, recv
-        self.halves = halves or {}
 
     def copies(self, step, c, halves=(0, 1)):
         place = self.place
         result = []
         for h, way, hop in WAYS:
-            if h not in halves or h not in self.halves.get(c, (0, 1)):
+            if h not in halves:
                 continue
             part = self.part.at[c, h]
             p, q = place.axes(h)
@@ -307,10 +306,9 @@
     return sum((b[k] + bits[k] - 2 * b[k] * bits[k]) * (1 << k) for k in range(3))
 
 
-PARTNERS = (0, 1, 4, 5, 2, 6, 3, 7)
-WHOLE = (1, 4, 5)
-SPREAD = (2, 3, 6, 7)
-SPREAD_HALVES = {2: (0, 1), 3: (0, 1), 6: (1,), 7: (0,)}
+PARTNERS = (0, 1, 3, 7, 4, 5, 2, 6)
+WHOLE = (1, 6, 7)
+SPREAD = (2, 3, 4, 5)
 TURNS = CHUNKS // 2
 SLOTS = 4
 
@@ -454,7 +452,7 @@
         copy.start()
 
     gatherer = Spreader(place, full, full_send, full_recv)
-    spreader = Spreader(place, part, spread_send, spread_recv, SPREAD_HALVES)
+    spreader = Spreader(place, part, spread_send, spread_recv)
     summer = Summer(place, part, (r1, r2, r3, r4), sum_send, sum_recv)
     state_summer = Summer(place, ready, (r1, r2, r3, r4), state_send, state_recv)
 
@@ -513,19 +511,13 @@
                 go_recv.at[c, h],
                 partner(c),
             )
-            for h in SPREAD_HALVES[c]
+            for h in range(2)
         ]
 
     def whole(c):
-        slot = 1 if c == 5 else 0
+        slot = 1 if c == 7 else 0
         return to_group(
             ready.at[slot], part.at[c], go_send.at[c, 0], go_recv.at[c, 0], partner(c)
-        )
-
-    def other_half(c):
-        h = 1 - SPREAD_HALVES[c][0]
-        return to_group(
-            ready.at[c - 6, h], part.at[c, h], go_send.at[c, h], go_recv.at[c, h], partner(c)
         )
 
     swaps[0].wait_recv()
@@ -633,6 +625,10 @@
     for c in SPREAD[:2]:
         spreader.arrive(1, c)
         spreader.start(2, c)
+    for c in SPREAD[2:]:
+        for copy in slices(c):
+            copy.wait_recv()
+        spreader.start(0, c)
     for b in range(row_blocks):
         gatherer.arrive(3, b)
 
@@ -652,11 +648,11 @@
         state_summer.sent(b)
     choose_whole(1, ready.at[0])
     whole(1).start()
-    choose_whole(5, ready.at[1])
-    whole(5).start()
+    choose_whole(7, ready.at[1])
+    whole(7).start()
     whole(1).wait_send()
-    choose_whole(4, ready.at[0])
-    whole(4).start()
+    choose_whole(6, ready.at[0])
+    whole(6).start()
     choose_whole(0, part.at[0])
 
     def back(c):
@@ -706,7 +702,7 @@
             if step < 4:
                 spreader.start(step, c)
 
-    def compute(j):
+    def widen(j):
         chunks = [part.at[2 * j + i] for i in range(2)]
         acc[...] = jnp.zeros_like(acc)
 
@@ -745,18 +741,14 @@
             inner = gate / (1.0 + jnp.exp(-gate)) * up * factor
             hidden[:, k * hidden_size : (k + 1) * hidden_size] = inner.astype(BF)
 
-        @pl.when(j == 0)
-        def _():
-            spread(3, SPREAD[:2])
-            spread(1, SPREAD[2:])
-
+    def narrow(j):
+        chunks = [part.at[2 * j + i] for i in range(2)]
         for chosen in (SPREAD[:2], SPREAD[2:]):
 
             @pl.when(2 * j == chosen[0])
             def _():
                 for c in chosen:
                     spreader.sent(c)
-
 
         @pl.loop(0, SIDE)
         def _(step):
@@ -771,6 +763,9 @@
                 for i in range(2):
                     summer.start(0, 2 * j + i, (0,))
 
+        for i in range(2):
+            summer.start(0, 2 * j + i, (1,))
+
     def turn(it, carry):
         def stage(lag, body):
             j = it - lag
@@ -785,6 +780,41 @@
                 summer.pass_on(step - 1, c)
 
             return body
+
+        @pl.when(it == 0)
+        def _():
+            spread(3, SPREAD[:2])
+            spread(1, SPREAD[2:])
+            whole(1).wait_recv()
+            side(1).wait_recv()
+            for load in loads:
+                load.wait()
+
+        for turn_at, chosen in ((1, SPREAD[:2]), (2, SPREAD[2:])):
+
+            @pl.when(it == turn_at)
+            def _():
+                spread(4, chosen)
+                for c in chosen:
+                    side(c).wait_recv()
+
+        @pl.when(it == 3)
+        def _():
+            for c in WHOLE[1:]:
+                whole(c).wait()
+                side(c).wait_recv()
+
+        @pl.when(it < TURNS)
+        def _():
+            widen(it)
+
+        @pl.when(it == 0)
+        def _():
+            spread(2, SPREAD[2:])
+
+        @pl.when(it == 1)
+        def _():
+            spread(3, SPREAD[2:])
 
         stage(5, mix)
         stage(4, finish_sum)
@@ -792,48 +822,9 @@
         stage(2, add(2))
         stage(1, add(1))
 
-        @pl.when(it == 0)
-        def _():
-            spread(0, SPREAD[2:])
-            whole(1).wait_recv()
-            side(1).wait_recv()
-            for load in loads:
-                load.wait()
-
-        @pl.when(it == 1)
-        def _():
-            spread(2, SPREAD[2:])
-            spread(4, SPREAD[:2])
-            for c in SPREAD[:2]:
-                side(c).wait_recv()
-
-        @pl.when(it == 2)
-        def _():
-            for c in WHOLE[1:]:
-                whole(c).wait_send()
-            for c in SPREAD[2:]:
-                choose_whole(c, ready.at[c - 6], (1 - SPREAD_HALVES[c][0],))
-                other_half(c).start()
-            for c in WHOLE[1:]:
-                whole(c).wait_recv()
-                side(c).wait_recv()
-
-        @pl.when(it == 3)
-        def _():
-            spread(4, SPREAD[2:])
-            for c in SPREAD[2:]:
-                other_half(c).wait_recv()
-                side(c).wait_recv()
-
         @pl.when(it < TURNS)
         def _():
-            compute(it)
-            for i in range(2):
-                summer.start(0, 2 * it + i, (1,))
-
-        @pl.when(it == 1)
-        def _():
-            spread(3, SPREAD[2:])
+            narrow(it)
 
         return carry
 
@@ -858,8 +849,6 @@
     for c in SPREAD:
         for copy in slices(c):
             copy.wait_send()
-    for c in SPREAD[2:]:
-        other_half(c).wait_send()
 
 
 def finish_layer(

time: 210 us -> 207 us (0.986)
  Pallas kernels: 190 us -> 187 us
    pallas_call x1, Pallas kernels: 190 us -> 187 us  [finish_layer(): pl.pallas_call(layer_kernel, out_shape=jax.ShapeDtypeStruct((SLICE, rows)...]
where the time goes in v7:
time: 207 us; the launch traced here: 206 us
  Pallas kernels  187 us (90%)
  matrix products  8.42 us (4%)
  other arithmetic  6.59 us (3%)
  local copies, waits for them, and re-layouts  4.06 us (2%)
    pallas_call x1, Pallas kernels, finish_layer(): pl.pallas_call(layer_kernel, out_shape=jax.ShapeDtypeStruct((SLICE, rows)...  187 us
    dot_general x1, matrix products, attend(): jnp.einsum('tgd,tpd->tgp', rows, kv_cache[0], preferred_element_type=F32)  4.56 us

profile of v7, /device:TPU:1, one launch (start us, length us, event | category | flops | bytes accessed | tf_op | source)
XLA Modules:
  0.0 206.4 jit_solution(16915388134407784232)
XLA Ops:
  0.0 0.0 copy-start
  0.0 0.9 broadcast_compare_fusion
  0.9 4.1 %select_reduce_fusion = bf16[256,896]{1,0:T(8,128)(2,1)S(1)} fusion(bf16[256,8,896]{2,1,0:T(8,128)(2,1)} %param.15, pred[8]{0:T(512)(128)(4,1)S(1)} %iota_compare_fusion.2), kind=kLoop, calls=%fused_computation.6 | loop fusion | flops 3440640 | bytes 4128776 | tf_op jit(solution)/shard_map/reduce_sum | solution.py:937
  5.0 0.2 copy.23
  5.2 0.3 copy.24
  5.5 0.0 copy-done
  5.5 0.1 fusion.23
  5.6 0.2 dynamic-slice_convert_fusion
  5.9 0.4 fusion.18
  6.3 0.1 copy.34
  6.4 4.6 %fusion.24 = (f32[256,7]{1,0:T(8,128)S(1)}, f32[256,7,64]{2,1,0:T(8,128)S(1)}) fusion(bf16[256,7,128]{2,1,0:T(8,128)(2,1)S(1)} %copy.24, bf16[2,256,64,128]{3,2,1,0:T(8,128)(2,1)} %param.17, pred[256,64]{1,0:T(8,128)(4,1)S(1)} %broadcast_compare_fusion), kind=kOutput, calls=%fused_computation.33 | convolution fusion | flops 29702400 | bytes 5135360 | tf_op jit(solution)/shard_map/tgd,tpd->tgp/dot_general | solution.py:942
  10.9 0.1 copy.26
  11.0 0.1 copy.27
  11.2 0.7 convert_reduce_fusion
  11.9 0.1 copy.31
  12.0 0.6 select_maximum_fusion.marks_ref
  12.6 0.1 copy.28
  12.8 3.5 %fusion.15 = bf16[256,7,128]{2,1,0:T(8,128)(2,1)S(1)} fusion(bf16[2,256,64,128]{3,2,1,0:T(8,128)(2,1)} %param.17, f32[256,128]{1,0:T(8,128)S(1)} %bitcast.71, f32[256,7]{1,0:T(8,128)S(1)} %copy.28, f32[256,7,64]{2,1,0:T(8,128)S(1)} %get-tuple-element.12, f32[256,7]{1,0:T(8,128)S(1)} %copy.27, pred[256,64]{1,0:T(8,128)(4,1)S(1)} %broadcast_compare_fusion), kind=kOutput, calls=%fused_computation.10 | convolution fusion | flops 30392320 | bytes 5273600 | tf_op jit(solution)/shard_map/tgp,tpd->tgd/dot_general | solution.py:951
  16.2 0.3 copy.29
  16.6 1.0 copy.32.numerator_ref
  17.5 187.3 %layer.1 = bf16[448,256]{1,0:T(8,128)(2,1)} custom-call(bf16[256,896]{1,0:T(8,128)(2,1)} %copy.32.numerator_ref, f32[16,256]{1,0:T(8,128)} %select_maximum_fusion.marks_ref, s32[2,256]{1,0:T(2,128)} %bitcast.73, f32[2,256]{1,0:T(2,128)} %bitcast.74, bf16[256,7168]{1,0:T(8,128)(2,1)} %residual_ref.1, bf16[448,7168]{1,0:T(8,128)(2,1)} %out_weight.1, ...), custom_call_target="tpu_custom_call" | custom-call | tf_op jit(solution)/shard_map/layer/pallas_call | solution.py:873
  204.8 1.6 copy.42
  (5 shorter events, 0.1 us)
Async XLA Ops:
  0.0 5.5 %copy-start = (bf16[2,256,8,128]{3,2,1,0:T(8,128)(2,1)S(1)}, bf16[2,256,8,128]{3,2,1,0:T(8,128)(2,1)}, u32[]{:S(2)}) copy-start(bf16[2,256,8,128]{3,2,1,0:T(8,128)(2,1)} %param.16) | copy-start | bytes 3145732

commit v8 on v7

--- a/solution.py
+++ b/solution.py
@@ -255,14 +255,15 @@
 
 
 class Spreader(Exchange):
-    def __init__(self, place, part, send, recv):
+    def __init__(self, place, part, send, recv, halves=None):
         self.place, self.part, self.send, self.recv = place, part, send, recv
+        self.halves = halves or {}
 
     def copies(self, step, c, halves=(0, 1)):
         place = self.place
         result = []
         for h, way, hop in WAYS:
-            if h not in halves:
+            if h not in halves or h not in self.halves.get(c, (0, 1)):
                 continue
             part = self.part.at[c, h]
             p, q = place.axes(h)
@@ -306,9 +307,10 @@
     return sum((b[k] + bits[k] - 2 * b[k] * bits[k]) * (1 << k) for k in range(3))
 
 
-PARTNERS = (0, 1, 3, 7, 4, 5, 2, 6)
+PARTNERS = (0, 1, 4, 5, 3, 7, 2, 6)
 WHOLE = (1, 6, 7)
 SPREAD = (2, 3, 4, 5)
+SPREAD_HALVES = {2: (0, 1), 3: (0, 1), 4: (1,), 5: (0,)}
 TURNS = CHUNKS // 2
 SLOTS = 4
 
@@ -452,7 +454,7 @@
         copy.start()
 
     gatherer = Spreader(place, full, full_send, full_recv)
-    spreader = Spreader(place, part, spread_send, spread_recv)
+    spreader = Spreader(place, part, spread_send, spread_recv, SPREAD_HALVES)
     summer = Summer(place, part, (r1, r2, r3, r4), sum_send, sum_recv)
     state_summer = Summer(place, ready, (r1, r2, r3, r4), state_send, state_recv)
 
@@ -511,13 +513,19 @@
                 go_recv.at[c, h],
                 partner(c),
             )
-            for h in range(2)
+            for h in SPREAD_HALVES[c]
         ]
 
     def whole(c):
         slot = 1 if c == 7 else 0
         return to_group(
             ready.at[slot], part.at[c], go_send.at[c, 0], go_recv.at[c, 0], partner(c)
+        )
+
+    def other_half(c):
+        h = 1 - SPREAD_HALVES[c][0]
+        return to_group(
+            ready.at[2, h], part.at[c, h], go_send.at[c, h], go_recv.at[c, h], partner(c)
         )
 
     swaps[0].wait_recv()
@@ -646,6 +654,9 @@
 
     for b in range(row_blocks):
         state_summer.sent(b)
+    for c in SPREAD[2:]:
+        choose_whole(c, ready.at[2], (1 - SPREAD_HALVES[c][0],))
+        other_half(c).start()
     choose_whole(1, ready.at[0])
     whole(1).start()
     choose_whole(7, ready.at[1])
@@ -797,6 +808,8 @@
                 spread(4, chosen)
                 for c in chosen:
                     side(c).wait_recv()
+                    if len(SPREAD_HALVES[c]) == 1:
+                        other_half(c).wait()
 
         @pl.when(it == 3)
         def _():
@@ -832,7 +845,7 @@
 
     total = mixing[...].T
     for_odd = jnp.concatenate([total[3 * LANES + SHARED :], total[: 3 * LANES]], axis=0)
-    mixed_ref[...] = jnp.where(is_odd == 1, for_odd, total[:SLICE]).astype(BF)
+    mixed_ref[...] = jnp.where(is_odd == 1, for_odd, total[:SLICE])
 
     @pl.loop(0, CHUNKS)
     def _(c):
@@ -872,7 +885,7 @@
     row_blocks = rows // CHUNK
     return pl.pallas_call(
         layer_kernel,
-        out_shape=jax.ShapeDtypeStruct((SLICE, rows), BF),
+        out_shape=jax.ShapeDtypeStruct((SLICE, rows), F32),
         in_specs=[vmem] * 4 + [hbm] * 8,
         out_specs=vmem,
         scratch_shapes=[
@@ -882,7 +895,7 @@
             pltpu.VMEM((row_blocks, SLICE, LANES), BF),
             pltpu.VMEM((CHUNKS, 2, 16, HALF, LANES), BF),
             pltpu.VMEM((row_blocks, 2, 16, HALF, LANES), BF),
-            pltpu.VMEM((2, 2, 16, HALF, LANES), BF),
+            pltpu.VMEM((3, 2, 16, HALF, LANES), BF),
             pltpu.VMEM((SLOTS, 2, 2, 2, HALF, LANES), BF),
             pltpu.VMEM((SLOTS, 2, 2, SIDE, HALF, LANES), BF),
             pltpu.VMEM((SLOTS, 2, 2, QUARTER, LANES), BF),
@@ -924,7 +937,7 @@
         dense_gate.T,
         dense_up.T,
         dense_down,
-    ).T
+    ).astype(BF).T
 
 
 def attend(queries, new_kv, kv_cache, lengths):

time: 207 us -> 202 us (0.976); the launches traced: 206 us -> 199 us
  Pallas kernels: 187 us -> 180 us
    pallas_call x1, Pallas kernels: 187 us -> 180 us  [finish_layer(): pl.pallas_call(layer_kernel, out_shape=jax.ShapeDtypeStruct((SLICE, rows)...]
where the time goes in v8:
time: 202 us; the launch traced here: 199 us
  Pallas kernels  180 us (89%)
  matrix products  8.42 us (4%)
  other arithmetic  8.32 us (4%)
  local copies, waits for them, and re-layouts  2.42 us (1%)
    pallas_call x1, Pallas kernels, finish_layer(): pl.pallas_call(layer_kernel, out_shape=jax.ShapeDtypeStruct((SLICE, rows)...  180 us
    dot_general x1, matrix products, attend(): jnp.einsum('tgd,tpd->tgp', rows, kv_cache[0], preferred_element_type=F32)  4.56 us
    reduce_sum x1, other arithmetic, attend(): rows = jnp.sum(jnp.where(heads, queries, 0).astype(F32), axis=1).astype(BF)  4.08 us

profile of v8, /device:TPU:1, one launch (start us, length us, event | category | flops | bytes accessed | tf_op | source)
XLA Modules:
  0.0 199.2 jit_solution(6872195852393067027)
XLA Ops:
  0.0 0.0 copy-start
  0.0 0.9 broadcast_compare_fusion
  0.9 4.1 %select_reduce_fusion = bf16[256,896]{1,0:T(8,128)(2,1)S(1)} fusion(bf16[256,8,896]{2,1,0:T(8,128)(2,1)} %param.15, pred[8]{0:T(512)(128)(4,1)S(1)} %iota_compare_fusion.2), kind=kLoop, calls=%fused_computation.6 | loop fusion | flops 3440640 | bytes 4128776 | tf_op jit(solution)/shard_map/reduce_sum | solution.py:950
  5.0 0.2 copy.23
  5.2 0.3 copy.24
  5.5 0.0 copy-done
  5.5 0.1 fusion.23
  5.6 0.2 dynamic-slice_convert_fusion
  5.9 0.4 fusion.18
  6.3 0.1 copy.34
  6.4 4.6 %fusion.24 = (f32[256,7]{1,0:T(8,128)S(1)}, f32[256,7,64]{2,1,0:T(8,128)S(1)}) fusion(bf16[256,7,128]{2,1,0:T(8,128)(2,1)S(1)} %copy.24, bf16[2,256,64,128]{3,2,1,0:T(8,128)(2,1)} %param.17, pred[256,64]{1,0:T(8,128)(4,1)S(1)} %broadcast_compare_fusion), kind=kOutput, calls=%fused_computation.34 | convolution fusion | flops 29702400 | bytes 5135360 | tf_op jit(solution)/shard_map/tgd,tpd->tgp/dot_general | solution.py:955
  10.9 0.1 copy.26
  11.0 0.1 copy.27
  11.2 0.7 convert_reduce_fusion
  11.9 0.1 copy.31
  12.0 0.6 select_maximum_fusion.marks_ref
  12.6 0.1 copy.28
  12.8 3.5 %fusion.15 = bf16[256,7,128]{2,1,0:T(8,128)(2,1)S(1)} fusion(bf16[2,256,64,128]{3,2,1,0:T(8,128)(2,1)} %param.17, f32[256,128]{1,0:T(8,128)S(1)} %bitcast.71, f32[256,7]{1,0:T(8,128)S(1)} %copy.28, f32[256,7,64]{2,1,0:T(8,128)S(1)} %get-tuple-element.12, f32[256,7]{1,0:T(8,128)S(1)} %copy.27, pred[256,64]{1,0:T(8,128)(4,1)S(1)} %broadcast_compare_fusion), kind=kOutput, calls=%fused_computation.10 | convolution fusion | flops 30392320 | bytes 5273600 | tf_op jit(solution)/shard_map/tgp,tpd->tgd/dot_general | solution.py:964
  16.2 0.3 copy.29
  16.6 1.0 copy.32.numerator_ref
  17.5 179.9 %layer.1 = f32[448,256]{1,0:T(8,128)} custom-call(bf16[256,896]{1,0:T(8,128)(2,1)} %copy.32.numerator_ref, f32[16,256]{1,0:T(8,128)} %select_maximum_fusion.marks_ref, s32[2,256]{1,0:T(2,128)} %bitcast.73, f32[2,256]{1,0:T(2,128)} %bitcast.74, bf16[256,7168]{1,0:T(8,128)(2,1)} %residual_ref.1, bf16[448,7168]{1,0:T(8,128)(2,1)} %out_weight.1, ...), custom_call_target="tpu_custom_call" | custom-call | tf_op jit(solution)/shard_map/layer/pallas_call | solution.py:886
  197.4 1.7 convert_bitcast_fusion
  (5 shorter events, 0.1 us)
Async XLA Ops:
  0.0 5.5 %copy-start = (bf16[2,256,8,128]{3,2,1,0:T(8,128)(2,1)S(1)}, bf16[2,256,8,128]{3,2,1,0:T(8,128)(2,1)}, u32[]{:S(2)}) copy-start(bf16[2,256,8,128]{3,2,1,0:T(8,128)(2,1)} %param.16) | copy-start | bytes 3145732

commit v9 on v8

--- a/solution.py
+++ b/solution.py
@@ -312,6 +312,7 @@
 SPREAD = (2, 3, 4, 5)
 SPREAD_HALVES = {2: (0, 1), 3: (0, 1), 4: (1,), 5: (0,)}
 TURNS = CHUNKS // 2
+IDLE_TURN = 3
 SLOTS = 4
 
 
@@ -777,14 +778,19 @@
         for i in range(2):
             summer.start(0, 2 * j + i, (1,))
 
+    def pair_of(started):
+        return started - started // TURNS
+
     def turn(it, carry):
+        computes = (it <= TURNS) & (it != IDLE_TURN)
+
         def stage(lag, body):
-            j = it - lag
-
-            @pl.when((j >= 0) & (j < TURNS))
+            started = it - lag
+
+            @pl.when((started >= 0) & (started <= TURNS) & (started != IDLE_TURN))
             def _():
                 for i in range(2):
-                    body(2 * j + i)
+                    body(2 * pair_of(started) + i)
 
         def add(step):
             def body(c):
@@ -811,15 +817,15 @@
                     if len(SPREAD_HALVES[c]) == 1:
                         other_half(c).wait()
 
-        @pl.when(it == 3)
+        @pl.when(it == TURNS)
         def _():
             for c in WHOLE[1:]:
                 whole(c).wait()
                 side(c).wait_recv()
 
-        @pl.when(it < TURNS)
+        @pl.when(computes)
         def _():
-            widen(it)
+            widen(pair_of(it))
 
         @pl.when(it == 0)
         def _():
@@ -835,13 +841,13 @@
         stage(2, add(2))
         stage(1, add(1))
 
-        @pl.when(it < TURNS)
+        @pl.when(computes)
         def _():
-            narrow(it)
+            narrow(pair_of(it))
 
         return carry
 
-    lax.fori_loop(0, TURNS + 5, turn, 0)
+    lax.fori_loop(0, TURNS + 6, turn, 0)
 
     total = mixing[...].T
     for_odd = jnp.concatenate([total[3 * LANES + SHARED :], total[: 3 * LANES]], axis=0)

time: 202 us -> 203 us (level)
  the two profiles are of different devices: /device:TPU:1 before, /device:TPU:0 now
where the time goes in v9:
time: 203 us
  Pallas kernels  183 us (90%)
  matrix products  8.42 us (4%)
  other arithmetic  8.32 us (4%)
  local copies, waits for them, and re-layouts  2.42 us (1%)
    pallas_call x1, Pallas kernels, finish_layer(): pl.pallas_call(layer_kernel, out_shape=jax.ShapeDtypeStruct((SLICE, rows)...  183 us
    dot_general x1, matrix products, attend(): jnp.einsum('tgd,tpd->tgp', rows, kv_cache[0], preferred_element_type=F32)  4.56 us
    reduce_sum x1, other arithmetic, attend(): rows = jnp.sum(jnp.where(heads, queries, 0).astype(F32), axis=1).astype(BF)  4.08 us

profile of v9, /device:TPU:0, one launch (start us, length us, event | category | flops | bytes accessed | tf_op | source)
XLA Modules:
  0.0 202.7 jit_solution(550173206132973048)
XLA Ops:
  0.0 0.0 copy-start
  0.0 0.9 broadcast_compare_fusion
  0.9 4.1 %select_reduce_fusion = bf16[256,896]{1,0:T(8,128)(2,1)S(1)} fusion(bf16[256,8,896]{2,1,0:T(8,128)(2,1)} %param.15, pred[8]{0:T(512)(128)(4,1)S(1)} %iota_compare_fusion.2), kind=kLoop, calls=%fused_computation.6 | loop fusion | flops 3440640 | bytes 4128776 | tf_op jit(solution)/shard_map/reduce_sum | solution.py:956
  5.0 0.2 copy.23
  5.2 0.3 copy.24
  5.5 0.0 copy-done
  5.5 0.1 fusion.23
  5.6 0.2 dynamic-slice_convert_fusion
  5.9 0.4 fusion.18
  6.3 0.1 copy.34
  6.4 4.6 %fusion.24 = (f32[256,7]{1,0:T(8,128)S(1)}, f32[256,7,64]{2,1,0:T(8,128)S(1)}) fusion(bf16[256,7,128]{2,1,0:T(8,128)(2,1)S(1)} %copy.24, bf16[2,256,64,128]{3,2,1,0:T(8,128)(2,1)} %param.17, pred[256,64]{1,0:T(8,128)(4,1)S(1)} %broadcast_compare_fusion), kind=kOutput, calls=%fused_computation.34 | convolution fusion | flops 29702400 | bytes 5135360 | tf_op jit(solution)/shard_map/tgd,tpd->tgp/dot_general | solution.py:961
  10.9 0.1 copy.26
  11.0 0.1 copy.27
  11.2 0.7 convert_reduce_fusion
  11.9 0.1 copy.31
  12.0 0.6 select_maximum_fusion.marks_ref
  12.6 0.1 copy.28
  12.8 3.5 %fusion.15 = bf16[256,7,128]{2,1,0:T(8,128)(2,1)S(1)} fusion(bf16[2,256,64,128]{3,2,1,0:T(8,128)(2,1)} %param.17, f32[256,128]{1,0:T(8,128)S(1)} %bitcast.71, f32[256,7]{1,0:T(8,128)S(1)} %copy.28, f32[256,7,64]{2,1,0:T(8,128)S(1)} %get-tuple-element.12, f32[256,7]{1,0:T(8,128)S(1)} %copy.27, pred[256,64]{1,0:T(8,128)(4,1)S(1)} %broadcast_compare_fusion), kind=kOutput, calls=%fused_computation.10 | convolution fusion | flops 30392320 | bytes 5273600 | tf_op jit(solution)/shard_map/tgp,tpd->tgd/dot_general | solution.py:970
  16.2 0.3 copy.29
  16.6 1.0 copy.32.numerator_ref
  17.5 183.4 %layer.1 = f32[448,256]{1,0:T(8,128)} custom-call(bf16[256,896]{1,0:T(8,128)(2,1)} %copy.32.numerator_ref, f32[16,256]{1,0:T(8,128)} %select_maximum_fusion.marks_ref, s32[2,256]{1,0:T(2,128)} %bitcast.73, f32[2,256]{1,0:T(2,128)} %bitcast.74, bf16[256,7168]{1,0:T(8,128)(2,1)} %residual_ref.1, bf16[448,7168]{1,0:T(8,128)(2,1)} %out_weight.1, ...), custom_call_target="tpu_custom_call" | custom-call | tf_op jit(solution)/shard_map/layer/pallas_call | solution.py:892
  201.0 1.7 convert_bitcast_fusion
  (5 shorter events, 0.1 us)
Async XLA Ops:
  0.0 5.5 %copy-start = (bf16[2,256,8,128]{3,2,1,0:T(8,128)(2,1)S(1)}, bf16[2,256,8,128]{3,2,1,0:T(8,128)(2,1)}, u32[]{:S(2)}) copy-start(bf16[2,256,8,128]{3,2,1,0:T(8,128)(2,1)} %param.16) | copy-start | bytes 3145732
